TPU v7x, 32 devices: a whole 2x2x4 slice. The times are simulated.
32 devices in a mesh: seq: 8 (over z, x), tensor: 2 (over y), dp: 2 (over core).
Axes of the slice: x: 2, y: 2, z: 4, core: 2. Of those that a mesh axis runs over, the one named last changes fastest.
Arguments:
- x_stream: bfloat16 [8192, 5120], P(('dp', 'seq'), 'tensor'), parts along dimension 0
- bc_stream: bfloat16 [8192, 256], P(('dp', 'seq')), parts along dimension 0, may hold values from -6 to 6
- z_gate: bfloat16 [8192, 5120], P(('dp', 'seq'), 'tensor'), parts along dimension 0
- dt_stream: bfloat16 [80, 8192], P('tensor', ('dp', 'seq')), parts along dimension 1, as said below
- doc_ids: int32 [8192], P(('dp', 'seq')), parts along dimension 0, may hold values from 0 to 7, never falling along the last dimension, each value on 1 to 2048 neighbouring positions
- conv_x: bfloat16 [4, 5120], P(None, 'tensor'), may hold values from -3 to 3
- conv_bc: bfloat16 [4, 256], replicated, may hold values from -3 to 3
- a_log: float32 [80], P('tensor')
- dt_bias: float32 [80], P('tensor'), as said below
- d_skip: float32 [80], P('tensor'), may hold values from 0.5 to 4
- norm_gain: float32 [5120], P('tensor'), may hold values from 0.5 to 1.5
- w_out: bfloat16 [5120, 2560], P('tensor'), may hold values from -0.078125 to 0.078125
Outputs:
- layer_out: bfloat16 [8192, 2560], P(('dp', 'seq'), 'tensor'), parts along dimension 0
There are 2 independent parts, one for each index of `dp`. A program takes and returns all parts, laid end to end along the dimension named above; an argument that names none is the same for every part. Nothing has to cross between parts.
Inputs may be any that keep to these rules, and one draw needn't show every extreme that they name: `doc_ids`: document ids never fall along the tokens; each document has 1 to 2048 tokens and one has exactly 2048. `dt_bias`: step size bias. `dt_stream`: step size logits.
All inputs are finite; a program needn't handle non-finite values.
Results may differ from a plain program's by a relative error of at most 0.017.
Values may be sent and summed in bfloat16 or wider, within the bound.
A program may use at most 64 MiB of HBM per device.

v0:
```python
import jax
import jax.numpy as jnp
from jax import lax
from jax.sharding import PartitionSpec as P

SPAN = 256


def from_behind(block, axis, distance):
    devices = range(lax.axis_size(axis))
    route = [(i - distance, i) for i in devices if i - distance in devices]
    return lax.ppermute(block, axis, route)


def causal_conv(extended, weights, ext_ids, own_ids, row_count):
    tap_count = weights.shape[0]
    total = jnp.zeros((row_count, extended.shape[1]), jnp.float32)
    for offset in range(tap_count):
        first_row = tap_count - 1 - offset
        window = extended[first_row : first_row + row_count]
        keep_mask = ext_ids[first_row : first_row + row_count] == own_ids
        total = total + jnp.where(
            keep_mask[:, None],
            window.astype(jnp.float32) * weights[offset].astype(jnp.float32),
            0.0,
        )
    return jax.nn.silu(total).astype(jnp.bfloat16)


def pass_state(device_decay, local_final):

    def hand_on(counter, carry_pair):
        passed = from_behind(carry_pair[0].astype(jnp.bfloat16), "seq", 1).astype(jnp.float32)
        return (device_decay[:, None, None] * passed + local_final, passed)

    return lax.fori_loop(
        0, lax.axis_size("seq") - 1, hand_on, (local_final, jnp.zeros_like(local_final))
    )[1]


def local(
    x_stream,
    bc_stream,
    z_gate,
    dt_stream,
    doc_ids,
    conv_x,
    conv_bc,
    a_log,
    dt_bias,
    d_skip,
    norm_gain,
    w_out,
):
    highest = lax.Precision.HIGHEST
    row_count = x_stream.shape[0]
    head_count = dt_stream.shape[0]
    inner_width = x_stream.shape[1]
    head_size = inner_width // head_count
    state_size = bc_stream.shape[1] // 2
    tap_count = conv_x.shape[0]
    blocks = row_count // SPAN
    edge_start = row_count - tap_count + 1
    own_ids = doc_ids.astype(jnp.float32)
    rim_x, rim_bc, rim_ids = from_behind(
        (x_stream[edge_start:], bc_stream[edge_start:], own_ids[edge_start:].astype(jnp.bfloat16)),
        "seq",
        1,
    )
    ext_ids = jnp.concatenate([rim_ids.astype(jnp.float32), own_ids])
    mixed_x = causal_conv(jnp.concatenate([rim_x, x_stream]), conv_x, ext_ids, own_ids, row_count)
    mixed_bc = causal_conv(
        jnp.concatenate([rim_bc, bc_stream]), conv_bc, ext_ids, own_ids, row_count
    )
    prior_id = ext_ids[tap_count - 2]
    step_size = jax.nn.softplus(dt_stream.astype(jnp.float32) + dt_bias[:, None])
    log_rates = -jnp.exp(a_log)[:, None] * step_size
    block_steps = step_size.reshape(head_count, blocks, SPAN)
    cum_rates = jnp.cumsum(log_rates.reshape(head_count, blocks, SPAN), axis=2)
    block_x = mixed_x.reshape(blocks, SPAN, head_count, head_size)
    b_vals = mixed_bc[:, :state_size].reshape(blocks, SPAN, state_size)
    c_vals = mixed_bc[:, state_size:].reshape(blocks, SPAN, state_size)
    c_wide = c_vals.astype(jnp.float32)
    block_ids = own_ids.reshape(blocks, SPAN)
    before = jnp.concatenate([prior_id[None], own_ids[SPAN - 1 :: SPAN][: blocks - 1]])
    carried = block_ids == before[:, None]
    entry_gain = jnp.where(carried[None], jnp.exp(cum_rates), 0.0)
    tail_weight = (
        jnp.where(
            (block_ids == block_ids[:, -1:])[None], jnp.exp(cum_rates[:, :, -1:] - cum_rates), 0.0
        )
        * block_steps
    )
    weighted = block_x.astype(jnp.float32) * jnp.transpose(tail_weight, (1, 2, 0))[..., None]
    block_states = jnp.einsum(
        "cshp,csn->chpn", weighted, b_vals.astype(jnp.float32), precision=highest
    )
    block_decay = jnp.where(carried[:, -1][None], jnp.exp(cum_rates[:, :, -1]), 0.0)
    device_decay = jnp.prod(block_decay, axis=1)
    skip_term = d_skip[None, None, :, None] * block_x.astype(jnp.float32)
    zero_state = jnp.zeros((head_count, head_size, state_size), jnp.float32)

    def advance(carry_state, inputs_now):
        decay_now, fresh_state = inputs_now
        return (decay_now[:, None, None] * carry_state + fresh_state, carry_state)

    local_final, local_entries = lax.scan(advance, zero_state, (block_decay.T, block_states))
    reached = jnp.einsum("ctn,chpn->cthp", c_wide, local_entries, precision=highest)
    lower_mask = jnp.tril(jnp.ones((SPAN, SPAN), jnp.bool_))
    same_doc = (block_ids[:, :, None] == block_ids[:, None, :]) & lower_mask[None]
    spread = cum_rates[:, :, :, None] - cum_rates[:, :, None, :]
    decay_now = jnp.where(same_doc[None], jnp.exp(jnp.minimum(spread, 0.0)), 0.0)
    scores = jnp.einsum("ctn,csn->cts", c_vals, b_vals, preferred_element_type=jnp.float32)
    weights = (scores[None] * decay_now * block_steps[:, :, None, :]).astype(jnp.bfloat16)
    result = (
        jnp.einsum("hcts,cshp->cthp", weights, block_x, preferred_element_type=jnp.float32)
        + reached * jnp.transpose(entry_gain, (1, 2, 0))[..., None]
        + skip_term
    )
    incoming = pass_state(device_decay, local_final)
    prefix = jnp.cumprod(
        jnp.concatenate([jnp.ones((head_count, 1), jnp.float32), block_decay[:, :-1]], axis=1),
        axis=1,
    )
    reach_term = jnp.einsum("ctn,hpn->cthp", c_wide, incoming, precision=highest)
    result = (
        result + reach_term * jnp.transpose(entry_gain * prefix[:, :, None], (1, 2, 0))[..., None]
    )
    y_vals = lax.optimization_barrier(result.reshape(row_count, inner_width).astype(jnp.bfloat16))
    gated = y_vals.astype(jnp.float32) * jax.nn.silu(z_gate.astype(jnp.float32))
    squares = lax.psum(jnp.sum(gated * gated, axis=1), "tensor")
    inv_norm = lax.rsqrt(squares / (inner_width * lax.axis_size("tensor")) + 1e-05)
    normed = (gated * inv_norm[:, None] * norm_gain[None, :]).astype(jnp.bfloat16)
    partial_value = jnp.dot(normed, w_out, preferred_element_type=jnp.float32)
    return lax.psum_scatter(
        partial_value.astype(jnp.bfloat16), "tensor", scatter_dimension=1, tiled=True
    )


def solution(mesh):
    return jax.shard_map(
        local,
        mesh=mesh,
        in_specs=(
            P(("dp", "seq"), "tensor"),
            P(("dp", "seq"), None),
            P(("dp", "seq"), "tensor"),
            P("tensor", ("dp", "seq")),
            P(("dp", "seq")),
            P(None, "tensor"),
            P(),
            P("tensor"),
            P("tensor"),
            P("tensor"),
            P("tensor"),
            P("tensor", None),
        ),
        out_specs=P(("dp", "seq"), "tensor"),
        check_vma=False,
    )
```

profile of v0, /device:TPU:0, one launch (start us, length us, event | category | flops | bytes accessed | tf_op | source)
XLA Modules:
  0.0 269.7 jit_solution(5106288090513626248)
XLA Ops:
  7.4 4.8 %collective-permute-start.1 = (bf16[3]{0:T(256)(128)(2,1)S(1)}, bf16[3]{0:T(256)(128)(2,1)S(1)}, u32[]{:S(2)}, u32[]{:S(2)}) collective-permute-start(bf16[3]{0:T(256)(128)(2,1)S(1)} %slice.99), channel_id=1, source_target_pairs={{0,4},{4,8},{8,12},{12,16},{16,20},{20,24},{24,28},{1,5},{5,9},{9,... | collective-permute-start | bytes 26 | tf_op jit(solution)/shard_map/ppermute | solution.py:12
  12.9 3.4 %collective-permute-start.3 = (bf16[3,256]{1,0:T(4,128)(2,1)S(1)}, bf16[3,256]{1,0:T(4,128)(2,1)S(1)}, u32[]{:S(2)}, u32[]{:S(2)}) collective-permute-start(bf16[3,256]{1,0:T(4,128)(2,1)S(1)} %slice.111), channel_id=1, source_target_pairs={{0,4},{4,8},{8,12},{12,16},{16,20},{20,24},{24,28},{1,5},{5,9},{9,... | collective-permute-start | bytes 4616 | tf_op jit(solution)/shard_map/ppermute | solution.py:12
  16.4 0.8 slice.101
  17.2 3.4 %collective-permute-start.2 = (bf16[3,2560]{1,0:T(4,128)(2,1)S(1)}, bf16[3,2560]{1,0:T(4,128)(2,1)S(1)}, u32[]{:S(2)}, u32[]{:S(2)}) collective-permute-start(bf16[3,2560]{1,0:T(4,128)(2,1)S(1)} %slice.101), channel_id=1, source_target_pairs={{0,4},{4,8},{8,12},{12,16},{16,20},{20,24},{24,28},{1,5},{5,9},{9,... | collective-permute-start | bytes 46088 | tf_op jit(solution)/shard_map/ppermute | solution.py:12
  20.7 4.5 %copy.47 = bf16[512,2560]{0,1:T(8,128)(2,1)} copy(bf16[512,2560]{1,0:T(8,128)(2,1)} %param.16) | data formatting | bytes 5242880 | tf_op args[0]
  25.6 1.2 reduce-window.9
  28.2 4.4 %copy.59 = bf16[512,2560]{0,1:T(8,128)(2,1)} copy(bf16[512,2560]{1,0:T(8,128)(2,1)} %param.18) | data formatting | bytes 5242880 | tf_op args[2]
  34.3 0.8 fusion.28
  35.2 0.8 multiply_convert_fusion.7
  36.6 13.1 %multiply_convert_fusion.3 = bf16[512,2560]{0,1:T(8,128)(2,1)} fusion(bf16[512,2560]{0,1:T(8,128)(2,1)} %copy.47, bf16[3,2560]{0,1:T(8,128)(2,1)S(1)} %copy.48, f32[2560]{0:T(1024)S(1)} %get-tuple-element.82, f32[2560]{0:T(1024)S(1)} %get-tuple-element.83, f32[2560]{0:T(1024)S(1)} %get-tuple-element.81, f32[2560]{0:T(1024)S(1)} %get-tuple-element.80, ...), kind=kLoop, calls=%fused_computation.28 | loop fusion | flops 38010880 | bytes 5301248 | tf_op jit(solution)/shard_map/convert_element_type | solution.py:27
  49.8 4.9 %reshape.115 = bf16[2,256,40,64]{1,0,3,2:T(2,128)(2,1)} reshape(bf16[512,2560]{0,1:T(8,128)(2,1)} %multiply_convert_fusion.3) | data formatting | bytes 5242880 | tf_op jit(solution)/shard_map/reshape | solution.py:80
  54.7 5.9 %fusion.8 = f32[2,40,64,128]{3,2,1,0:T(8,128)} fusion(bf16[2,256,128,1]{2,1,3,0:T(8,128)(2,1)S(1)} %bitcast.81, f32[2,256,40]{1,2,0:T(8,128)S(1)} %get-tuple-element.112, bf16[2,256,40,64]{1,0,3,2:T(2,128)(2,1)} %reshape.115), kind=kOutput, calls=%fused_computation.17 | convolution fusion | flops 2015887360 | bytes 5455872 | tf_op jit(solution)/shard_map/cshp,csn->chpn/dot_general | solution.py:95
  60.6 5.5 %while.26 = (s32[]{:T(128)}, f32[40,64,128]{2,1,0:T(8,128)S(1)}, f32[2,40,64,128]{3,2,1,0:T(8,128)}, f32[2,40]{1,0:T(2,128)S(1)}, f32[2,40,64,128]{3,2,1,0:T(8,128)}, /*index=5*/s32[]{:T(128)}, s32[]{:T(128)}) while((s32[]{:T(128)}, f32[40,64,128]{2,1,0:T(8,128)S(1)}, f32[2,40,64,128]{3,2,1,0:T(8,128)}, f32[2,40]{1,0:T(2,128)S(1)}, ...), condition=%wide.region_3.4_spmd.clone, body=%wide.region_2.3_spmd.clone.sunk | while | flops 1310723 | bytes 6554688 | solution.py:107
  60.6 1.3 bitcast_dynamic-update-slice_fusion.2
  61.9 1.5 bitcast_add_fusion.3
  63.4 1.2 bitcast_dynamic-update-slice_fusion.2
  64.6 1.5 bitcast_add_fusion.3
  66.3 115.3 %while.25 = (s32[]{:T(128)}, bf16[40,64,128]{2,1,0:T(8,128)(2,1)S(1)}, f32[40,64,128]{2,1,0:T(8,128)}, f32[40]{0:T(128)S(1)}, f32[40,64,128]{2,1,0:T(8,128)S(1)}, /*index=5*/s32[]{:T(128)}) while((s32[]{:T(128)}, bf16[40,64,128]{2,1,0:T(8,128)(2,1)S(1)}, f32[40,64,128]{2,1,0:T(8,128)}, f32[40]{0:T(128)S(1)}, f32[40,64,128]{2,1,0:T(8,128)S(1)}, ...), condition=%wide.region_6.7_spmd, body=%wide.region_5.6_spmd.sunk | while | flops 1310722 | bytes 6553869 | solution.py:36
  66.3 3.5 %collective-permute-start = (bf16[40,64,128]{2,1,0:T(8,128)(2,1)S(1)}, bf16[40,64,128]{2,1,0:T(8,128)(2,1)S(1)}, u32[]{:S(2)}, u32[]{:S(2)}) collective-permute-start(bf16[40,64,128]{2,1,0:T(8,128)(2,1)S(1)} %get-tuple-element.219), channel_id=1, source_target_pairs={{0,4},{4,8},{8,12},{12,16},{16,20},{20,24},{24,28},{1,5},{5,9},{9,... | collective-permute-start | bytes 1966088 | tf_op jit(solution)/shard_map/while/body/eval_jaxpr/ppermute | solution.py:12
  69.8 13.1 %collective-permute-done = bf16[40,64,128]{2,1,0:T(8,128)(2,1)S(1)} collective-permute-done((bf16[40,64,128]{2,1,0:T(8,128)(2,1)S(1)}, bf16[40,64,128]{2,1,0:T(8,128)(2,1)S(1)}, u32[]{:S(2)}, u32[]{:S(2)}) %collective-permute-start) | collective-permute-done | bytes 655392 | tf_op jit(solution)/shard_map/while/body/eval_jaxpr/ppermute | solution.py:12
  82.9 1.3 multiply_add_fusion.2
  84.1 4.4 %collective-permute-start = (bf16[40,64,128]{2,1,0:T(8,128)(2,1)S(1)}, bf16[40,64,128]{2,1,0:T(8,128)(2,1)S(1)}, u32[]{:S(2)}, u32[]{:S(2)}) collective-permute-start(bf16[40,64,128]{2,1,0:T(8,128)(2,1)S(1)} %get-tuple-element.219), channel_id=1, source_target_pairs={{0,4},{4,8},{8,12},{12,16},{16,20},{20,24},{24,28},{1,5},{5,9},{9,... | collective-permute-start | bytes 1966088 | tf_op jit(solution)/shard_map/while/body/eval_jaxpr/ppermute | solution.py:12
  88.6 12.2 %collective-permute-done = bf16[40,64,128]{2,1,0:T(8,128)(2,1)S(1)} collective-permute-done((bf16[40,64,128]{2,1,0:T(8,128)(2,1)S(1)}, bf16[40,64,128]{2,1,0:T(8,128)(2,1)S(1)}, u32[]{:S(2)}, u32[]{:S(2)}) %collective-permute-start) | collective-permute-done | bytes 655392 | tf_op jit(solution)/shard_map/while/body/eval_jaxpr/ppermute | solution.py:12
  100.7 1.3 multiply_add_fusion.2
  102.0 4.4 %collective-permute-start = (bf16[40,64,128]{2,1,0:T(8,128)(2,1)S(1)}, bf16[40,64,128]{2,1,0:T(8,128)(2,1)S(1)}, u32[]{:S(2)}, u32[]{:S(2)}) collective-permute-start(bf16[40,64,128]{2,1,0:T(8,128)(2,1)S(1)} %get-tuple-element.219), channel_id=1, source_target_pairs={{0,4},{4,8},{8,12},{12,16},{16,20},{20,24},{24,28},{1,5},{5,9},{9,... | collective-permute-start | bytes 1966088 | tf_op jit(solution)/shard_map/while/body/eval_jaxpr/ppermute | solution.py:12
  106.4 11.2 %collective-permute-done = bf16[40,64,128]{2,1,0:T(8,128)(2,1)S(1)} collective-permute-done((bf16[40,64,128]{2,1,0:T(8,128)(2,1)S(1)}, bf16[40,64,128]{2,1,0:T(8,128)(2,1)S(1)}, u32[]{:S(2)}, u32[]{:S(2)}) %collective-permute-start) | collective-permute-done | bytes 655392 | tf_op jit(solution)/shard_map/while/body/eval_jaxpr/ppermute | solution.py:12
  117.7 1.3 multiply_add_fusion.2
  119.0 5.2 %collective-permute-start = (bf16[40,64,128]{2,1,0:T(8,128)(2,1)S(1)}, bf16[40,64,128]{2,1,0:T(8,128)(2,1)S(1)}, u32[]{:S(2)}, u32[]{:S(2)}) collective-permute-start(bf16[40,64,128]{2,1,0:T(8,128)(2,1)S(1)} %get-tuple-element.219), channel_id=1, source_target_pairs={{0,4},{4,8},{8,12},{12,16},{16,20},{20,24},{24,28},{1,5},{5,9},{9,... | collective-permute-start | bytes 1966088 | tf_op jit(solution)/shard_map/while/body/eval_jaxpr/ppermute | solution.py:12
  124.2 10.3 %collective-permute-done = bf16[40,64,128]{2,1,0:T(8,128)(2,1)S(1)} collective-permute-done((bf16[40,64,128]{2,1,0:T(8,128)(2,1)S(1)}, bf16[40,64,128]{2,1,0:T(8,128)(2,1)S(1)}, u32[]{:S(2)}, u32[]{:S(2)}) %collective-permute-start) | collective-permute-done | bytes 655392 | tf_op jit(solution)/shard_map/while/body/eval_jaxpr/ppermute | solution.py:12
  134.5 1.3 multiply_add_fusion.2
  135.8 5.3 %collective-permute-start = (bf16[40,64,128]{2,1,0:T(8,128)(2,1)S(1)}, bf16[40,64,128]{2,1,0:T(8,128)(2,1)S(1)}, u32[]{:S(2)}, u32[]{:S(2)}) collective-permute-start(bf16[40,64,128]{2,1,0:T(8,128)(2,1)S(1)} %get-tuple-element.219), channel_id=1, source_target_pairs={{0,4},{4,8},{8,12},{12,16},{16,20},{20,24},{24,28},{1,5},{5,9},{9,... | collective-permute-start | bytes 1966088 | tf_op jit(solution)/shard_map/while/body/eval_jaxpr/ppermute | solution.py:12
  141.1 9.4 %collective-permute-done = bf16[40,64,128]{2,1,0:T(8,128)(2,1)S(1)} collective-permute-done((bf16[40,64,128]{2,1,0:T(8,128)(2,1)S(1)}, bf16[40,64,128]{2,1,0:T(8,128)(2,1)S(1)}, u32[]{:S(2)}, u32[]{:S(2)}) %collective-permute-start) | collective-permute-done | bytes 655392 | tf_op jit(solution)/shard_map/while/body/eval_jaxpr/ppermute | solution.py:12
  150.5 1.3 multiply_add_fusion.2
  151.8 5.3 %collective-permute-start = (bf16[40,64,128]{2,1,0:T(8,128)(2,1)S(1)}, bf16[40,64,128]{2,1,0:T(8,128)(2,1)S(1)}, u32[]{:S(2)}, u32[]{:S(2)}) collective-permute-start(bf16[40,64,128]{2,1,0:T(8,128)(2,1)S(1)} %get-tuple-element.219), channel_id=1, source_target_pairs={{0,4},{4,8},{8,12},{12,16},{16,20},{20,24},{24,28},{1,5},{5,9},{9,... | collective-permute-start | bytes 1966088 | tf_op jit(solution)/shard_map/while/body/eval_jaxpr/ppermute | solution.py:12
  157.1 8.5 %collective-permute-done = bf16[40,64,128]{2,1,0:T(8,128)(2,1)S(1)} collective-permute-done((bf16[40,64,128]{2,1,0:T(8,128)(2,1)S(1)}, bf16[40,64,128]{2,1,0:T(8,128)(2,1)S(1)}, u32[]{:S(2)}, u32[]{:S(2)}) %collective-permute-start) | collective-permute-done | bytes 655392 | tf_op jit(solution)/shard_map/while/body/eval_jaxpr/ppermute | solution.py:12
  165.6 1.3 multiply_add_fusion.2
  166.9 5.3 %collective-permute-start = (bf16[40,64,128]{2,1,0:T(8,128)(2,1)S(1)}, bf16[40,64,128]{2,1,0:T(8,128)(2,1)S(1)}, u32[]{:S(2)}, u32[]{:S(2)}) collective-permute-start(bf16[40,64,128]{2,1,0:T(8,128)(2,1)S(1)} %get-tuple-element.219), channel_id=1, source_target_pairs={{0,4},{4,8},{8,12},{12,16},{16,20},{20,24},{24,28},{1,5},{5,9},{9,... | collective-permute-start | bytes 1966088 | tf_op jit(solution)/shard_map/while/body/eval_jaxpr/ppermute | solution.py:12
  172.2 8.0 %collective-permute-done = bf16[40,64,128]{2,1,0:T(8,128)(2,1)S(1)} collective-permute-done((bf16[40,64,128]{2,1,0:T(8,128)(2,1)S(1)}, bf16[40,64,128]{2,1,0:T(8,128)(2,1)S(1)}, u32[]{:S(2)}, u32[]{:S(2)}) %collective-permute-start) | collective-permute-done | bytes 655392 | tf_op jit(solution)/shard_map/while/body/eval_jaxpr/ppermute | solution.py:12
  180.2 1.3 multiply_add_fusion.2
  181.5 3.7 %fusion.23 = f32[2,256,40,64]{1,3,2,0:T(8,128)S(1)} fusion(bf16[2,256,128,1]{2,1,3,0:T(8,128)(2,1)S(1)} %bitcast.78, f32[40,64,128]{2,1,0:T(8,128)} %get-tuple-element.61), kind=kOutput, calls=%fused_computation.42 | convolution fusion | flops 2013265920 | bytes 6684672 | tf_op jit(solution)/shard_map/ctn,hpn->cthp/dot_general | solution.py:125
  185.3 2.2 fusion.34
  187.5 7.8 %fusion.11 = bf16[2,256,40,64]{1,3,2,0:T(8,128)(2,1)S(1)} fusion(f32[2,256,40,64]{1,3,2,0:T(8,128)S(1)} %fusion.23, f32[2,256,40,64]{1,3,2,0:T(8,128)S(1)} %fusion.34, f32[2,256,40]{1,2,0:T(8,128)S(1)} %copy-done.6, f32[40]{0:T(128)S(1)} %copy-done.15, f32[2,256,40]{1,2,0:T(8,128)S(1)} %copy-done.5, f32[40,2,256]{2,0,1:T(8,128)S(1)} %bitcast.84, ...), kind=kOutput, calls=%fused_computation.20 | convolution fusion | flops 713031680 | bytes 16711840 | tf_op jit(solution)/shard_map/hcts,cshp->cthp/dot_general | solution.py:116
  195.3 2.7 %copy.58 = bf16[2,256,40,64]{1,0,3,2:T(2,128)(2,1)S(1)} copy(bf16[2,256,40,64]{1,3,2,0:T(8,128)(2,1)S(1)} %fusion.11) | data formatting | bytes 5242880 | tf_op jit(solution)/shard_map/convert_element_type | solution.py:129
  198.6 1.5 copy-done.2
  200.1 1.8 multiply_reduce_fusion
  201.9 4.9 %psum.7 = f32[512]{0:T(512)S(1)} all-reduce(f32[512]{0:T(512)S(1)} %multiply_reduce_fusion), channel_id=1, replica_groups=mesh['seq'=8,'tensor'=2,'dp'=2] {'tensor'}, use_global_device_ids=true, to_apply=%region_9.10 | all-reduce | flops 512 | bytes 4096 | tf_op jit(solution)/shard_map/psum | solution.py:131
  206.9 13.7 %convolution_convert_fusion = bf16[512,2560]{1,0:T(8,128)(2,1)} fusion(bf16[2560,2560]{1,0:T(8,128)(2,1)} %param.27, f32[2560]{0:T(1024)S(1)} %copy-done.13, f32[512]{0:T(512)S(1)} %add_rsqrt_fusion, bf16[512,2560]{0,1:T(8,128)(2,1)S(1)} %copy-done, bf16[512,2560]{0,1:T(8,128)(2,1)} %bitcast.75), kind=kOutput, calls=%fused_computation.29 | convolution fusion | flops 6725304320 | bytes 20983808 | tf_op jit(solution)/shard_map/dot_general | solution.py:134
  220.5 42.3 %reduce-scatter.2.cloned.1.call-done = bf16[512,1280]{1,0:T(8,128)(2,1)} async-done(((bf16[512,2560]{1,0:T(8,128)(2,1)}), bf16[512,1280]{1,0:T(8,128)(2,1)}) %reduce-scatter.2.cloned.1.call-update) | async-done | bytes 1310736 | tf_op jit(solution)/shard_map/reduce_scatter | solution.py:135
  (79 shorter events, 6.5 us)
Async XLA Ops:
  6.5 18.8 %copy-start.14 = (f32[40]{0:T(128)S(1)}, f32[40]{0:T(128)}, u32[]{:S(2)}) copy-start(f32[40]{0:T(128)} %param.23) | copy-start | bytes 484
  6.5 18.8 %copy-start.9 = (bf16[40,512]{1,0:T(8,128)(2,1)S(1)}, bf16[40,512]{1,0:T(8,128)(2,1)}, u32[]{:S(2)}) copy-start(bf16[40,512]{1,0:T(8,128)(2,1)} %param.19) | copy-start | bytes 122884
  6.5 18.8 %copy-start.12 = (f32[40]{0:T(128)S(1)}, f32[40]{0:T(128)}, u32[]{:S(2)}) copy-start(f32[40]{0:T(128)} %param.24) | copy-start | bytes 484
  6.5 20.7 %copy-start.11 = (bf16[4,256]{1,0:T(4,128)(2,1)S(1)}, bf16[4,256]{1,0:T(4,128)(2,1)}, u32[]{:S(2)}) copy-start(bf16[4,256]{1,0:T(4,128)(2,1)} %param.22) | copy-start | bytes 6148
  6.5 20.8 %copy-start.8 = (bf16[4,2560]{1,0:T(4,128)(2,1)S(1)}, bf16[4,2560]{1,0:T(4,128)(2,1)}, u32[]{:S(2)}) copy-start(bf16[4,2560]{1,0:T(4,128)(2,1)} %param.21) | copy-start | bytes 61444
  6.5 256.3 %reduce-scatter.2.cloned.1.call-start = ((), (), s32[]{:S(2)}) async-start(), calls=%async_computation.1 | async-start | bytes 3932160 | tf_op jit(solution)/shard_map/reduce_scatter | solution.py:135
  7.4 25.2 %collective-permute-start.1 = (bf16[3]{0:T(256)(128)(2,1)S(1)}, bf16[3]{0:T(256)(128)(2,1)S(1)}, u32[]{:S(2)}, u32[]{:S(2)}) collective-permute-start(bf16[3]{0:T(256)(128)(2,1)S(1)} %slice.99), channel_id=1, source_target_pairs={{0,4},{4,8},{8,12},{12,16},{16,20},{20,24},{24,28},{1,5},{5,9},{9,... | collective-permute-start | bytes 26 | tf_op jit(solution)/shard_map/ppermute | solution.py:12
  12.9 22.3 %collective-permute-start.3 = (bf16[3,256]{1,0:T(4,128)(2,1)S(1)}, bf16[3,256]{1,0:T(4,128)(2,1)S(1)}, u32[]{:S(2)}, u32[]{:S(2)}) collective-permute-start(bf16[3,256]{1,0:T(4,128)(2,1)S(1)} %slice.111), channel_id=1, source_target_pairs={{0,4},{4,8},{8,12},{12,16},{16,20},{20,24},{24,28},{1,5},{5,9},{9,... | collective-permute-start | bytes 4616 | tf_op jit(solution)/shard_map/ppermute | solution.py:12
  17.2 19.1 %collective-permute-start.2 = (bf16[3,2560]{1,0:T(4,128)(2,1)S(1)}, bf16[3,2560]{1,0:T(4,128)(2,1)S(1)}, u32[]{:S(2)}, u32[]{:S(2)}) collective-permute-start(bf16[3,2560]{1,0:T(4,128)(2,1)S(1)} %slice.101), channel_id=1, source_target_pairs={{0,4},{4,8},{8,12},{12,16},{16,20},{20,24},{24,28},{1,5},{5,9},{9,... | collective-permute-start | bytes 46088 | tf_op jit(solution)/shard_map/ppermute | solution.py:12
  20.7 14.4 %copy-start.10 = (s32[512]{0:T(512)S(1)}, s32[512]{0:T(512)}, u32[]{:S(2)}) copy-start(s32[512]{0:T(512)} %param.20) | copy-start | bytes 6148
  20.7 14.5 %copy-start.4 = (bf16[512,256]{1,0:T(8,128)(2,1)S(1)}, bf16[512,256]{1,0:T(8,128)(2,1)}, u32[]{:S(2)}) copy-start(bf16[512,256]{1,0:T(8,128)(2,1)} %param.17) | copy-start | bytes 786436
  66.3 16.6 %collective-permute-start = (bf16[40,64,128]{2,1,0:T(8,128)(2,1)S(1)}, bf16[40,64,128]{2,1,0:T(8,128)(2,1)S(1)}, u32[]{:S(2)}, u32[]{:S(2)}) collective-permute-start(bf16[40,64,128]{2,1,0:T(8,128)(2,1)S(1)} %get-tuple-element.219), channel_id=1, source_target_pairs={{0,4},{4,8},{8,12},{12,16},{16,20},{20,24},{24,28},{1,5},{5,9},{9,... | collective-permute-start | bytes 1966088 | tf_op jit(solution)/shard_map/while/body/eval_jaxpr/ppermute | solution.py:12
  84.1 16.6 %collective-permute-start = (bf16[40,64,128]{2,1,0:T(8,128)(2,1)S(1)}, bf16[40,64,128]{2,1,0:T(8,128)(2,1)S(1)}, u32[]{:S(2)}, u32[]{:S(2)}) collective-permute-start(bf16[40,64,128]{2,1,0:T(8,128)(2,1)S(1)} %get-tuple-element.219), channel_id=1, source_target_pairs={{0,4},{4,8},{8,12},{12,16},{16,20},{20,24},{24,28},{1,5},{5,9},{9,... | collective-permute-start | bytes 1966088 | tf_op jit(solution)/shard_map/while/body/eval_jaxpr/ppermute | solution.py:12
  102.0 15.7 %collective-permute-start = (bf16[40,64,128]{2,1,0:T(8,128)(2,1)S(1)}, bf16[40,64,128]{2,1,0:T(8,128)(2,1)S(1)}, u32[]{:S(2)}, u32[]{:S(2)}) collective-permute-start(bf16[40,64,128]{2,1,0:T(8,128)(2,1)S(1)} %get-tuple-element.219), channel_id=1, source_target_pairs={{0,4},{4,8},{8,12},{12,16},{16,20},{20,24},{24,28},{1,5},{5,9},{9,... | collective-permute-start | bytes 1966088 | tf_op jit(solution)/shard_map/while/body/eval_jaxpr/ppermute | solution.py:12
  119.0 15.6 %collective-permute-start = (bf16[40,64,128]{2,1,0:T(8,128)(2,1)S(1)}, bf16[40,64,128]{2,1,0:T(8,128)(2,1)S(1)}, u32[]{:S(2)}, u32[]{:S(2)}) collective-permute-start(bf16[40,64,128]{2,1,0:T(8,128)(2,1)S(1)} %get-tuple-element.219), channel_id=1, source_target_pairs={{0,4},{4,8},{8,12},{12,16},{16,20},{20,24},{24,28},{1,5},{5,9},{9,... | collective-permute-start | bytes 1966088 | tf_op jit(solution)/shard_map/while/body/eval_jaxpr/ppermute | solution.py:12
  135.8 14.7 %collective-permute-start = (bf16[40,64,128]{2,1,0:T(8,128)(2,1)S(1)}, bf16[40,64,128]{2,1,0:T(8,128)(2,1)S(1)}, u32[]{:S(2)}, u32[]{:S(2)}) collective-permute-start(bf16[40,64,128]{2,1,0:T(8,128)(2,1)S(1)} %get-tuple-element.219), channel_id=1, source_target_pairs={{0,4},{4,8},{8,12},{12,16},{16,20},{20,24},{24,28},{1,5},{5,9},{9,... | collective-permute-start | bytes 1966088 | tf_op jit(solution)/shard_map/while/body/eval_jaxpr/ppermute | solution.py:12
  151.8 13.8 %collective-permute-start = (bf16[40,64,128]{2,1,0:T(8,128)(2,1)S(1)}, bf16[40,64,128]{2,1,0:T(8,128)(2,1)S(1)}, u32[]{:S(2)}, u32[]{:S(2)}) collective-permute-start(bf16[40,64,128]{2,1,0:T(8,128)(2,1)S(1)} %get-tuple-element.219), channel_id=1, source_target_pairs={{0,4},{4,8},{8,12},{12,16},{16,20},{20,24},{24,28},{1,5},{5,9},{9,... | collective-permute-start | bytes 1966088 | tf_op jit(solution)/shard_map/while/body/eval_jaxpr/ppermute | solution.py:12
  166.9 13.4 %collective-permute-start = (bf16[40,64,128]{2,1,0:T(8,128)(2,1)S(1)}, bf16[40,64,128]{2,1,0:T(8,128)(2,1)S(1)}, u32[]{:S(2)}, u32[]{:S(2)}) collective-permute-start(bf16[40,64,128]{2,1,0:T(8,128)(2,1)S(1)} %get-tuple-element.219), channel_id=1, source_target_pairs={{0,4},{4,8},{8,12},{12,16},{16,20},{20,24},{24,28},{1,5},{5,9},{9,... | collective-permute-start | bytes 1966088 | tf_op jit(solution)/shard_map/while/body/eval_jaxpr/ppermute | solution.py:12
  181.5 3.7 %copy-start.3 = (f32[2,40,64,128]{3,2,1,0:T(8,128)S(1)}, f32[2,40,64,128]{3,2,1,0:T(8,128)}, u32[]{:S(2)}) copy-start(f32[2,40,64,128]{3,2,1,0:T(8,128)} %get-tuple-element.59) | copy-start | bytes 7864324
  185.2 2.3 copy-start.1
  185.2 2.3 copy-start.5
  185.2 2.3 copy-start.6
  185.2 2.3 copy-start.7
  185.2 2.3 copy-start.15
  195.3 4.8 %copy-start = (bf16[512,2560]{0,1:T(8,128)(2,1)S(1)}, bf16[512,2560]{0,1:T(8,128)(2,1)}, u32[]{:S(2)}) copy-start(bf16[512,2560]{0,1:T(8,128)(2,1)} %copy.59) | copy-start | bytes 7864324
  198.1 8.8 %copy-start.13 = (f32[2560]{0:T(1024)S(1)}, f32[2560]{0:T(1024)}, u32[]{:S(2)}) copy-start(f32[2560]{0:T(1024)} %param.26) | copy-start | bytes 30724
  198.6 1.5 copy-start.2
Sparse Core Ops, SparseCore 0:
  220.6 42.1 reduce-scatter.1
where the time goes:
time: 271 us; the launch traced here: 270 us
  waiting for transfers between devices  115 us (42%)
  starting transfers between devices  45.2 us (17%)
  other arithmetic  34.5 us (13%)
  matrix products  33.5 us (12%)
  local copies, waits for them, and re-layouts  22.6 us (8%)
  between operations  13.8 us (5%)
  blocking collectives  4.93 us (2%)
    ppermute x10, waiting for transfers between devices, from_behind(): return lax.ppermute(block, axis, route)  72.8 us
    ppermute x10, starting transfers between devices, from_behind(): return lax.ppermute(block, axis, route)  45.2 us
    reduce_scatter x1, waiting for transfers between devices, local(): lax.psum_scatter(partial_value.astype(jnp.bfloat16), 'tensor', scatter_di...  42.3 us
    convert_element_type x2, other arithmetic, causal_conv(): return jax.nn.silu(total).astype(jnp.bfloat16)  13.9 us
    dot_general x1, matrix products, local(): partial_value = jnp.dot(normed, w_out, preferred_element_type=jnp.float32)  13.7 us
    unnamed x35, local copies, waits for them, and re-layouts  10.9 us
    add x7, other arithmetic, hand_on(): return (device_decay[:, None, None] * passed + local_final, passed)  8.96 us
    dot_general x1, matrix products, local(): jnp.einsum('hcts,cshp->cthp', weights, block_x, preferred_element_type=jn...  7.8 us
  transfers between devices with their start and end apart: 11, of which 8 were waited for; matrix products, arithmetic and copies ran while one was open for 6% of the time, Pallas kernels for 0%

commit v1 on v0

--- a/solution.py
+++ b/solution.py
@@ -27,15 +27,33 @@
     return jax.nn.silu(total).astype(jnp.bfloat16)
 
 
-def pass_state(device_decay, local_final):
+def shifted(block, axis, distance):
+    count = lax.axis_size(axis)
+    return lax.ppermute(block, axis, [(i, i + distance) for i in range(count - distance)])
 
-    def hand_on(counter, carry_pair):
-        passed = from_behind(carry_pair[0].astype(jnp.bfloat16), "seq", 1).astype(jnp.float32)
-        return (device_decay[:, None, None] * passed + local_final, passed)
 
-    return lax.fori_loop(
-        0, lax.axis_size("seq") - 1, hand_on, (local_final, jnp.zeros_like(local_final))
-    )[1]
+def pass_state(decays, local_final):
+    count = lax.axis_size("seq")
+    me = lax.axis_index("seq")
+    partner = [(i, i ^ 1) for i in range(count)]
+    odd = (me % 2) == 1
+    other = lax.ppermute(local_final.astype(jnp.bfloat16), "seq", partner).astype(jnp.float32)
+    first = jnp.where(odd, other, local_final)
+    second = jnp.where(odd, local_final, other)
+    pair = me // 2
+    pair_decays = decays.reshape(count // 2, 2, -1)
+    whole_pair = second + pair_decays[pair, 1][:, None, None] * first
+    both = pair_decays[:, 0] * pair_decays[:, 1]
+    entering = shifted(whole_pair.astype(jnp.bfloat16), "seq", 2).astype(jnp.float32)
+    covered = both
+    reach = 1
+    while reach < count // 4:
+        nearer = jnp.where(pair >= 1, covered[jnp.maximum(pair - 1, 0)], 0.0)
+        farther = shifted(entering.astype(jnp.bfloat16), "seq", 2 * reach).astype(jnp.float32)
+        entering = entering + nearer[:, None, None] * farther
+        covered = covered * jnp.concatenate([jnp.zeros_like(covered[:reach]), covered[:-reach]])
+        reach *= 2
+    return jnp.where(odd, other + pair_decays[pair, 0][:, None, None] * entering, entering)
 
 
 def local(
@@ -52,7 +70,6 @@
     norm_gain,
     w_out,
 ):
-    highest = lax.Precision.HIGHEST
     row_count = x_stream.shape[0]
     head_count = dt_stream.shape[0]
     inner_width = x_stream.shape[1]
@@ -62,12 +79,18 @@
     blocks = row_count // SPAN
     edge_start = row_count - tap_count + 1
     own_ids = doc_ids.astype(jnp.float32)
-    rim_x, rim_bc, rim_ids = from_behind(
-        (x_stream[edge_start:], bc_stream[edge_start:], own_ids[edge_start:].astype(jnp.bfloat16)),
-        "seq",
-        1,
+    tail_ids = jnp.broadcast_to(
+        own_ids[edge_start:].astype(jnp.bfloat16)[:, None], (tap_count - 1, 128)
     )
-    ext_ids = jnp.concatenate([rim_ids.astype(jnp.float32), own_ids])
+    rim = shifted(
+        jnp.concatenate([x_stream[edge_start:], bc_stream[edge_start:], tail_ids], axis=1), "seq", 1
+    )
+    rim_x = rim[:, :inner_width]
+    rim_bc = rim[:, inner_width : inner_width + 2 * state_size]
+    rim_ids = jnp.where(
+        lax.axis_index("seq") == 0, -1.0, rim[:, inner_width + 2 * state_size].astype(jnp.float32)
+    )
+    ext_ids = jnp.concatenate([rim_ids, own_ids])
     mixed_x = causal_conv(jnp.concatenate([rim_x, x_stream]), conv_x, ext_ids, own_ids, row_count)
     mixed_bc = causal_conv(
         jnp.concatenate([rim_bc, bc_stream]), conv_bc, ext_ids, own_ids, row_count
@@ -80,7 +103,6 @@
     block_x = mixed_x.reshape(blocks, SPAN, head_count, head_size)
     b_vals = mixed_bc[:, :state_size].reshape(blocks, SPAN, state_size)
     c_vals = mixed_bc[:, state_size:].reshape(blocks, SPAN, state_size)
-    c_wide = c_vals.astype(jnp.float32)
     block_ids = own_ids.reshape(blocks, SPAN)
     before = jnp.concatenate([prior_id[None], own_ids[SPAN - 1 :: SPAN][: blocks - 1]])
     carried = block_ids == before[:, None]
@@ -91,12 +113,14 @@
         )
         * block_steps
     )
-    weighted = block_x.astype(jnp.float32) * jnp.transpose(tail_weight, (1, 2, 0))[..., None]
+    weighted = (
+        block_x.astype(jnp.float32) * jnp.transpose(tail_weight, (1, 2, 0))[..., None]
+    ).astype(jnp.bfloat16)
     block_states = jnp.einsum(
-        "cshp,csn->chpn", weighted, b_vals.astype(jnp.float32), precision=highest
+        "cshp,csn->chpn", weighted, b_vals, preferred_element_type=jnp.float32
     )
     block_decay = jnp.where(carried[:, -1][None], jnp.exp(cum_rates[:, :, -1]), 0.0)
-    device_decay = jnp.prod(block_decay, axis=1)
+    decays = lax.all_gather(jnp.prod(block_decay, axis=1), "seq")
     skip_term = d_skip[None, None, :, None] * block_x.astype(jnp.float32)
     zero_state = jnp.zeros((head_count, head_size, state_size), jnp.float32)
 
@@ -105,7 +129,7 @@
         return (decay_now[:, None, None] * carry_state + fresh_state, carry_state)
 
     local_final, local_entries = lax.scan(advance, zero_state, (block_decay.T, block_states))
-    reached = jnp.einsum("ctn,chpn->cthp", c_wide, local_entries, precision=highest)
+    reached = jnp.einsum("ctn,chpn->cthp", c_vals, local_entries.astype(jnp.bfloat16), preferred_element_type=jnp.float32)
     lower_mask = jnp.tril(jnp.ones((SPAN, SPAN), jnp.bool_))
     same_doc = (block_ids[:, :, None] == block_ids[:, None, :]) & lower_mask[None]
     spread = cum_rates[:, :, :, None] - cum_rates[:, :, None, :]
@@ -117,12 +141,12 @@
         + reached * jnp.transpose(entry_gain, (1, 2, 0))[..., None]
         + skip_term
     )
-    incoming = pass_state(device_decay, local_final)
+    incoming = pass_state(decays, local_final)
     prefix = jnp.cumprod(
         jnp.concatenate([jnp.ones((head_count, 1), jnp.float32), block_decay[:, :-1]], axis=1),
         axis=1,
     )
-    reach_term = jnp.einsum("ctn,hpn->cthp", c_wide, incoming, precision=highest)
+    reach_term = jnp.einsum("ctn,hpn->cthp", c_vals, incoming.astype(jnp.bfloat16), preferred_element_type=jnp.float32)
     result = (
         result + reach_term * jnp.transpose(entry_gain * prefix[:, :, None], (1, 2, 0))[..., None]
     )
@@ -130,11 +154,26 @@
     gated = y_vals.astype(jnp.float32) * jax.nn.silu(z_gate.astype(jnp.float32))
     squares = lax.psum(jnp.sum(gated * gated, axis=1), "tensor")
     inv_norm = lax.rsqrt(squares / (inner_width * lax.axis_size("tensor")) + 1e-05)
-    normed = (gated * inv_norm[:, None] * norm_gain[None, :]).astype(jnp.bfloat16)
-    partial_value = jnp.dot(normed, w_out, preferred_element_type=jnp.float32)
-    return lax.psum_scatter(
-        partial_value.astype(jnp.bfloat16), "tensor", scatter_dimension=1, tiled=True
-    )
+    scaled = (gated * norm_gain[None, :]).astype(jnp.bfloat16)
+    members = lax.axis_size("tensor")
+    member = lax.axis_index("tensor")
+    width = w_out.shape[1] // members
+    chunks = 2
+    length = row_count // chunks
+    pieces = []
+    for chunk in range(chunks):
+        rows = slice(chunk * length, (chunk + 1) * length)
+        product = jnp.dot(scaled[rows], w_out, preferred_element_type=jnp.float32).astype(
+            jnp.bfloat16
+        )
+        total = lax.dynamic_slice_in_dim(product, member * width, width, 1).astype(jnp.float32)
+        for distance in range(1, members):
+            target = (member + distance) % members
+            block = lax.dynamic_slice_in_dim(product, target * width, width, 1)
+            route = [(i, (i + distance) % members) for i in range(members)]
+            total = total + lax.ppermute(block, "tensor", route).astype(jnp.float32)
+        pieces.append((total * inv_norm[rows][:, None]).astype(jnp.bfloat16))
+    return jnp.concatenate(pieces)
 
 
 def solution(mesh):

time: 271 us -> 166 us (0.61)
  waiting for transfers between devices: 115 us -> 13.9 us
  blocking collectives: 4.93 us -> 49.3 us
  starting transfers between devices: 45.2 us -> 15.1 us
  between operations: 13.8 us -> 1.11 us
  matrix products: 33.5 us -> 24.4 us
  local copies, waits for them, and re-layouts: 22.6 us -> 26.4 us
    ppermute x10 -> x6, waiting for transfers between devices: 72.8 us -> 13.9 us  [the longest x3 13.9 us: shifted(): lax.ppermute(block, axis, [(i, i + distance) for i in range(count - dista...]
    reduce_scatter x1 -> x0, waiting for transfers between devices: 42.3 us -> none  [local(): lax.psum_scatter(partial_value.astype(jnp.bfloat16), 'tensor', scatter_di...]
    ppermute x10 -> x6, starting transfers between devices: 45.2 us -> 15.1 us  [the longest x3 11.6 us: shifted(): lax.ppermute(block, axis, [(i, i + distance) for i in range(count - dista...]
    unnamed x0 -> x1, blocking collectives: none -> 26.4 us
    psum x1, blocking collectives: 4.93 us -> 22.9 us  [local(): squares = lax.psum(jnp.sum(gated * gated, axis=1), 'tensor')]
    dot_general x4 -> x5, matrix products: 25.5 us -> 15.6 us  [the longest x2 7.16 us: local(): jnp.dot(scaled[rows], w_out, preferred_element_type=jnp.float32)]
    add x7 -> x0, other arithmetic: 8.96 us -> none  [hand_on(): return (device_decay[:, None, None] * passed + local_final, passed)]
    convert_element_type x1 -> x5, other arithmetic: 0.01 us -> 4.39 us  [the longest x2 1.51 us: local(): pieces.append((total * inv_norm[rows][:, None]).astype(jnp.bfloat16))]
  transfers between devices with their start and end apart: 11 -> 6, of which waited for: 8 -> 2; matrix products, arithmetic and copies ran while one was open for 6% -> 12% of each run, Pallas kernels for 0% -> 0%
where the time goes in v1:
time: 166 us; the launch traced here: 164 us
  blocking collectives  49.3 us (30%)
  other arithmetic  34.1 us (21%)
  local copies, waits for them, and re-layouts  26.4 us (16%)
  matrix products  24.4 us (15%)
  starting transfers between devices  15.1 us (9%)
  waiting for transfers between devices  13.9 us (8%)
    unnamed x1, blocking collectives  26.4 us
    psum x1, blocking collectives, local(): squares = lax.psum(jnp.sum(gated * gated, axis=1), 'tensor')  22.9 us
    ppermute x3, waiting for transfers between devices, shifted(): lax.ppermute(block, axis, [(i, i + distance) for i in range(count - dista...  13.9 us
    convert_element_type x2, other arithmetic, causal_conv(): return jax.nn.silu(total).astype(jnp.bfloat16)  13.3 us
    ppermute x3, starting transfers between devices, shifted(): lax.ppermute(block, axis, [(i, i + distance) for i in range(count - dista...  11.6 us
    unnamed x72, local copies, waits for them, and re-layouts  9.81 us
    dot_general x1, matrix products, local(): jnp.einsum('hcts,cshp->cthp', weights, block_x, preferred_element_type=jn...  8.64 us
    dot_general x2, matrix products, local(): jnp.dot(scaled[rows], w_out, preferred_element_type=jnp.float32)  7.16 us
  transfers between devices with their start and end apart: 6, of which 2 were waited for; matrix products, arithmetic and copies ran while one was open for 12% of the time, Pallas kernels for 0%

profile of v1, /device:TPU:0, one launch (start us, length us, event | category | flops | bytes accessed | tf_op | source)
XLA Modules:
  0.0 164.4 jit_solution(11631277515373281600)
XLA Ops:
  0.0 0.7 fusion.51
  0.8 0.8 slice.129
  1.6 0.7 slice.130
  2.3 4.8 %collective-permute-start = (bf16[3,2944]{1,0:T(4,128)(2,1)S(1)}, bf16[3,2944]{1,0:T(4,128)(2,1)S(1)}, u32[]{:S(2)}, u32[]{:S(2)}) collective-permute-start(bf16[3,2944]{1,0:T(4,128)(2,1)S(1)} %pad_maximum_fusion.3), channel_id=1, source_target_pairs={{0,4},{4,8},{8,12},{12,16},{16,20},{20,24},{24,28},{1,5},{5,9},{9,... | collective-permute-start | bytes 53000 | tf_op jit(solution)/shard_map/ppermute | solution.py:32
  7.2 0.7 exponential_negate_fusion
  7.9 1.5 compare_select_fusion
  9.5 1.2 reduce-window.9
  11.0 0.6 copy-done.7
  11.8 0.8 slice_convert_fusion.3
  12.6 1.6 convert_reduce_fusion.3
  14.5 4.5 %copy.64 = bf16[512,2560]{0,1:T(8,128)(2,1)} copy(bf16[512,2560]{1,0:T(8,128)(2,1)} %param.14) | data formatting | bytes 5242880 | tf_op args[0]
  19.1 0.5 slice.155
  19.6 0.7 pad_maximum_fusion.5
  20.3 0.6 broadcast_compare_fusion
  21.1 0.6 fusion.47
  22.4 0.8 multiply_convert_fusion.8
  23.2 0.7 fusion.48
  24.3 12.5 %multiply_convert_fusion.3 = bf16[512,2560]{0,1:T(8,128)(2,1)} fusion(bf16[512,2560]{0,1:T(8,128)(2,1)} %copy.64, bf16[3,2560]{0,1:T(8,128)(2,1)S(1)} %copy.65, f32[2560]{0:T(1024)S(1)} %get-tuple-element.55, f32[2560]{0:T(1024)} %get-tuple-element.56, f32[2560]{0:T(1024)S(1)} %get-tuple-element.54, f32[2560]{0:T(1024)S(1)} %get-tuple-element.53, ...), kind=kLoop, calls=%fused_computation.27 | loop fusion | flops 38010880 | bytes 5301248 | tf_op jit(solution)/shard_map/convert_element_type | solution.py:27
  36.8 5.0 %reshape.140 = bf16[2,256,40,64]{1,0,3,2:T(2,128)(2,1)} reshape(bf16[512,2560]{0,1:T(8,128)(2,1)} %multiply_convert_fusion.3) | data formatting | bytes 5242880 | tf_op jit(solution)/shard_map/reshape | solution.py:103
  41.9 0.8 fusion.40
  42.6 4.1 %fusion.18 = f32[2,40,64,128]{3,2,1,0:T(8,128)} fusion(bf16[2,256,128,1]{2,1,3,0:T(8,128)(2,1)S(1)} %bitcast.90, f32[2,256,40]{1,2,0:T(8,128)S(1)} %get-tuple-element.75, bf16[2,256,40,64]{1,0,3,2:T(2,128)(2,1)} %reshape.140), kind=kOutput, calls=%fused_computation.36 | convolution fusion | flops 339476480 | bytes 5455872 | tf_op jit(solution)/shard_map/cshp,csn->chpn/dot_general | solution.py:119
  46.7 3.6 %while.13 = (s32[]{:T(128)}, f32[40,64,128]{2,1,0:T(8,128)S(1)}, bf16[2,40,64,128]{3,2,1,0:T(8,128)(2,1)S(1)}, f32[2,40]{1,0:T(2,128)S(1)}, f32[2,40,64,128]{3,2,1,0:T(8,128)}, /*index=5*/s32[]{:T(128)}, s32[]{:T(128)}) while((s32[]{:T(128)}, f32[40,64,128]{2,1,0:T(8,128)S(1)}, bf16[2,40,64,128]{3,2,1,0:T(8,128)(2,1)S(1)}, ...), condition=%wide.region_3.4_spmd.clone, body=%wide.region_2.3_spmd.clone.sunk | while | flops 1310723 | bytes 5898820 | solution.py:131
  47.0 1.5 bitcast_add_fusion.3
  48.8 1.5 bitcast_add_fusion.3
  50.3 1.1 convert_element_type.145
  51.4 1.6 collective-permute-start.1
  53.0 0.6 dynamic-slice.1
  54.4 26.4 %all-reduce = f32[320]{0:T(512)S(1)} all-reduce(f32[320]{0:T(512)S(1)} %dynamic-update-slice), channel_id=2, replica_groups=mesh['seq'=8,'tensor'=2,'dp'=2] {'seq'}, use_global_device_ids=true, to_apply=%add | all-reduce | flops 320 | bytes 2560
  80.9 1.1 fusion.24
  82.1 2.1 %collective-permute-start.2 = (bf16[40,64,128]{2,1,0:T(8,128)(2,1)}, bf16[40,64,128]{2,1,0:T(8,128)(2,1)}, u32[]{:S(2)}, u32[]{:S(2)}) collective-permute-start(bf16[40,64,128]{2,1,0:T(8,128)(2,1)} %fusion.24), channel_id=1, source_target_pairs={{0,8},{4,12},{8,16},{12,20},{16,24},{20,28},{1,9},{5,13},{9,17},{1... | collective-permute-start | bytes 1966088 | tf_op jit(solution)/shard_map/ppermute | solution.py:32
  84.2 0.6 copy.98
  84.9 3.0 %copy.76 = bf16[512,2560]{0,1:T(8,128)(2,1)S(1)} copy(bf16[512,2560]{1,0:T(8,128)(2,1)} %param.16) | data formatting | bytes 5242880 | tf_op args[2]
  88.1 6.4 %collective-permute-done.2 = bf16[40,64,128]{2,1,0:T(8,128)(2,1)} collective-permute-done((bf16[40,64,128]{2,1,0:T(8,128)(2,1)}, bf16[40,64,128]{2,1,0:T(8,128)(2,1)}, u32[]{:S(2)}, u32[]{:S(2)}) %collective-permute-start.2) | collective-permute-done | bytes 655392 | tf_op jit(solution)/shard_map/ppermute | solution.py:32
  94.5 4.6 %collective-permute-start.3 = (bf16[40,64,128]{2,1,0:T(8,128)(2,1)}, bf16[40,64,128]{2,1,0:T(8,128)(2,1)S(1)}, u32[]{:S(2)}, u32[]{:S(2)}) collective-permute-start(bf16[40,64,128]{2,1,0:T(8,128)(2,1)} %collective-permute-done.2), channel_id=1, source_target_pairs={{0,8},{4,12},{8,16},{12,20},{16,24},{20,28},{1,9},{5,13},{9,17},{1... | collective-permute-start | bytes 1966088 | tf_op jit(solution)/shard_map/ppermute | solution.py:32
  99.3 2.2 %fusion.53 = f32[2,256,40,64]{1,3,2,0:T(8,128)S(1)} fusion(bf16[2,256,128,1]{2,1,3,0:T(8,128)(2,1)S(1)} %bitcast.88, bf16[2,40,64,128]{3,2,1,0:T(8,128)(2,1)} %copy-done.1), kind=kOutput, calls=%fused_computation.122 | convolution fusion | flops 335544320 | bytes 6684672 | tf_op jit(solution)/shard_map/ctn,chpn->cthp/dot_general | solution.py:132
  101.5 7.5 %collective-permute-done.3 = bf16[40,64,128]{2,1,0:T(8,128)(2,1)S(1)} collective-permute-done((bf16[40,64,128]{2,1,0:T(8,128)(2,1)}, bf16[40,64,128]{2,1,0:T(8,128)(2,1)S(1)}, u32[]{:S(2)}, u32[]{:S(2)}) %collective-permute-start.3) | collective-permute-done | bytes 655392 | tf_op jit(solution)/shard_map/ppermute | solution.py:32
  109.0 2.1 %fusion.33 = f32[2,256,40,64]{1,3,2,0:T(8,128)S(1)} fusion(bf16[2,256,128,1]{2,1,3,0:T(8,128)(2,1)S(1)} %bitcast.89, bf16[40,64,128]{2,1,0:T(8,128)(2,1)S(1)} %collective-permute-done.3, bf16[40,64,128]{2,1,0:T(8,128)(2,1)} %collective-permute-done.2, bf16[40,64,128]{2,1,0:T(8,128)(2,1)S(1)} %collective-permute-done.1, f32[40]{0:T(128)S(1)} %fusion.41, ...), kind=kOutput, calls=%fused_computation.57 | convolution fusion | flops 338493440 | bytes 7340353 | tf_op jit(solution)/shard_map/ctn,hpn->cthp/dot_general | solution.py:149
  111.3 8.6 %fusion.11 = bf16[2,256,40,64]{1,3,2,0:T(8,128)(2,1)} fusion(f32[2,256,40,64]{1,3,2,0:T(8,128)S(1)} %fusion.33, f32[2,256,40,64]{1,3,2,0:T(8,128)S(1)} %fusion.53, f32[2,256,40]{1,2,0:T(8,128)S(1)} %copy-done.10, f32[40]{0:T(128)S(1)} %copy-done.27, f32[2,256,40]{1,2,0:T(8,128)S(1)} %copy-done.9, f32[40,2,256]{2,0,1:T(8,128)S(1)} %bitcast.94, ...), kind=kOutput, calls=%fused_computation.19 | convolution fusion | flops 713031680 | bytes 16711840 | tf_op jit(solution)/shard_map/hcts,cshp->cthp/dot_general | solution.py:140
  119.9 4.5 %copy.75 = bf16[2,256,40,64]{1,0,3,2:T(2,128)(2,1)S(1)} copy(bf16[2,256,40,64]{1,3,2,0:T(8,128)(2,1)} %fusion.11) | data formatting | bytes 5242880 | tf_op jit(solution)/shard_map/convert_element_type | solution.py:153
  125.1 2.7 %multiply_reduce_fusion = (f32[512]{0:T(512)S(1)}, bf16[512,2560]{0,1:T(8,128)(2,1)S(1)}) fusion(bf16[512,2560]{0,1:T(8,128)(2,1)S(1)} %copy.76, bf16[512,2560]{0,1:T(8,128)(2,1)S(1)} %bitcast.85, f32[2560]{0:T(1024)S(1)} %copy-done.12), kind=kLoop, calls=%fused_computation.25 | loop fusion | flops 14417408 | bytes 7876608 | tf_op jit(solution)/shard_map/reduce_sum | solution.py:155
  127.9 3.6 %convolution_convert_fusion.1 = bf16[256,2560]{1,0:T(8,128)(2,1)S(1)} fusion(bf16[2560,2560]{1,0:T(8,128)(2,1)S(1)} %bitcast.84, bf16[512,2560]{0,1:T(8,128)(2,1)S(1)} %get-tuple-element.70), kind=kOutput, calls=%fused_computation.31 | convolution fusion | flops 3356098560 | bytes 15728640 | tf_op jit(solution)/shard_map/dot_general | solution.py:166
  131.5 3.6 %convolution_convert_fusion = bf16[256,2560]{1,0:T(8,128)(2,1)S(1)} fusion(bf16[2560,2560]{1,0:T(8,128)(2,1)S(1)} %bitcast.84, bf16[512,2560]{0,1:T(8,128)(2,1)S(1)} %get-tuple-element.70), kind=kOutput, calls=%fused_computation.30 | convolution fusion | flops 3356098560 | bytes 15728640 | tf_op jit(solution)/shard_map/dot_general | solution.py:166
  135.1 0.9 constant_dynamic-slice_fusion.3
  136.0 1.5 collective-permute-start.4
  137.5 0.9 constant_dynamic-slice_fusion.2
  138.9 22.9 %psum.7 = f32[512]{0:T(512)S(1)} all-reduce(f32[512]{0:T(512)S(1)} %get-tuple-element.69), channel_id=1, replica_groups=mesh['seq'=8,'tensor'=2,'dp'=2] {'tensor'}, use_global_device_ids=true, to_apply=%region_7.8 | all-reduce | flops 512 | bytes 4096 | tf_op jit(solution)/shard_map/psum | solution.py:155
  161.8 1.3 multiply_convert_fusion.7
  163.3 1.1 pad_maximum_fusion.1
  (114 shorter events, 5.2 us)
Async XLA Ops:
  2.3 16.6 %collective-permute-start = (bf16[3,2944]{1,0:T(4,128)(2,1)S(1)}, bf16[3,2944]{1,0:T(4,128)(2,1)S(1)}, u32[]{:S(2)}, u32[]{:S(2)}) collective-permute-start(bf16[3,2944]{1,0:T(4,128)(2,1)S(1)} %pad_maximum_fusion.3), channel_id=1, source_target_pairs={{0,4},{4,8},{8,12},{12,16},{16,20},{20,24},{24,28},{1,5},{5,9},{9,... | collective-permute-start | bytes 53000 | tf_op jit(solution)/shard_map/ppermute | solution.py:32
  11.0 0.6 copy-start.7
  11.8 9.3 %copy-start.13 = (f32[40,2]{0,1:T(2,128)}, f32[40,2]{0,1:T(2,128)S(1)}, u32[]{:S(2)}) copy-start(f32[40,2]{0,1:T(2,128)S(1)} %slice_reduce_fusion) | copy-start | bytes 964
  14.5 7.8 %copy-start.15 = (s32[512]{0:T(512)S(1)}, s32[512]{0:T(512)}, u32[]{:S(2)}) copy-start(s32[512]{0:T(512)} %param.18) | copy-start | bytes 6148
  14.5 7.9 %copy-start.6 = (bf16[512,256]{1,0:T(8,128)(2,1)S(1)}, bf16[512,256]{1,0:T(8,128)(2,1)}, u32[]{:S(2)}) copy-start(bf16[512,256]{1,0:T(8,128)(2,1)} %param.15) | copy-start | bytes 786436
  20.9 1.3 copy-start.21
  21.7 0.5 copy-start.23
  22.4 0.8 copy-start.16
  22.4 0.8 copy-start.17
  22.4 0.9 copy-start.18
  22.4 1.5 copy-start.19
  36.8 5.0 %copy-start.26 = (f32[40,1]{0,1:T(1,128)S(1)}, f32[40,1]{0,1:T(1,128)}, u32[]{:S(2)}) copy-start(f32[40,1]{0,1:T(1,128)} %slice.164) | copy-start | bytes 484
  36.8 5.0 %copy-start.4 = (f32[40,512]{1,0:T(8,128)S(1)}, f32[40,512]{1,0:T(8,128)}, u32[]{:S(2)}) copy-start(f32[40,512]{1,0:T(8,128)} %get-tuple-element.76) | copy-start | bytes 245764
  36.8 5.0 %copy-start.14 = (f32[40,2]{0,1:T(2,128)S(1)}, f32[40,2]{0,1:T(2,128)}, u32[]{:S(2)}) copy-start(f32[40,2]{0,1:T(2,128)} %copy-done.13) | copy-start | bytes 964
  36.8 5.0 %copy-start.20 = (pred[2,256]{1,0:T(4,128)(4,1)S(1)}, pred[2,256]{1,0:T(4,128)(4,1)}, u32[]{:S(2)}) copy-start(pred[2,256]{1,0:T(4,128)(4,1)} %get-tuple-element.89) | copy-start | bytes 1540
  36.8 5.0 %copy-start.22 = (pred[2,256]{1,0:T(4,128)(4,1)S(1)}, pred[2,256]{1,0:T(4,128)(4,1)}, u32[]{:S(2)}) copy-start(pred[2,256]{1,0:T(4,128)(4,1)} %copy-done.21) | copy-start | bytes 1540
  36.8 5.8 %copy-start.2 = (bf16[512,128]{1,0:T(8,128)(2,1)S(1)}, bf16[512,128]{1,0:T(8,128)(2,1)}, u32[]{:S(2)}) copy-start(bf16[512,128]{1,0:T(8,128)(2,1)} %get-tuple-element.71) | copy-start | bytes 393220
  42.6 4.1 %copy-start.24 = (f32[40,2]{0,1:T(2,128)S(1)}, f32[40,2]{0,1:T(2,128)}, u32[]{:S(2)}) copy-start(f32[40,2]{0,1:T(2,128)} %copy-done.23) | copy-start | bytes 964
  46.7 6.2 %copy-start.28 = (u32[32]{0:T(128)S(1)}, u32[32]{0:T(128)}, u32[]{:S(2)}) copy-start(u32[32]{0:T(128)} %constant.95) | copy-start | bytes 388
  46.7 7.4 %copy-start.25 = (f32[40]{0:T(128)S(1)}, f32[40]{0:T(128)}, u32[]{:S(2)}) copy-start(f32[40]{0:T(128)} %get-tuple-element.67) | copy-start | bytes 484
  50.3 34.5 %copy-start.1 = (bf16[2,40,64,128]{3,2,1,0:T(8,128)(2,1)}, bf16[2,40,64,128]{3,2,1,0:T(8,128)(2,1)S(1)}, u32[]{:S(2)}) copy-start(bf16[2,40,64,128]{3,2,1,0:T(8,128)(2,1)S(1)} %get-tuple-element.33) | copy-start | bytes 3932164
  50.3 33.9 %copy-start.5 = (f32[40,512]{1,0:T(8,128)S(1)}, f32[40,512]{1,0:T(8,128)}, u32[]{:S(2)}) copy-start(f32[40,512]{1,0:T(8,128)} %get-tuple-element.76) | copy-start | bytes 245764
  51.4 29.5 %collective-permute-start.1 = (bf16[40,64,128]{2,1,0:T(8,128)(2,1)}, bf16[40,64,128]{2,1,0:T(8,128)(2,1)S(1)}, u32[]{:S(2)}, u32[]{:S(2)}) collective-permute-start(bf16[40,64,128]{2,1,0:T(8,128)(2,1)} %convert_element_type.145), channel_id=1, source_target_pairs={{0,4},{4,0},{8,12},{12,8},{16,20},{20,16},{24,28},{28,24},{1,5},{5... | collective-permute-start | bytes 1966088 | tf_op jit(solution)/shard_map/ppermute | solution.py:40
  82.1 12.4 %collective-permute-start.2 = (bf16[40,64,128]{2,1,0:T(8,128)(2,1)}, bf16[40,64,128]{2,1,0:T(8,128)(2,1)}, u32[]{:S(2)}, u32[]{:S(2)}) collective-permute-start(bf16[40,64,128]{2,1,0:T(8,128)(2,1)} %fusion.24), channel_id=1, source_target_pairs={{0,8},{4,12},{8,16},{12,20},{16,24},{20,28},{1,9},{5,13},{9,17},{1... | collective-permute-start | bytes 1966088 | tf_op jit(solution)/shard_map/ppermute | solution.py:32
  84.9 14.2 %copy-start.3 = (bf16[512,128]{1,0:T(8,128)(2,1)S(1)}, bf16[512,128]{1,0:T(8,128)(2,1)}, u32[]{:S(2)}) copy-start(bf16[512,128]{1,0:T(8,128)(2,1)} %get-tuple-element.71) | copy-start | bytes 393220
  94.5 14.5 %collective-permute-start.3 = (bf16[40,64,128]{2,1,0:T(8,128)(2,1)}, bf16[40,64,128]{2,1,0:T(8,128)(2,1)S(1)}, u32[]{:S(2)}, u32[]{:S(2)}) collective-permute-start(bf16[40,64,128]{2,1,0:T(8,128)(2,1)} %collective-permute-done.2), channel_id=1, source_target_pairs={{0,8},{4,12},{8,16},{12,20},{16,24},{20,28},{1,9},{5,13},{9,17},{1... | collective-permute-start | bytes 1966088 | tf_op jit(solution)/shard_map/ppermute | solution.py:32
  109.0 2.2 %copy-start = (bf16[2,256,40,64]{1,0,3,2:T(2,128)(2,1)S(1)}, bf16[2,256,40,64]{1,0,3,2:T(2,128)(2,1)}, u32[]{:S(2)}) copy-start(bf16[2,256,40,64]{1,0,3,2:T(2,128)(2,1)} %reshape.140) | copy-start | bytes 7864324
  109.0 2.2 %copy-start.8 = (f32[40,2,256]{2,0,1:T(8,128)S(1)}, f32[40,2,256]{2,0,1:T(8,128)}, u32[]{:S(2)}) copy-start(f32[40,2,256]{2,0,1:T(8,128)} %copy-done.7) | copy-start | bytes 245764
  109.0 2.2 %copy-start.9 = (f32[2,256,40]{1,2,0:T(8,128)S(1)}, f32[2,256,40]{1,2,0:T(8,128)}, u32[]{:S(2)}) copy-start(f32[2,256,40]{1,2,0:T(8,128)} %get-tuple-element.73) | copy-start | bytes 245764
  109.0 2.2 %copy-start.10 = (f32[2,256,40]{1,2,0:T(8,128)S(1)}, f32[2,256,40]{1,2,0:T(8,128)}, u32[]{:S(2)}) copy-start(f32[2,256,40]{1,2,0:T(8,128)} %get-tuple-element.74) | copy-start | bytes 245764
  109.0 2.2 %copy-start.11 = (f32[5,2,8,256]{3,2,0,1:T(8,128)S(1)}, f32[5,2,8,256]{3,2,0,1:T(8,128)}, u32[]{:S(2)}) copy-start(f32[5,2,8,256]{3,2,0,1:T(8,128)} %copy.98) | copy-start | bytes 245764
  109.0 2.2 %copy-start.27 = (f32[40]{0:T(128)S(1)}, f32[40]{0:T(128)}, u32[]{:S(2)}) copy-start(f32[40]{0:T(128)} %param.23) | copy-start | bytes 484
  109.0 18.8 %slice-start = ((s8[13107200]{0:T(1024)(128)(4,1)}), s8[4194304]{0:T(1024)(128)(4,1)S(1)}, s32[]{:S(2)}) async-start(s8[13107200]{0:T(1024)(128)(4,1)} %bitcast.83), calls=%async_computation | async-start | bytes 8388608
  111.2 16.6 %slice-start.1 = ((s8[13107200]{0:T(1024)(128)(4,1)}), s8[4194304]{0:T(1024)(128)(4,1)S(1)}, s32[]{:S(2)}) async-start(s8[13107200]{0:T(1024)(128)(4,1)} %bitcast.83), calls=%async_computation.1 | async-start | bytes 8388608
  111.3 16.6 %slice-start.2 = ((s8[13107200]{0:T(1024)(128)(4,1)}), s8[4194304]{0:T(1024)(128)(4,1)S(1)}, s32[]{:S(2)}) async-start(s8[13107200]{0:T(1024)(128)(4,1)} %bitcast.83), calls=%async_computation.2 | async-start | bytes 8388608
  111.3 16.6 %slice-start.3 = ((s8[13107200]{0:T(1024)(128)(4,1)}), s8[524288]{0:T(1024)(128)(4,1)S(1)}, s32[]{:S(2)}) async-start(s8[13107200]{0:T(1024)(128)(4,1)} %bitcast.83), calls=%async_computation.3 | async-start | bytes 1048576
  124.4 0.7 copy-start.12
  136.0 25.8 %collective-permute-start.4 = (bf16[256,1280]{1,0:T(8,128)(2,1)}, bf16[256,1280]{1,0:T(8,128)(2,1)}, u32[]{:S(2)}, u32[]{:S(2)}) collective-permute-start(bf16[256,1280]{1,0:T(8,128)(2,1)} %constant_dynamic-slice_fusion.3), channel_id=1, source_target_pairs={{0,2},{2,0},{1,3},{3,1},{4,6},{6,4},{5,7},{7,5},{8,10},{10,8},{9,1... | collective-permute-start | bytes 1966088 | tf_op jit(solution)/shard_map/ppermute | solution.py:174
  138.4 24.7 %collective-permute-start.5 = (bf16[256,1280]{1,0:T(8,128)(2,1)}, bf16[256,1280]{1,0:T(8,128)(2,1)S(1)}, u32[]{:S(2)}, u32[]{:S(2)}) collective-permute-start(bf16[256,1280]{1,0:T(8,128)(2,1)} %constant_dynamic-slice_fusion.2), channel_id=1, source_target_pairs={{0,2},{2,0},{1,3},{3,1},{4,6},{6,4},{5,7},{7,5},{8,10},{10,8},{9,1... | collective-permute-start | bytes 1966088 | tf_op jit(solution)/shard_map/ppermute | solution.py:174

commit v2 on v0

v2 whole, which is shorter than its diff:
```python
import functools

import jax
import jax.numpy as jnp
from jax import lax
from jax.experimental import pallas as pl
from jax.experimental.pallas import tpu as pltpu
from jax.sharding import PartitionSpec as P

SPAN = 256
HEADS_PAD = 128
EXTRA = 16
VMEM_BYTES = 48 * 1024 * 1024


def shifted(block, axis, distance):
    count = lax.axis_size(axis)
    return lax.ppermute(block, axis, [(i, i + distance) for i in range(count - distance)])


def group_lanes(width):
    return 256 if width % 256 == 0 else 128


def silu(v):
    return v / (1.0 + jnp.exp(-v))


def spread_heads(columns, width, lanes):
    rows = columns.shape[0]
    lane = lax.broadcasted_iota(jnp.int32, (rows, 128), 1)
    per_tile = 128 // width
    tiles = []
    for tile in range(lanes // 128):
        value = jnp.broadcast_to(columns[:, tile * per_tile : tile * per_tile + 1], (rows, 128))
        for k in range(1, per_tile):
            head = tile * per_tile + k
            value = jnp.where(
                lane >= k * width, jnp.broadcast_to(columns[:, head : head + 1], (rows, 128)), value
            )
        tiles.append(value)
    return jnp.concatenate(tiles, axis=1)


def conv_taps(ext, weights, keeps, rows):
    wide = weights.shape[1]
    total = weights[0:1] * ext[pl.ds(8, rows), :wide]
    for k in range(1, weights.shape[0]):
        total = total + jnp.where(keeps[k - 1][:, :wide], weights[k : k + 1] * ext[pl.ds(8 - k, rows), :wide], 0.0)
    return silu(total)


def states_kernel(
    head_size,
    x_ref, rim_x_ref, bc_ref, rim_bc_ref, step_ref, rate_ref, flags_ref, conv_x_ref, conv_bc_ref,
    mixed_ref, bc_out_ref, cum_ref, cum_t_ref, step_t_ref, gain_t_ref, fresh_ref, decay_ref, msg_ref,
    ext, tail_t, b_t,
):
    rows, width = x_ref.shape
    blocks = rows // SPAN
    size = group_lanes(width)
    per_group = size // head_size
    state_size = bc_ref.shape[1] // 2
    flags = flags_ref[...]
    taps = conv_x_ref.shape[0]
    keeps = [
        jnp.broadcast_to(flags[:, k : k + 1], (rows, ext.shape[1])) > 0.5 for k in range(taps - 1)
    ]
    carried = jnp.broadcast_to(flags[:, 3:4], (rows, HEADS_PAD)) > 0.5
    in_tail = jnp.broadcast_to(flags[:, 4:5], (rows, HEADS_PAD)) > 0.5

    ext[0:8, :] = rim_bc_ref[...]
    ext[8 : 8 + rows, :] = bc_ref[...].astype(jnp.float32)
    mixed_bc = conv_taps(ext, conv_bc_ref[...], keeps, rows)
    bc_out_ref[...] = mixed_bc.astype(jnp.bfloat16)
    row_id = lax.broadcasted_iota(jnp.int32, (SPAN, SPAN), 0)
    col_id = lax.broadcasted_iota(jnp.int32, (SPAN, SPAN), 1)
    upper = (row_id <= col_id).astype(jnp.float32)
    for b in range(blocks):
        span = slice(b * SPAN, (b + 1) * SPAN)
        b_t[:, span] = mixed_bc[span, :state_size].T.astype(jnp.bfloat16)
        cum = jnp.dot(
            rate_ref[:, span], upper,
            precision=lax.Precision.HIGHEST, preferred_element_type=jnp.float32,
        )
        cum_ref[:, span] = cum
        cum_t = cum.T
        step_t = step_ref[:, span].T
        cum_t_ref[span, :] = cum_t
        step_t_ref[span, :] = step_t
        gain_t_ref[span, :] = jnp.where(carried[span], jnp.exp(cum_t), 0.0)
        tail_t[span, :] = jnp.where(
            in_tail[span], jnp.exp(cum_t[SPAN - 1 : SPAN] - cum_t), 0.0
        ) * step_t

    def group(c, unused):
        lanes = pl.ds(pl.multiple_of(c * size, size), size)
        turn = lax.rem(HEADS_PAD - c * per_group, HEADS_PAD)
        ext[0:8, :size] = rim_x_ref[:, lanes]
        ext[8 : 8 + rows, :size] = x_ref[:, lanes].astype(jnp.float32)
        mixed = conv_taps(ext, conv_x_ref[:, lanes], keeps, rows).astype(jnp.bfloat16)
        mixed_ref[:, lanes] = mixed
        weight = spread_heads(pltpu.roll(tail_t[...], turn, 1), head_size, size)
        weighted = (mixed.astype(jnp.float32) * weight).astype(jnp.bfloat16)
        running = None
        through = None
        for b in range(blocks):
            span = slice(b * SPAN, (b + 1) * SPAN)
            fresh = jnp.dot(b_t[:, span], weighted[span], preferred_element_type=jnp.float32)
            ends = gain_t_ref[(b + 1) * SPAN - 8 : (b + 1) * SPAN, :]
            decay = spread_heads(pltpu.roll(ends, turn, 1), head_size, size)[7:8]
            fresh_ref[b, :, lanes] = fresh
            decay_ref[b, :, lanes] = jnp.broadcast_to(decay, (8, size))
            running = fresh if b == 0 else decay * running + fresh
            through = decay if b == 0 else through * decay
        msg_ref[0:state_size, lanes] = running.astype(jnp.bfloat16)
        high = through.astype(jnp.bfloat16)
        low = through - high.astype(jnp.float32)
        both = jnp.concatenate(
            [
                jnp.broadcast_to(high.astype(jnp.float32), (8, size)),
                jnp.broadcast_to(low, (8, size)),
            ]
        )
        msg_ref[state_size : state_size + EXTRA, lanes] = both.astype(jnp.bfloat16)
        return unused

    lax.fori_loop(0, width // size, group, 0)


def mix_kernel(
    head_size,
    mixed_ref, bc_ref, cum_ref, cum_t_ref, step_t_ref, ids_col_ref, ids_row_ref, skip_ref,
    out_ref,
    scores,
):
    width = mixed_ref.shape[1]
    size = group_lanes(width)
    per_group = size // head_size
    state_size = bc_ref.shape[1] // 2
    half = SPAN // 2
    row_id = lax.broadcasted_iota(jnp.int32, (SPAN, SPAN), 0)
    col_id = lax.broadcasted_iota(jnp.int32, (SPAN, SPAN), 1)
    raw = lax.dot_general(
        bc_ref[:, state_size:], bc_ref[:, :state_size], (((1,), (1,)), ((), ())),
        preferred_element_type=jnp.float32,
    )
    same = (ids_col_ref[...] == ids_row_ref[...]) & (col_id <= row_id)
    scores[...] = jnp.where(same, raw, 0.0)

    def group(c, unused):
        lanes = pl.ds(pl.multiple_of(c * size, size), size)
        turn = lax.rem(HEADS_PAD - c * per_group, HEADS_PAD)
        cum_t = pltpu.roll(cum_t_ref[...], turn, 1)
        steps = spread_heads(pltpu.roll(step_t_ref[...], turn, 1), head_size, size)
        x = mixed_ref[:, lanes].astype(jnp.float32)
        stepped = (x * steps).astype(jnp.bfloat16)
        tops, bottoms = [], []
        for k in range(per_group):
            own = slice(k * head_size, (k + 1) * head_size)
            column = cum_t[:, k : k + 1]
            row = cum_ref[pl.ds(c * per_group + k, 1), :]
            top = scores[:half, :half] * jnp.exp(jnp.minimum(column[:half] - row[:, :half], 0.0))
            bottom = scores[half:, :] * jnp.exp(jnp.minimum(column[half:] - row, 0.0))
            tops.append(
                jnp.dot(
                    top.astype(jnp.bfloat16), stepped[:half, own],
                    preferred_element_type=jnp.float32,
                )
            )
            bottoms.append(
                jnp.dot(
                    bottom.astype(jnp.bfloat16), stepped[:, own],
                    preferred_element_type=jnp.float32,
                )
            )
        skip = skip_ref[:, lanes]
        out_ref[:half, lanes] = jnp.concatenate(tops, axis=1) + skip * x[:half]
        out_ref[half:, lanes] = jnp.concatenate(bottoms, axis=1) + skip * x[half:]
        return unused

    lax.fori_loop(0, width // size, group, 0)


def gate_kernel(
    head_size,
    state_ref, bc_ref, gain_t_ref, part_ref, z_ref, norm_ref,
    out_ref, squares_ref,
):
    width = part_ref.shape[1]
    size = group_lanes(width)
    per_group = size // head_size
    state_size = bc_ref.shape[1] // 2
    c_vals = bc_ref[:, state_size:]

    def group(c, squares):
        lanes = pl.ds(pl.multiple_of(c * size, size), size)
        turn = lax.rem(HEADS_PAD - c * per_group, HEADS_PAD)
        gain = spread_heads(pltpu.roll(gain_t_ref[...], turn, 1), head_size, size)
        reached = jnp.dot(c_vals, state_ref[:, lanes], preferred_element_type=jnp.float32)
        y = (part_ref[:, lanes] + gain * reached).astype(jnp.bfloat16).astype(jnp.float32)
        gated = y * silu(z_ref[:, lanes].astype(jnp.float32))
        out_ref[:, lanes] = (gated * norm_ref[:, lanes]).astype(jnp.bfloat16)
        square = gated * gated
        for tile in range(size // 128):
            squares = squares + square[:, tile * 128 : (tile + 1) * 128]
        return squares

    squares_ref[...] = lax.fori_loop(
        0, width // size, group, jnp.zeros((SPAN, 128), jnp.float32)
    )


def call(kernel, out_shape, scratch, flops, moved, *operands):
    return pl.pallas_call(
        kernel,
        out_shape=out_shape,
        in_specs=[pl.BlockSpec(memory_space=pltpu.VMEM)] * len(operands),
        out_specs=jax.tree.map(lambda _: pl.BlockSpec(memory_space=pltpu.VMEM), out_shape),
        scratch_shapes=scratch,
        compiler_params=pltpu.CompilerParams(vmem_limit_bytes=VMEM_BYTES),
        cost_estimate=pl.CostEstimate(flops=flops, bytes_accessed=moved, transcendentals=0),
    )(*operands)


def split_message(message):
    state_size = message.shape[0] - EXTRA
    wide = message.astype(jnp.float32)
    return wide[:state_size], wide[state_size : state_size + 1] + wide[state_size + 8 : state_size + 9]


def merge(near, far):
    near_state, near_decay = near
    far_state, far_decay = far
    return near_state + near_decay * far_state, near_decay * far_decay


def pack_message(pair):
    state, decay = pair
    width = state.shape[1]
    high = decay.astype(jnp.bfloat16)
    low = (decay - high.astype(jnp.float32)).astype(jnp.bfloat16)
    return jnp.concatenate(
        [
            state.astype(jnp.bfloat16),
            jnp.broadcast_to(high, (8, width)),
            jnp.broadcast_to(low, (8, width)),
        ]
    )


def pass_state(message):
    count = lax.axis_size("seq")
    odd = (lax.axis_index("seq") % 2) == 1
    other = lax.ppermute(message, "seq", [(i, i ^ 1) for i in range(count)])
    first = split_message(jnp.where(odd, other, message))
    second = split_message(jnp.where(odd, message, other))
    entering = shifted(pack_message(merge(second, first)), "seq", 2)
    reach = 1
    while reach < count // 4:
        farther = shifted(entering, "seq", 2 * reach)
        joined = merge(split_message(entering), split_message(farther))
        reach *= 2
        if reach < count // 4:
            entering = pack_message(joined)
        else:
            entering = joined
    if reach == 1:
        entering = split_message(entering)
    alone = split_message(other)
    return jnp.where(odd, merge(alone, entering)[0], entering[0])


def local(
    x_stream,
    bc_stream,
    z_gate,
    dt_stream,
    doc_ids,
    conv_x,
    conv_bc,
    a_log,
    dt_bias,
    d_skip,
    norm_gain,
    w_out,
):
    rows, width = x_stream.shape
    heads = dt_stream.shape[0]
    head_size = width // heads
    bc_width = bc_stream.shape[1]
    state_size = bc_width // 2
    taps = conv_x.shape[0]
    blocks = rows // SPAN
    edge = rows - taps + 1
    f32, bf16 = jnp.float32, jnp.bfloat16
    own_ids = doc_ids.astype(f32)
    tail_ids = jnp.broadcast_to(own_ids[edge:].astype(bf16)[:, None], (taps - 1, 128))
    rim = shifted(
        jnp.concatenate([x_stream[edge:], bc_stream[edge:], tail_ids], axis=1), "seq", 1
    )
    step = jax.nn.softplus(dt_stream.astype(f32) + dt_bias[:, None])
    rate = -jnp.exp(a_log)[:, None] * step
    step = jnp.pad(step, ((0, HEADS_PAD - heads), (0, 0)))
    rate = jnp.pad(rate, ((0, HEADS_PAD - heads), (0, 0)))
    rim_wide = jnp.pad(rim.astype(f32), ((8 - taps + 1, 0), (0, 0)))
    rim_ids = jnp.where(lax.axis_index("seq") == 0, -1.0, rim[:, width + bc_width].astype(f32))
    ext_ids = jnp.concatenate([rim_ids, own_ids])
    block_ids = own_ids.reshape(blocks, SPAN)
    prior = jnp.concatenate([ext_ids[taps - 2][None], own_ids[SPAN - 1 :: SPAN][: blocks - 1]])
    columns = [(ext_ids[taps - 1 - k : taps - 1 - k + rows] == own_ids) for k in range(1, taps)]
    columns.append((block_ids == prior[:, None]).reshape(rows))
    columns.append((block_ids == block_ids[:, -1:]).reshape(rows))
    flags = jnp.stack([c.astype(f32) for c in columns], axis=1)

    shape = jax.ShapeDtypeStruct
    mixed, mixed_bc, cum, cum_t, step_t, gain_t, fresh, decay, message = call(
        functools.partial(states_kernel, head_size),
        (
            shape((rows, width), bf16),
            shape((rows, bc_width), bf16),
            shape((HEADS_PAD, rows), f32),
            shape((rows, HEADS_PAD), f32),
            shape((rows, HEADS_PAD), f32),
            shape((rows, HEADS_PAD), f32),
            shape((blocks, state_size, width), f32),
            shape((blocks, 8, width), f32),
            shape((state_size + EXTRA, width), bf16),
        ),
        [
            pltpu.VMEM((rows + 8, max(bc_width, group_lanes(width))), f32),
            pltpu.VMEM((rows, HEADS_PAD), f32),
            pltpu.VMEM((state_size, rows), bf16),
        ],
        2 * rows * state_size * width,
        8 * rows * width,
        x_stream, rim_wide[:, :width], bc_stream, rim_wide[:, width : width + bc_width], step, rate,
        flags, conv_x.astype(f32), conv_bc.astype(f32),
    )
    skip_row = jnp.repeat(d_skip, head_size)[None, :]
    parts = []
    for b in range(blocks):
        span = slice(b * SPAN, (b + 1) * SPAN)
        parts.append(
            call(
                functools.partial(mix_kernel, head_size),
                shape((SPAN, width), f32),
                [pltpu.VMEM((SPAN, SPAN), f32)],
                2 * SPAN * SPAN * width * 16,
                8 * SPAN * width,
                mixed[span], mixed_bc[span], cum[:, span], cum_t[span], step_t[span],
                own_ids[span][:, None], own_ids[span][None, :], skip_row,
            )
        )
    state = pass_state(message)

    members = lax.axis_size("tensor")
    member = lax.axis_index("tensor")
    out_width = w_out.shape[1] // members
    pieces = []
    for b in range(blocks):
        span = slice(b * SPAN, (b + 1) * SPAN)
        scaled, squares = call(
            functools.partial(gate_kernel, head_size),
            (shape((SPAN, width), bf16), shape((SPAN, 128), f32)),
            [],
            2 * SPAN * state_size * width,
            12 * SPAN * width,
            state.astype(bf16), mixed_bc[span], gain_t[span], parts[b], z_gate[span],
            norm_gain[None, :],
        )
        if b + 1 < blocks:
            state = decay[b, 0:1] * state + fresh[b]
        product = jnp.dot(scaled, w_out, preferred_element_type=f32).astype(bf16)
        total = lax.dynamic_slice_in_dim(product, member * out_width, out_width, 1).astype(f32)
        square = jnp.sum(squares, axis=1, keepdims=True)
        high = square.astype(bf16)
        low = (square - high.astype(f32)).astype(bf16)
        lane = lax.broadcasted_iota(jnp.int32, (SPAN, 128), 1)
        aside = jnp.where(lane == 0, high, jnp.where(lane == 1, low, jnp.zeros_like(low)))
        for distance in range(1, members):
            target = (member + distance) % members
            block = lax.dynamic_slice_in_dim(product, target * out_width, out_width, 1)
            route = [(i, (i + distance) % members) for i in range(members)]
            got = lax.ppermute(jnp.concatenate([block, aside], axis=1), "tensor", route)
            total = total + got[:, :out_width].astype(f32)
            square = square + jnp.sum(got[:, out_width : out_width + 2].astype(f32), axis=1, keepdims=True)
        inv_norm = lax.rsqrt(square / (width * members) + 1e-05)
        pieces.append((total * inv_norm).astype(bf16))
    return jnp.concatenate(pieces)


def solution(mesh):
    return jax.shard_map(
        local,
        mesh=mesh,
        in_specs=(
            P(("dp", "seq"), "tensor"),
            P(("dp", "seq"), None),
            P(("dp", "seq"), "tensor"),
            P("tensor", ("dp", "seq")),
            P(("dp", "seq")),
            P(None, "tensor"),
            P(),
            P("tensor"),
            P("tensor"),
            P("tensor"),
            P("tensor"),
            P("tensor", None),
        ),
        out_specs=P(("dp", "seq"), "tensor"),
        check_vma=False,
    )
```

time: 271 us -> 147 us (0.54)
  waiting for transfers between devices: 115 us -> 50.4 us
  Pallas kernels: 0 us -> 37.8 us
  starting transfers between devices: 45.2 us -> 16.5 us
  matrix products: 33.5 us -> 12.4 us
  other arithmetic: 34.5 us -> 14.1 us
  between operations: 13.8 us -> 0.65 us
  local copies, waits for them, and re-layouts: 22.6 us -> 14.6 us
  blocking collectives: 4.93 us -> 0 us
    reduce_scatter x1 -> x0, waiting for transfers between devices: 42.3 us -> none  [local(): lax.psum_scatter(partial_value.astype(jnp.bfloat16), 'tensor', scatter_di...]
    pallas_call x0 -> x5, Pallas kernels: none -> 37.8 us  [call(): pl.pallas_call(kernel, out_shape=out_shape, in_specs=[pl.BlockSpec(memory...]
    ppermute x10 -> x6, starting transfers between devices: 45.2 us -> 16.5 us  [the longest x3 13 us: shifted(): lax.ppermute(block, axis, [(i, i + distance) for i in range(count - dista...]
    ppermute x10 -> x6, waiting for transfers between devices: 72.8 us -> 50.4 us  [the longest x2 23.5 us: local(): got = lax.ppermute(jnp.concatenate([block, aside], axis=1), 'tensor', route)]
    dot_general x6 -> x2, matrix products: 33.5 us -> 12.4 us  [local(): product = jnp.dot(scaled, w_out, preferred_element_type=f32).astype(bf16)]
    add x9 -> x3, other arithmetic: 12 us -> 0.1 us  [split_message(): wide[state_size:state_size + 1] + wide[state_size + 8:state_size + 9]]
    convert_element_type x3 -> x12, other arithmetic: 13.9 us -> 4.87 us  [the longest x1 1.76 us: local(): state.astype(bf16)]
    reshape x3 -> x1, local copies, waits for them, and re-layouts: 4.98 us -> 0.01 us  [local(): block_ids = own_ids.reshape(blocks, SPAN)]
  transfers between devices with their start and end apart: 11 -> 6, of which waited for: 8 -> 5; matrix products, arithmetic and copies ran while one was open for 6% -> 8% of each run, Pallas kernels for 0% -> 10%
where the time goes in v2:
time: 147 us; the launch traced here: 146 us
  waiting for transfers between devices  50.4 us (34%)
  Pallas kernels  37.8 us (26%)
  starting transfers between devices  16.5 us (11%)
  local copies, waits for them, and re-layouts  14.6 us (10%)
  other arithmetic  14.1 us (10%)
  matrix products  12.4 us (8%)
    pallas_call x5, Pallas kernels, call(): pl.pallas_call(kernel, out_shape=out_shape, in_specs=[pl.BlockSpec(memory...  37.8 us
    ppermute x2, waiting for transfers between devices, local(): got = lax.ppermute(jnp.concatenate([block, aside], axis=1), 'tensor', route)  23.5 us
    ppermute x1, waiting for transfers between devices, pass_state(): other = lax.ppermute(message, 'seq', [(i, i ^ 1) for i in range(count)])  16.1 us
    ppermute x3, starting transfers between devices, shifted(): lax.ppermute(block, axis, [(i, i + distance) for i in range(count - dista...  13 us
    dot_general x2, matrix products, local(): product = jnp.dot(scaled, w_out, preferred_element_type=f32).astype(bf16)  12.4 us
    ppermute x3, waiting for transfers between devices, shifted(): lax.ppermute(block, axis, [(i, i + distance) for i in range(count - dista...  10.7 us
    unnamed x60, local copies, waits for them, and re-layouts  6.43 us
  transfers between devices with their start and end apart: 6, of which 5 were waited for; matrix products, arithmetic and copies ran while one was open for 8% of the time, Pallas kernels for 10%

profile of v2, /device:TPU:0, one launch (start us, length us, event | category | flops | bytes accessed | tf_op | source)
XLA Modules:
  0.0 146.4 jit_solution(1947557058800169591)
XLA Ops:
  0.0 0.7 fusion.18
  0.8 0.7 slice.156
  1.5 0.8 slice.155
  2.3 4.8 %collective-permute-start = (bf16[3,2944]{1,0:T(4,128)(2,1)S(1)}, bf16[3,2944]{1,0:T(4,128)(2,1)S(1)}, u32[]{:S(2)}, u32[]{:S(2)}) collective-permute-start(bf16[3,2944]{1,0:T(4,128)(2,1)S(1)} %pad_maximum_fusion.4), channel_id=1, source_target_pairs={{0,4},{4,8},{8,12},{12,16},{16,20},{20,24},{24,28},{1,5},{5,9},{9,... | collective-permute-start | bytes 53000 | tf_op jit(solution)/shard_map/ppermute | solution.py:18
  7.2 0.7 exponential_negate_fusion
  8.2 1.9 %fusion.10 = (bf16[256,2560]{1,0:T(8,128)(2,1)S(1)}, bf16[256,2560]{1,0:T(8,128)(2,1)S(1)}) fusion(bf16[512,2560]{1,0:T(8,128)(2,1)} %param.14), kind=kLoop, calls=%fused_computation.61 | loop fusion | bytes 5242880 | tf_op jit(solution)/shard_map/slice | solution.py:369
  10.3 0.6 iota_compare_fusion
  11.1 0.8 copy.31.ids_col_ref
  12.0 0.7 broadcast_in_dim_reshape.3.skip_ref
  12.7 0.8 copy.32.ids_col_ref
  13.7 0.5 slice.164
  14.2 0.7 pad_maximum_fusion.6
  15.1 0.6 stack.31
  15.7 0.9 copy.30.flags_ref
  16.6 0.7 pad_convert_fusion.1.rim_bc_ref
  17.3 0.9 copy-done.2
  18.3 12.6 %shard_map.118 = (bf16[512,2560]{1,0:T(8,128)(2,1)S(1)}, bf16[512,256]{1,0:T(8,128)(2,1)S(1)}, f32[128,512]{1,0:T(8,128)S(1)}, f32[512,128]{1,0:T(8,128)S(1)}, f...) custom-call(bf16[512,2560]{1,0:T(8,128)(2,1)} %x_ref.1, ...), custom_call_target="tpu_custom_call" | custom-call | flops 335544320 | bytes 10485760 | tf_op jit(solution)/shard_map/pallas_call | solution.py:215
  30.8 1.5 %collective-permute-start.1 = (bf16[144,2560]{1,0:T(8,128)(2,1)S(1)}, bf16[144,2560]{1,0:T(8,128)(2,1)S(1)}, u32[]{:S(2)}, u32[]{:S(2)}) collective-permute-start(bf16[144,2560]{1,0:T(8,128)(2,1)S(1)} %get-tuple-element.18), channel_id=1, source_target_pairs={{0,4},{4,0},{8,12},{12,8},{16,20},{20,16},{24,28},{28,24},{1,5},{5... | collective-permute-start | bytes 2211848 | tf_op jit(solution)/shard_map/ppermute | solution.py:255
  32.6 16.1 %collective-permute-done.1 = bf16[144,2560]{1,0:T(8,128)(2,1)S(1)} collective-permute-done((bf16[144,2560]{1,0:T(8,128)(2,1)S(1)}, bf16[144,2560]{1,0:T(8,128)(2,1)S(1)}, u32[]{:S(2)}, u32[]{:S(2)}) %collective-permute-start.1) | collective-permute-done | bytes 737312 | tf_op jit(solution)/shard_map/ppermute | solution.py:255
  48.8 0.5 select_convert_fusion.1
  49.7 3.5 %collective-permute-start.2 = (bf16[144,2560]{1,0:T(8,128)(2,1)S(1)}, bf16[144,2560]{1,0:T(8,128)(2,1)S(1)}, u32[]{:S(2)}, u32[]{:S(2)}) collective-permute-start(bf16[144,2560]{1,0:T(8,128)(2,1)S(1)} %pad_maximum_fusion.1), channel_id=1, source_target_pairs={{0,8},{4,12},{8,16},{12,20},{16,24},{20,28},{1,9},{5,13},{9,17},{1... | collective-permute-start | bytes 2211848 | tf_op jit(solution)/shard_map/ppermute | solution.py:18
  53.3 7.6 %shard_map.119.part_ref = f32[256,2560]{1,0:T(8,128)S(1)} custom-call(bf16[256,2560]{1,0:T(8,128)(2,1)S(1)} %get-tuple-element.41.mixed_ref, bf16[256,256]{1,0:T(8,128)(2,1)S(1)} %get-tuple-element.56.bc_ref, f32[128,256]{1,0:T(8,128)S(1)} %get-tuple-element.52.cum_ref, f32[256,128]{1,0:T(8,128)S(1)} %get-tuple-element.74.cum_t_ref, ...), custom_call_target="tpu_custom_call" | custom-call | flops 5368709120 | bytes 5242880 | tf_op jit(solution)/shard_map/pallas_call | solution.py:215
  60.9 1.6 %copy-done = f32[256,2560]{1,0:T(8,128)} copy-done((f32[256,2560]{1,0:T(8,128)}, f32[256,2560]{1,0:T(8,128)S(1)}, u32[]{:S(2)}) %copy-start) | copy-done | bytes 2621464
  62.5 5.3 %collective-permute-done.2 = bf16[144,2560]{1,0:T(8,128)(2,1)S(1)} collective-permute-done((bf16[144,2560]{1,0:T(8,128)(2,1)S(1)}, bf16[144,2560]{1,0:T(8,128)(2,1)S(1)}, u32[]{:S(2)}, u32[]{:S(2)}) %collective-permute-start.2) | collective-permute-done | bytes 737312 | tf_op jit(solution)/shard_map/ppermute | solution.py:18
  67.7 4.6 %collective-permute-start.3 = (bf16[144,2560]{1,0:T(8,128)(2,1)S(1)}, bf16[144,2560]{1,0:T(8,128)(2,1)S(1)}, u32[]{:S(2)}, u32[]{:S(2)}) collective-permute-start(bf16[144,2560]{1,0:T(8,128)(2,1)S(1)} %collective-permute-done.2), channel_id=1, source_target_pairs={{0,8},{4,12},{8,16},{12,20},{16,24},{20,28},{1,9},{5,13},{9,17},{1... | collective-permute-start | bytes 2211848 | tf_op jit(solution)/shard_map/ppermute | solution.py:18
  72.4 7.6 %shard_map.121.part_ref = f32[256,2560]{1,0:T(8,128)S(1)} custom-call(bf16[256,2560]{1,0:T(8,128)(2,1)S(1)} %get-tuple-element.42.mixed_ref, bf16[256,256]{1,0:T(8,128)(2,1)S(1)} %get-tuple-element.57.bc_ref, f32[128,256]{1,0:T(8,128)S(1)} %get-tuple-element.53.cum_ref, f32[256,128]{1,0:T(8,128)S(1)} %get-tuple-element.73.cum_t_ref, ...), custom_call_target="tpu_custom_call" | custom-call | flops 5368709120 | bytes 5242880 | tf_op jit(solution)/shard_map/pallas_call | solution.py:215
  80.2 5.5 %collective-permute-done.3 = bf16[144,2560]{1,0:T(8,128)(2,1)S(1)} collective-permute-done((bf16[144,2560]{1,0:T(8,128)(2,1)S(1)}, bf16[144,2560]{1,0:T(8,128)(2,1)S(1)}, u32[]{:S(2)}, u32[]{:S(2)}) %collective-permute-start.3) | collective-permute-done | bytes 737312 | tf_op jit(solution)/shard_map/ppermute | solution.py:18
  85.7 1.8 %fusion.9 = (bf16[128,2560]{1,0:T(8,128)(2,1)S(1)}, bf16[128,2560]{1,0:T(8,128)(2,1)S(1)}) fusion(bf16[144,2560]{1,0:T(8,128)(2,1)S(1)} %collective-permute-done.3, f32[2560]{0:T(1024)S(1)} %fusion.4, f32[144,2560]{1,0:T(8,128)S(1)} %convert_element_type.155, f32[2560]{0:T(1024)S(1)} %fusion.6, f32[144,2560]{1,0:T(8,128)S(1)} %get-tuple-element.47, ...), kind=kLoop, calls=%fused_computation.60 | loop fusion | flops 3276800 | bytes 5928961 | tf_op jit(solution)/shard_map/convert_element_type | solution.py:369
  87.5 5.0 %shard_map.120 = (bf16[256,2560]{1,0:T(8,128)(2,1)S(1)}, f32[256,128]{1,0:T(8,128)S(1)}) custom-call(bf16[128,2560]{1,0:T(8,128)(2,1)S(1)} %get-tuple-element.37.state_ref, bf16[256,256]{1,0:T(8,128)(2,1)S(1)} %get-tuple-element.56.bc_ref, f32[256,128]{1,0:T(8,128)S(1)} %get-tuple-element.54.gain_t_ref, f32[256,2560]{1,0:T(8,128)} %copy-done, ...), custom_call_target="tpu_custom_call" | custom-call | flops 167772160 | bytes 7864320 | tf_op jit(solution)/shard_map/pallas_call | solution.py:215
  92.5 0.6 copy-done.5
  93.2 1.1 copy-done.7
  94.2 1.0 reduce_sum.36
  95.3 5.0 %shard_map.122 = (bf16[256,2560]{1,0:T(8,128)(2,1)S(1)}, f32[256,128]{1,0:T(8,128)S(1)}) custom-call(bf16[128,2560]{1,0:T(8,128)(2,1)S(1)} %get-tuple-element.38.state_ref, bf16[256,256]{1,0:T(8,128)(2,1)S(1)} %get-tuple-element.57.bc_ref, f32[256,128]{1,0:T(8,128)S(1)} %get-tuple-element.55.gain_t_ref, f32[256,2560]{1,0:T(8,128)} %copy-done.1, ...), custom_call_target="tpu_custom_call" | custom-call | flops 167772160 | bytes 7864320 | tf_op jit(solution)/shard_map/pallas_call | solution.py:215
  100.3 1.0 copy-done.9
  101.5 8.8 %convolution_convert_fusion = bf16[256,2560]{1,0:T(8,128)(2,1)S(1)} fusion(bf16[256,2560]{1,0:T(8,128)(2,1)} %copy-done.9, bf16[2560,2560]{1,0:T(8,128)(2,1)} %param.23), kind=kOutput, calls=%fused_computation | convolution fusion | flops 3356098560 | bytes 15728640 | tf_op jit(solution)/shard_map/dot_general | solution.py:374
  110.4 0.6 copy-done.21
  111.2 0.9 pad_maximum_fusion.3
  112.2 1.5 %collective-permute-start.5 = (bf16[256,1408]{1,0:T(8,128)(2,1)}, bf16[256,1408]{1,0:T(8,128)(2,1)S(1)}, u32[]{:S(2)}, u32[]{:S(2)}) collective-permute-start(bf16[256,1408]{1,0:T(8,128)(2,1)} %pad_maximum_fusion.3), channel_id=1, source_target_pairs={{0,2},{2,0},{1,3},{3,1},{4,6},{6,4},{5,7},{7,5},{8,10},{10,8},{9,1... | collective-permute-start | bytes 2162696 | tf_op jit(solution)/shard_map/ppermute | solution.py:385
  113.7 3.6 %convolution_convert_fusion.1 = bf16[256,2560]{1,0:T(8,128)(2,1)S(1)} fusion(bf16[256,2560]{1,0:T(8,128)(2,1)S(1)} %copy-done.8, bf16[2560,2560]{1,0:T(8,128)(2,1)S(1)} %bitcast.27), kind=kOutput, calls=%fused_computation.1 | convolution fusion | flops 3356098560 | bytes 15728640 | tf_op jit(solution)/shard_map/dot_general | solution.py:374
  117.4 0.9 pad_maximum_fusion.2
  118.3 0.3 copy-done.12
  118.6 0.5 collective-permute-start.4
  119.1 12.3 %collective-permute-done.5 = bf16[256,1408]{1,0:T(8,128)(2,1)S(1)} collective-permute-done((bf16[256,1408]{1,0:T(8,128)(2,1)}, bf16[256,1408]{1,0:T(8,128)(2,1)S(1)}, u32[]{:S(2)}, u32[]{:S(2)}) %collective-permute-start.5) | collective-permute-done | bytes 720928 | tf_op jit(solution)/shard_map/ppermute | solution.py:385
  131.6 11.2 %collective-permute-done.4 = bf16[256,1408]{1,0:T(8,128)(2,1)} collective-permute-done((bf16[256,1408]{1,0:T(8,128)(2,1)}, bf16[256,1408]{1,0:T(8,128)(2,1)}, u32[]{:S(2)}, u32[]{:S(2)}) %collective-permute-start.4) | collective-permute-done | bytes 720928 | tf_op jit(solution)/shard_map/ppermute | solution.py:385
  142.8 0.9 convert_reduce_fusion.1
  143.8 0.2 multiply_convert_fusion
  144.0 1.3 multiply_convert_fusion.1
  145.3 1.1 pad_maximum_fusion
  (104 shorter events, 2.7 us)
Async XLA Ops:
  2.3 11.1 %collective-permute-start = (bf16[3,2944]{1,0:T(4,128)(2,1)S(1)}, bf16[3,2944]{1,0:T(4,128)(2,1)S(1)}, u32[]{:S(2)}, u32[]{:S(2)}) collective-permute-start(bf16[3,2944]{1,0:T(4,128)(2,1)S(1)} %pad_maximum_fusion.4), channel_id=1, source_target_pairs={{0,4},{4,8},{8,12},{12,16},{16,20},{20,24},{24,28},{1,5},{5,9},{9,... | collective-permute-start | bytes 53000 | tf_op jit(solution)/shard_map/ppermute | solution.py:18
  8.1 2.0 %copy-start.15 = (bf16[40,512]{1,0:T(8,128)(2,1)S(1)}, bf16[40,512]{1,0:T(8,128)(2,1)}, u32[]{:S(2)}) copy-start(bf16[40,512]{1,0:T(8,128)(2,1)} %param.15) | copy-start | bytes 122884
  8.1 2.0 %copy-start.20 = (f32[40]{0:T(128)S(1)}, f32[40]{0:T(128)}, u32[]{:S(2)}) copy-start(f32[40]{0:T(128)} %param.20) | copy-start | bytes 484
  8.1 2.9 %copy-start.16 = (bf16[4,2560]{1,0:T(4,128)(2,1)S(1)}, bf16[4,2560]{1,0:T(4,128)(2,1)}, u32[]{:S(2)}) copy-start(bf16[4,2560]{1,0:T(4,128)(2,1)} %param.17) | copy-start | bytes 61444
  8.1 2.9 %copy-start.19 = (bf16[4,256]{1,0:T(4,128)(2,1)S(1)}, bf16[4,256]{1,0:T(4,128)(2,1)}, u32[]{:S(2)}) copy-start(bf16[4,256]{1,0:T(4,128)(2,1)} %param.18) | copy-start | bytes 6148
  8.1 3.7 %copy-start.23 = (f32[40]{0:T(128)S(1)}, f32[40]{0:T(128)}, u32[]{:S(2)}) copy-start(f32[40]{0:T(128)} %param.21) | copy-start | bytes 484
  8.2 4.5 %copy-start.17 = (f32[2560]{0:T(1024)S(1)}, f32[2560]{0:T(1024)}, u32[]{:S(2)}) copy-start(f32[2560]{0:T(1024)} %param.22) | copy-start | bytes 30724
  10.1 4.8 %copy-start.18 = (s32[512]{0:T(512)S(1)}, s32[512]{0:T(512)}, u32[]{:S(2)}) copy-start(s32[512]{0:T(512)} %param.16) | copy-start | bytes 6148
  13.5 1.7 %copy-start.14 = (bf16[3,2944]{1,0:T(4,128)(2,1)}, bf16[3,2944]{1,0:T(4,128)(2,1)S(1)}, u32[]{:S(2)}) copy-start(bf16[3,2944]{1,0:T(4,128)(2,1)S(1)} %collective-permute-done) | copy-start | bytes 52996
  17.3 0.9 copy-start.2
  30.8 18.0 %collective-permute-start.1 = (bf16[144,2560]{1,0:T(8,128)(2,1)S(1)}, bf16[144,2560]{1,0:T(8,128)(2,1)S(1)}, u32[]{:S(2)}, u32[]{:S(2)}) collective-permute-start(bf16[144,2560]{1,0:T(8,128)(2,1)S(1)} %get-tuple-element.18), channel_id=1, source_target_pairs={{0,4},{4,0},{8,12},{12,8},{16,20},{20,16},{24,28},{28,24},{1,5},{5... | collective-permute-start | bytes 2211848 | tf_op jit(solution)/shard_map/ppermute | solution.py:255
  49.6 3.7 %copy-start.4 = (f32[256,1]{1,0:T(8,128)S(1)}, f32[256,1]{1,0:T(8,128)}, u32[]{:S(2)}) copy-start(f32[256,1]{1,0:T(8,128)} %copy.31.ids_col_ref) | copy-start | bytes 3076
  49.6 3.7 %copy-start.6 = (f32[1,2560]{1,0:T(1,128)S(1)}, f32[1,2560]{1,0:T(1,128)}, u32[]{:S(2)}) copy-start(f32[1,2560]{1,0:T(1,128)} %broadcast_in_dim_reshape.3.skip_ref) | copy-start | bytes 30724
  49.7 18.0 %collective-permute-start.2 = (bf16[144,2560]{1,0:T(8,128)(2,1)S(1)}, bf16[144,2560]{1,0:T(8,128)(2,1)S(1)}, u32[]{:S(2)}, u32[]{:S(2)}) collective-permute-start(bf16[144,2560]{1,0:T(8,128)(2,1)S(1)} %pad_maximum_fusion.1), channel_id=1, source_target_pairs={{0,8},{4,12},{8,16},{12,20},{16,24},{20,28},{1,9},{5,13},{9,17},{1... | collective-permute-start | bytes 2211848 | tf_op jit(solution)/shard_map/ppermute | solution.py:18
  53.3 19.1 %copy-start.3 = (f32[256,1]{1,0:T(8,128)S(1)}, f32[256,1]{1,0:T(8,128)}, u32[]{:S(2)}) copy-start(f32[256,1]{1,0:T(8,128)} %copy.32.ids_col_ref) | copy-start | bytes 3076
  60.9 1.6 %copy-start = (f32[256,2560]{1,0:T(8,128)}, f32[256,2560]{1,0:T(8,128)S(1)}, u32[]{:S(2)}) copy-start(f32[256,2560]{1,0:T(8,128)S(1)} %shard_map.119.part_ref) | copy-start | bytes 7864324
  67.7 18.0 %collective-permute-start.3 = (bf16[144,2560]{1,0:T(8,128)(2,1)S(1)}, bf16[144,2560]{1,0:T(8,128)(2,1)S(1)}, u32[]{:S(2)}, u32[]{:S(2)}) collective-permute-start(bf16[144,2560]{1,0:T(8,128)(2,1)S(1)} %collective-permute-done.2), channel_id=1, source_target_pairs={{0,8},{4,12},{8,16},{12,20},{16,24},{20,28},{1,9},{5,13},{9,17},{1... | collective-permute-start | bytes 2211848 | tf_op jit(solution)/shard_map/ppermute | solution.py:18
  80.0 7.5 %copy-start.1 = (f32[256,2560]{1,0:T(8,128)}, f32[256,2560]{1,0:T(8,128)S(1)}, u32[]{:S(2)}) copy-start(f32[256,2560]{1,0:T(8,128)S(1)} %shard_map.121.part_ref) | copy-start | bytes 7864324
  92.5 0.7 copy-start.5
  93.2 1.1 copy-start.7
  100.3 1.1 copy-start.9
  101.5 12.2 %slice-start = ((s8[13107200]{0:T(1024)(128)(4,1)}), s8[4194304]{0:T(1024)(128)(4,1)S(1)}, s32[]{:S(2)}) async-start(s8[13107200]{0:T(1024)(128)(4,1)} %bitcast.26), calls=%async_computation | async-start | bytes 8388608
  101.5 12.2 %slice-start.1 = ((s8[13107200]{0:T(1024)(128)(4,1)}), s8[4194304]{0:T(1024)(128)(4,1)S(1)}, s32[]{:S(2)}) async-start(s8[13107200]{0:T(1024)(128)(4,1)} %bitcast.26), calls=%async_computation.1 | async-start | bytes 8388608
  101.5 12.2 %slice-start.2 = ((s8[13107200]{0:T(1024)(128)(4,1)}), s8[4194304]{0:T(1024)(128)(4,1)S(1)}, s32[]{:S(2)}) async-start(s8[13107200]{0:T(1024)(128)(4,1)} %bitcast.26), calls=%async_computation.2 | async-start | bytes 8388608
  101.5 12.2 %slice-start.3 = ((s8[13107200]{0:T(1024)(128)(4,1)}), s8[524288]{0:T(1024)(128)(4,1)S(1)}, s32[]{:S(2)}) async-start(s8[13107200]{0:T(1024)(128)(4,1)} %bitcast.26), calls=%async_computation.3 | async-start | bytes 1048576
  110.3 1.9 %copy-start.10 = (bf16[256,2560]{1,0:T(8,128)(2,1)}, bf16[256,2560]{1,0:T(8,128)(2,1)S(1)}, u32[]{:S(2)}) copy-start(bf16[256,2560]{1,0:T(8,128)(2,1)S(1)} %convolution_convert_fusion) | copy-start | bytes 3932164
  110.3 0.7 copy-start.21
  110.4 0.7 copy-start.22
  110.4 3.4 %copy-start.8 = (bf16[256,2560]{1,0:T(8,128)(2,1)S(1)}, bf16[256,2560]{1,0:T(8,128)(2,1)}, u32[]{:S(2)}) copy-start(bf16[256,2560]{1,0:T(8,128)(2,1)} %copy-done.7) | copy-start | bytes 3932164
  112.2 19.3 %collective-permute-start.5 = (bf16[256,1408]{1,0:T(8,128)(2,1)}, bf16[256,1408]{1,0:T(8,128)(2,1)S(1)}, u32[]{:S(2)}, u32[]{:S(2)}) collective-permute-start(bf16[256,1408]{1,0:T(8,128)(2,1)} %pad_maximum_fusion.3), channel_id=1, source_target_pairs={{0,2},{2,0},{1,3},{3,1},{4,6},{6,4},{5,7},{7,5},{8,10},{10,8},{9,1... | collective-permute-start | bytes 2162696 | tf_op jit(solution)/shard_map/ppermute | solution.py:385
  117.3 1.3 copy-start.12
  117.3 26.4 %copy-start.11 = (bf16[256,2560]{1,0:T(8,128)(2,1)S(1)}, bf16[256,2560]{1,0:T(8,128)(2,1)}, u32[]{:S(2)}) copy-start(bf16[256,2560]{1,0:T(8,128)(2,1)} %copy-done.10) | copy-start | bytes 3932164
  118.6 24.2 %collective-permute-start.4 = (bf16[256,1408]{1,0:T(8,128)(2,1)}, bf16[256,1408]{1,0:T(8,128)(2,1)}, u32[]{:S(2)}, u32[]{:S(2)}) collective-permute-start(bf16[256,1408]{1,0:T(8,128)(2,1)} %pad_maximum_fusion.2), channel_id=1, source_target_pairs={{0,2},{2,0},{1,3},{3,1},{4,6},{6,4},{5,7},{7,5},{8,10},{10,8},{9,1... | collective-permute-start | bytes 2162696 | tf_op jit(solution)/shard_map/ppermute | solution.py:385
  119.1 24.8 %copy-start.13 = (bf16[256,2560]{1,0:T(8,128)(2,1)S(1)}, bf16[256,2560]{1,0:T(8,128)(2,1)}, u32[]{:S(2)}) copy-start(bf16[256,2560]{1,0:T(8,128)(2,1)} %copy-done.12) | copy-start | bytes 3932164

commit v3 on v2

--- a/solution.py
+++ b/solution.py
@@ -211,6 +211,134 @@
     )
 
 
+def tail_kernel(head_size, chunk, blocks, *refs):
+    state_ref, fresh_ref, decay_ref, bc_ref, gain_t_ref, z_ref, norm_ref, w_ref = refs[:8]
+    part_refs = refs[8 : 8 + blocks]
+    out_ref = refs[8 + blocks]
+    (
+        w_far, w_near, scaled, state, sums, sends, gots, row_sends, row_gots,
+        w_sems, send_sems, got_sems, row_send_sems, row_got_sems,
+    ) = refs[9 + blocks :]
+    rows, width = z_ref.shape
+    out_width = out_ref.shape[1]
+    count = rows // chunk
+    per_block = SPAN // chunk
+    size = group_lanes(width)
+    per_group = size // head_size
+    state_size = bc_ref.shape[1] // 2
+    me = lax.axis_index("tensor")
+    peer = 1 - me
+    barrier = pltpu.get_barrier_semaphore()
+    pl.semaphore_signal(
+        barrier, inc=1, device_id={"tensor": peer}, device_id_type=pl.DeviceIdType.MESH
+    )
+    loads = [
+        pltpu.make_async_copy(
+            w_ref.at[:, pl.ds(pl.multiple_of(who * out_width, 128), out_width)],
+            place,
+            w_sems.at[k],
+        )
+        for k, (who, place) in enumerate(((peer, w_far), (me, w_near)))
+    ]
+    for load in loads:
+        load.start()
+    tile = 256 if out_width % 256 == 0 else 128
+
+    def product(q, weights, store):
+        def columns(j, unused):
+            lanes = pl.ds(pl.multiple_of(j * tile, tile), tile)
+            store(
+                lanes,
+                jnp.dot(
+                    scaled[q * chunk : (q + 1) * chunk, :], weights[:, lanes],
+                    preferred_element_type=jnp.float32,
+                ).astype(jnp.bfloat16),
+            )
+            return unused
+
+        lax.fori_loop(0, out_width // tile, columns, 0)
+
+    copies = []
+    for q in range(count):
+        b, within = q // per_block, q % per_block
+        here = slice(q * chunk, (q + 1) * chunk)
+        inner = slice(within * chunk, (within + 1) * chunk)
+
+        def group(c, squares):
+            lanes = pl.ds(pl.multiple_of(c * size, size), size)
+            turn = lax.rem(HEADS_PAD - c * per_group, HEADS_PAD)
+            if q == 0:
+                state[:, lanes] = state_ref[:, lanes].astype(jnp.bfloat16)
+            elif within == 0:
+                state[:, lanes] = (
+                    decay_ref[b - 1, 0:1, lanes] * state[:, lanes].astype(jnp.float32)
+                    + fresh_ref[b - 1, :, lanes]
+                ).astype(jnp.bfloat16)
+            gain = spread_heads(pltpu.roll(gain_t_ref[here, :], turn, 1), head_size, size)
+            reached = jnp.dot(
+                bc_ref[here, state_size:], state[:, lanes], preferred_element_type=jnp.float32
+            )
+            y = part_refs[b][inner, lanes] + gain * reached
+            y = y.astype(jnp.bfloat16).astype(jnp.float32)
+            gated = y * silu(z_ref[here, lanes].astype(jnp.float32))
+            scaled[here, lanes] = (gated * norm_ref[:, lanes]).astype(jnp.bfloat16)
+            square = gated * gated
+            for k in range(size // 128):
+                squares = squares + square[:, k * 128 : (k + 1) * 128]
+            return squares
+
+        squares = lax.fori_loop(0, width // size, group, jnp.zeros((chunk, 128), jnp.float32))
+        row = jnp.sum(squares.T, axis=0, keepdims=True)
+        row_sends[q] = jnp.broadcast_to(row, (8, chunk))
+        if q == 0:
+            loads[0].wait()
+
+        def put(lanes, value):
+            sends[q, :, lanes] = value
+
+        product(q, w_far, put)
+        if q == 0:
+            pl.semaphore_wait(barrier, 1)
+        pair = [
+            pltpu.make_async_remote_copy(
+                src_ref=source.at[q],
+                dst_ref=landing.at[q],
+                send_sem=out_sems.at[q],
+                recv_sem=in_sems.at[q],
+                device_id={"tensor": peer},
+                device_id_type=pl.DeviceIdType.MESH,
+            )
+            for source, landing, out_sems, in_sems in (
+                (row_sends, row_gots, row_send_sems, row_got_sems),
+                (sends, gots, send_sems, got_sems),
+            )
+        ]
+        for copy in pair:
+            copy.start()
+        copies.append(pair)
+
+    loads[1].wait()
+    for q in range(count):
+        here = slice(q * chunk, (q + 1) * chunk)
+
+        def keep(lanes, value):
+            sums[:, lanes] = value
+
+        product(q, w_near, keep)
+        for copy in copies[q]:
+            copy.wait_recv()
+        row = row_sends[q, 0:1, :] + row_gots[q, 0:1, :]
+        inv_row = lax.rsqrt(row / (2 * width) + 1e-05)
+        inv = jnp.broadcast_to(inv_row, (128, chunk)).T
+        for j in range(out_width // 128):
+            lanes = slice(j * 128, (j + 1) * 128)
+            total = sums[:, lanes].astype(jnp.float32) + gots[q, :, lanes].astype(jnp.float32)
+            out_ref[here, lanes] = (total * inv).astype(jnp.bfloat16)
+    for pair in copies:
+        for copy in pair:
+            copy.wait_send()
+
+
 def call(kernel, out_shape, scratch, flops, moved, *operands):
     return pl.pallas_call(
         kernel,
@@ -357,6 +485,40 @@
     members = lax.axis_size("tensor")
     member = lax.axis_index("tensor")
     out_width = w_out.shape[1] // members
+    if members == 2 and out_width % 128 == 0:
+        chunk = 128
+        count = rows // chunk
+        vmem = pl.BlockSpec(memory_space=pltpu.VMEM)
+        return pl.pallas_call(
+            functools.partial(tail_kernel, head_size, chunk, blocks),
+            out_shape=shape((rows, out_width), bf16),
+            in_specs=[vmem] * 7 + [pl.BlockSpec(memory_space=pl.ANY)] + [vmem] * blocks,
+            out_specs=vmem,
+            scratch_shapes=[
+                pltpu.VMEM((width, out_width), bf16),
+                pltpu.VMEM((width, out_width), bf16),
+                pltpu.VMEM((rows, width), bf16),
+                pltpu.VMEM((state_size, width), bf16),
+                pltpu.VMEM((chunk, out_width), bf16),
+                pltpu.VMEM((count, chunk, out_width), bf16),
+                pltpu.VMEM((count, chunk, out_width), bf16),
+                pltpu.VMEM((count, 8, chunk), f32),
+                pltpu.VMEM((count, 8, chunk), f32),
+                pltpu.SemaphoreType.DMA((2,)),
+                pltpu.SemaphoreType.DMA((count,)),
+                pltpu.SemaphoreType.DMA((count,)),
+                pltpu.SemaphoreType.DMA((count,)),
+                pltpu.SemaphoreType.DMA((count,)),
+            ],
+            compiler_params=pltpu.CompilerParams(
+                collective_id=0, has_side_effects=True, vmem_limit_bytes=VMEM_BYTES
+            ),
+            cost_estimate=pl.CostEstimate(
+                flops=2 * rows * width * w_out.shape[1],
+                bytes_accessed=2 * width * w_out.shape[1],
+                transcendentals=0,
+            ),
+        )(state, fresh, decay, mixed_bc, gain_t, z_gate, norm_gain[None, :], w_out, *parts)
     pieces = []
     for b in range(blocks):
         span = slice(b * SPAN, (b + 1) * SPAN)

time: 147 us -> 134 us (0.912)
  Pallas kernels: 37.8 us -> 64.5 us
  waiting for transfers between devices: 50.4 us -> 26.9 us
  matrix products: 12.4 us -> 0 us
  other arithmetic: 14.1 us -> 8.34 us
  local copies, waits for them, and re-layouts: 14.6 us -> 18.8 us
  starting transfers between devices: 16.5 us -> 14.3 us
    pallas_call x0 -> x1, Pallas kernels: none -> 36.5 us  [local(): pl.pallas_call(functools.partial(tail_kernel, head_size, chunk, blocks),...]
    ppermute x2 -> x0, waiting for transfers between devices: 23.5 us -> none  [local(): got = lax.ppermute(jnp.concatenate([block, aside], axis=1), 'tensor', route)]
    dot_general x2 -> x0, matrix products: 12.4 us -> none  [local(): product = jnp.dot(scaled, w_out, preferred_element_type=f32).astype(bf16)]
    pallas_call x5 -> x3, Pallas kernels: 37.8 us -> 28 us  [call(): pl.pallas_call(kernel, out_shape=out_shape, in_specs=[pl.BlockSpec(memory...]
    unnamed x60 -> x41, local copies, waits for them, and re-layouts: 6.43 us -> 11.1 us
    ppermute x1, waiting for transfers between devices: 16.1 us -> 12.6 us  [pass_state(): other = lax.ppermute(message, 'seq', [(i, i ^ 1) for i in range(count)])]
    ppermute x3, waiting for transfers between devices: 10.7 us -> 14.3 us  [shifted(): lax.ppermute(block, axis, [(i, i + distance) for i in range(count - dista...]
    convert_element_type x5 -> x0, other arithmetic: 3.28 us -> none  [the longest x1 1.76 us: local(): state.astype(bf16)]
  transfers between devices with their start and end apart: 6 -> 4, of which waited for: 5 -> 2; matrix products, arithmetic and copies ran while one was open for 8% -> 6% of each run, Pallas kernels for 10% -> 11%
where the time goes in v3:
time: 134 us; the launch traced here: 133 us
  Pallas kernels  64.5 us (48%)
  waiting for transfers between devices  26.9 us (20%)
  local copies, waits for them, and re-layouts  18.8 us (14%)
  starting transfers between devices  14.3 us (11%)
  other arithmetic  8.34 us (6%)
    pallas_call x1, Pallas kernels, local(): pl.pallas_call(functools.partial(tail_kernel, head_size, chunk, blocks),...  36.5 us
    pallas_call x3, Pallas kernels, call(): pl.pallas_call(kernel, out_shape=out_shape, in_specs=[pl.BlockSpec(memory...  28 us
    ppermute x3, waiting for transfers between devices, shifted(): lax.ppermute(block, axis, [(i, i + distance) for i in range(count - dista...  14.3 us
    ppermute x3, starting transfers between devices, shifted(): lax.ppermute(block, axis, [(i, i + distance) for i in range(count - dista...  12.8 us
    ppermute x1, waiting for transfers between devices, pass_state(): other = lax.ppermute(message, 'seq', [(i, i ^ 1) for i in range(count)])  12.6 us
    unnamed x41, local copies, waits for them, and re-layouts  11.1 us
  transfers between devices with their start and end apart: 4, of which 2 were waited for; matrix products, arithmetic and copies ran while one was open for 6% of the time, Pallas kernels for 11%

profile of v3, /device:TPU:0, one launch (start us, length us, event | category | flops | bytes accessed | tf_op | source)
XLA Modules:
  0.0 133.2 jit_solution(4683483972570288986)
XLA Ops:
  0.0 0.7 fusion.14
  0.7 0.1 slice.125
  0.8 0.7 slice.124
  1.5 0.8 slice.123
  2.3 4.8 %collective-permute-start = (bf16[3,2944]{1,0:T(4,128)(2,1)S(1)}, bf16[3,2944]{1,0:T(4,128)(2,1)S(1)}, u32[]{:S(2)}, u32[]{:S(2)}) collective-permute-start(bf16[3,2944]{1,0:T(4,128)(2,1)S(1)} %pad_maximum_fusion.1), channel_id=1, source_target_pairs={{0,4},{4,8},{8,12},{12,16},{16,20},{20,24},{24,28},{1,5},{5,9},{9,... | collective-permute-start | bytes 53000 | tf_op jit(solution)/shard_map/ppermute | solution.py:18
  7.2 0.7 exponential_negate_fusion
  7.9 0.2 slice_reduce_fusion
  8.1 0.9 broadcast_multiply_fusion
  9.0 0.1 slice.134
  9.2 0.7 convert_element_type.56.conv_x_ref
  9.9 0.7 convert_element_type.57.conv_bc_ref
  10.7 0.1 convert_select_fusion
  10.8 0.1 pad_maximum_fusion.2
  10.9 0.5 slice.132
  11.4 0.8 pad_maximum_fusion.3
  12.2 0.8 slice_compare_fusion
  13.1 0.9 copy.30.flags_ref
  14.0 0.9 copy-done.3
  14.9 0.9 copy-done.4
  15.9 12.8 %shard_map.118 = (bf16[512,2560]{1,0:T(8,128)(2,1)S(1)}, bf16[512,256]{1,0:T(8,128)(2,1)S(1)}, f32[128,512]{1,0:T(8,128)S(1)}, f32[512,128]{1,0:T(8,128)S(1)}, f...) custom-call(bf16[512,2560]{1,0:T(8,128)(2,1)} %x_ref.1, ...), custom_call_target="tpu_custom_call" | custom-call | flops 335544320 | bytes 10485760 | tf_op jit(solution)/shard_map/pallas_call | solution.py:343
  28.6 0.7 copy-done.5
  29.3 0.7 copy-done.7
  30.1 0.7 copy-done.8
  30.7 0.7 copy-done.10
  31.5 0.7 copy-done.12
  32.2 1.5 %collective-permute-start.1 = (bf16[144,2560]{1,0:T(8,128)(2,1)}, bf16[144,2560]{1,0:T(8,128)(2,1)}, u32[]{:S(2)}, u32[]{:S(2)}) collective-permute-start(bf16[144,2560]{1,0:T(8,128)(2,1)} %get-tuple-element.14), channel_id=1, source_target_pairs={{0,4},{4,0},{8,12},{12,8},{16,20},{20,16},{24,28},{28,24},{1,5},{5... | collective-permute-start | bytes 2211848 | tf_op jit(solution)/shard_map/ppermute | solution.py:383
  33.7 0.7 broadcast_in_dim.51.refs_6_
  34.4 0.8 copy.31.ids_col_ref
  35.2 0.7 broadcast_in_dim.54
  35.9 0.7 broadcast_in_dim_reshape.3.skip_ref
  36.6 0.1 copy.32.ids_col_ref
  36.8 1.0 fusion.11
  37.9 12.6 %collective-permute-done.1 = bf16[144,2560]{1,0:T(8,128)(2,1)} collective-permute-done((bf16[144,2560]{1,0:T(8,128)(2,1)}, bf16[144,2560]{1,0:T(8,128)(2,1)}, u32[]{:S(2)}, u32[]{:S(2)}) %collective-permute-start.1) | collective-permute-done | bytes 737312 | tf_op jit(solution)/shard_map/ppermute | solution.py:383
  50.4 2.1 %select_convert_fusion.1 = (f32[144,2560]{1,0:T(8,128)S(1)}, f32[144,2560]{1,0:T(8,128)S(1)}, f32[144,2560]{1,0:T(8,128)S(1)}) fusion(bf16[144,2560]{1,0:T(8,128)(2,1)} %get-tuple-element.14, bf16[144,2560]{1,0:T(8,128)(2,1)} %collective-permute-done.1, pred[]{:T(512)S(6)} %eq.41), kind=kLoop, calls=%fused_computation.8 | loop fusion | flops 1843200 | bytes 5898241 | tf_op jit(solution)/shard_map/convert_element_type | solution.py:356
  52.6 0.2 fusion.1
  52.9 3.5 %collective-permute-start.2 = (bf16[144,2560]{1,0:T(8,128)(2,1)S(1)}, bf16[144,2560]{1,0:T(8,128)(2,1)S(1)}, u32[]{:S(2)}, u32[]{:S(2)}) collective-permute-start(bf16[144,2560]{1,0:T(8,128)(2,1)S(1)} %pad_maximum_fusion), channel_id=1, source_target_pairs={{0,8},{4,12},{8,16},{12,20},{16,24},{20,28},{1,9},{5,13},{9,17},{1... | collective-permute-start | bytes 2211848 | tf_op jit(solution)/shard_map/ppermute | solution.py:18
  56.5 0.2 fusion.8
  56.6 14.3 %collective-permute-done.2 = bf16[144,2560]{1,0:T(8,128)(2,1)S(1)} collective-permute-done((bf16[144,2560]{1,0:T(8,128)(2,1)S(1)}, bf16[144,2560]{1,0:T(8,128)(2,1)S(1)}, u32[]{:S(2)}, u32[]{:S(2)}) %collective-permute-start.2) | collective-permute-done | bytes 737312 | tf_op jit(solution)/shard_map/ppermute | solution.py:18
  70.9 4.4 %collective-permute-start.3 = (bf16[144,2560]{1,0:T(8,128)(2,1)S(1)}, bf16[144,2560]{1,0:T(8,128)(2,1)S(1)}, u32[]{:S(2)}, u32[]{:S(2)}) collective-permute-start(bf16[144,2560]{1,0:T(8,128)(2,1)S(1)} %collective-permute-done.2), channel_id=1, source_target_pairs={{0,8},{4,12},{8,16},{12,20},{16,24},{20,28},{1,9},{5,13},{9,17},{1... | collective-permute-start | bytes 2211848 | tf_op jit(solution)/shard_map/ppermute | solution.py:18
  75.4 7.6 %shard_map.119.refs_8_ = f32[256,2560]{1,0:T(8,128)S(1)} custom-call(bf16[256,2560]{1,0:T(8,128)(2,1)S(1)} %get-tuple-element.26.mixed_ref, bf16[256,256]{1,0:T(8,128)(2,1)S(1)} %get-tuple-element.39.bc_ref, f32[128,256]{1,0:T(8,128)S(1)} %get-tuple-element.37.cum_ref, f32[256,128]{1,0:T(8,128)S(1)} %get-tuple-element.53.cum_t_ref, ...), custom_call_target="tpu_custom_call" | custom-call | flops 5368709120 | bytes 5242880 | tf_op jit(solution)/shard_map/pallas_call | solution.py:343
  83.0 1.5 %copy-done.1 = f32[256,2560]{1,0:T(8,128)} copy-done((f32[256,2560]{1,0:T(8,128)}, f32[256,2560]{1,0:T(8,128)S(1)}, u32[]{:S(2)}) %copy-start.1) | copy-done | bytes 2621464
  84.5 7.6 %shard_map.120.refs_9_ = f32[256,2560]{1,0:T(8,128)S(1)} custom-call(bf16[256,2560]{1,0:T(8,128)(2,1)S(1)} %get-tuple-element.25.mixed_ref, bf16[256,256]{1,0:T(8,128)(2,1)S(1)} %get-tuple-element.38.bc_ref, f32[128,256]{1,0:T(8,128)S(1)} %get-tuple-element.36.cum_ref, f32[256,128]{1,0:T(8,128)S(1)} %get-tuple-element.54.cum_t_ref, ...), custom_call_target="tpu_custom_call" | custom-call | flops 5368709120 | bytes 5242880 | tf_op jit(solution)/shard_map/pallas_call | solution.py:343
  92.1 1.5 %copy-done.2 = f32[256,2560]{1,0:T(8,128)} copy-done((f32[256,2560]{1,0:T(8,128)}, f32[256,2560]{1,0:T(8,128)S(1)}, u32[]{:S(2)}) %copy-start.2) | copy-done | bytes 2621464
  93.7 0.1 convert_element_type.65
  93.9 0.3 fusion.2.refs_0_
  94.2 1.4 %copy-done = f32[2,128,2560]{2,1,0:T(8,128)S(1)} copy-done((f32[2,128,2560]{2,1,0:T(8,128)S(1)}, f32[2,128,2560]{2,1,0:T(8,128)}, u32[]{:S(2)}) %copy-start) | copy-done | bytes 2621464
  95.6 36.5 %shard_map.121 = bf16[512,1280]{1,0:T(8,128)(2,1)S(1)} custom-call(f32[128,2560]{1,0:T(8,128)S(1)} %fusion.2.refs_0_, f32[2,128,2560]{2,1,0:T(8,128)S(1)} %copy-done, f32[2,8,2560]{2,1,0:T(8,128)S(1)} %copy-done.13, bf16[512,256]{1,0:T(8,128)(2,1)S(1)} %get-tuple-element.17.refs_3_, f32[512,128]{1,0:T(8,128)S(1)} %copy-done.6, bf16[512,2560]{1,0:T(8,128)(2,1)} %refs_5_.1, ...), custom_call_target="tpu_custom_call" | custom-call | flops 6710886400 | bytes 13107200 | tf_op jit(solution)/shard_map/pallas_call | solution.py:492
  132.1 1.1 copy.36
  (57 shorter events, 0.8 us)
Async XLA Ops:
  2.3 8.3 %collective-permute-start = (bf16[3,2944]{1,0:T(4,128)(2,1)S(1)}, bf16[3,2944]{1,0:T(4,128)(2,1)S(1)}, u32[]{:S(2)}, u32[]{:S(2)}) collective-permute-start(bf16[3,2944]{1,0:T(4,128)(2,1)S(1)} %pad_maximum_fusion.1), channel_id=1, source_target_pairs={{0,4},{4,8},{8,12},{12,16},{16,20},{20,24},{24,28},{1,5},{5,9},{9,... | collective-permute-start | bytes 53000 | tf_op jit(solution)/shard_map/ppermute | solution.py:18
  14.0 0.9 copy-start.3
  14.9 0.9 copy-start.4
  28.6 0.7 copy-start.5
  29.3 0.7 copy-start.7
  30.1 0.7 copy-start.8
  30.7 0.7 copy-start.10
  31.5 0.7 copy-start.12
  32.1 5.6 %copy-start.9 = (f32[512,128]{1,0:T(8,128)S(1)}, f32[512,128]{1,0:T(8,128)}, u32[]{:S(2)}) copy-start(f32[512,128]{1,0:T(8,128)} %copy-done.8) | copy-start | bytes 786436
  32.1 5.6 %copy-start.11 = (f32[512,128]{1,0:T(8,128)S(1)}, f32[512,128]{1,0:T(8,128)}, u32[]{:S(2)}) copy-start(f32[512,128]{1,0:T(8,128)} %copy-done.10) | copy-start | bytes 786436
  32.2 18.3 %collective-permute-start.1 = (bf16[144,2560]{1,0:T(8,128)(2,1)}, bf16[144,2560]{1,0:T(8,128)(2,1)}, u32[]{:S(2)}, u32[]{:S(2)}) collective-permute-start(bf16[144,2560]{1,0:T(8,128)(2,1)} %get-tuple-element.14), channel_id=1, source_target_pairs={{0,4},{4,0},{8,12},{12,8},{16,20},{20,16},{24,28},{28,24},{1,5},{5... | collective-permute-start | bytes 2211848 | tf_op jit(solution)/shard_map/ppermute | solution.py:383
  33.7 2.9 %copy-start.16 = (f32[256]{0:T(256)}, f32[256]{0:T(256)S(1)}, u32[]{:S(2)}) copy-start(f32[256]{0:T(256)S(1)} %get-tuple-element.48) | copy-start | bytes 3076
  52.9 18.0 %collective-permute-start.2 = (bf16[144,2560]{1,0:T(8,128)(2,1)S(1)}, bf16[144,2560]{1,0:T(8,128)(2,1)S(1)}, u32[]{:S(2)}, u32[]{:S(2)}) collective-permute-start(bf16[144,2560]{1,0:T(8,128)(2,1)S(1)} %pad_maximum_fusion), channel_id=1, source_target_pairs={{0,8},{4,12},{8,16},{12,20},{16,24},{20,28},{1,9},{5,13},{9,17},{1... | collective-permute-start | bytes 2211848 | tf_op jit(solution)/shard_map/ppermute | solution.py:18
  56.4 18.9 %copy-start.14 = (f32[256,1]{1,0:T(8,128)S(1)}, f32[256,1]{1,0:T(8,128)}, u32[]{:S(2)}) copy-start(f32[256,1]{1,0:T(8,128)} %copy.31.ids_col_ref) | copy-start | bytes 3076
  56.4 18.9 %copy-start.15 = (f32[1,2560]{1,0:T(1,128)S(1)}, f32[1,2560]{1,0:T(1,128)}, u32[]{:S(2)}) copy-start(f32[1,2560]{1,0:T(1,128)} %broadcast_in_dim_reshape.3.skip_ref) | copy-start | bytes 30724
  56.5 18.9 %copy-start.17 = (f32[256]{0:T(256)S(1)}, f32[256]{0:T(256)}, u32[]{:S(2)}) copy-start(f32[256]{0:T(256)} %copy-done.16) | copy-start | bytes 3076
  70.9 22.9 %collective-permute-start.3 = (bf16[144,2560]{1,0:T(8,128)(2,1)S(1)}, bf16[144,2560]{1,0:T(8,128)(2,1)S(1)}, u32[]{:S(2)}, u32[]{:S(2)}) collective-permute-start(bf16[144,2560]{1,0:T(8,128)(2,1)S(1)} %collective-permute-done.2), channel_id=1, source_target_pairs={{0,8},{4,12},{8,16},{12,20},{16,24},{20,28},{1,9},{5,13},{9,17},{1... | collective-permute-start | bytes 2211848 | tf_op jit(solution)/shard_map/ppermute | solution.py:18
  83.0 1.5 %copy-start.1 = (f32[256,2560]{1,0:T(8,128)}, f32[256,2560]{1,0:T(8,128)S(1)}, u32[]{:S(2)}) copy-start(f32[256,2560]{1,0:T(8,128)S(1)} %shard_map.119.refs_8_) | copy-start | bytes 7864324
  92.1 1.5 %copy-start.2 = (f32[256,2560]{1,0:T(8,128)}, f32[256,2560]{1,0:T(8,128)S(1)}, u32[]{:S(2)}) copy-start(f32[256,2560]{1,0:T(8,128)S(1)} %shard_map.120.refs_9_) | copy-start | bytes 7864324
  93.8 1.7 %copy-start = (f32[2,128,2560]{2,1,0:T(8,128)S(1)}, f32[2,128,2560]{2,1,0:T(8,128)}, u32[]{:S(2)}) copy-start(f32[2,128,2560]{2,1,0:T(8,128)} %get-tuple-element.15.refs_1_) | copy-start | bytes 7864324
  93.9 1.7 %copy-start.6 = (f32[512,128]{1,0:T(8,128)S(1)}, f32[512,128]{1,0:T(8,128)}, u32[]{:S(2)}) copy-start(f32[512,128]{1,0:T(8,128)} %copy-done.5) | copy-start | bytes 786436
  93.9 1.8 %copy-start.13 = (f32[2,8,2560]{2,1,0:T(8,128)S(1)}, f32[2,8,2560]{2,1,0:T(8,128)}, u32[]{:S(2)}) copy-start(f32[2,8,2560]{2,1,0:T(8,128)} %copy-done.12) | copy-start | bytes 491524

commit v4 on v3

--- a/solution.py
+++ b/solution.py
@@ -182,6 +182,228 @@
     lax.fori_loop(0, width // size, group, 0)
 
 
+def chain_kernel(
+    head_size,
+    state_ref, mixed_ref, bc_ref, cum_ref, cum_t_ref, step_t_ref, gain_t_ref, ids_col_ref,
+    ids_row_ref, skip_ref,
+    part_ref, enter_ref,
+    scores, got, whole, near, far, sent, landed, own_decay, got_decay, pair_decay, near_decay,
+    decay_sems, got_sems, whole_sems, far_sems, land_sems,
+):
+    rows, width = mixed_ref.shape
+    size = group_lanes(width)
+    per_group = size // head_size
+    groups = width // size
+    pieces = groups // 2
+    blocks = rows // SPAN
+    state_size = bc_ref.shape[1] // 2
+    half = SPAN // 2
+    f32, bf16 = jnp.float32, jnp.bfloat16
+    count = lax.axis_size("seq")
+    me = lax.axis_index("seq")
+    parity = lax.rem(me, 2)
+    odd = parity == 1
+    partner = me + 1 - 2 * parity
+    has_up = me < count - 2
+    has_down = me >= 2
+    has_far = me >= 4
+    above = lax.rem(me + 2, count)
+    below = lax.rem(me + count - 2, count)
+    mesh_type = pl.DeviceIdType.MESH
+
+    barrier = pltpu.get_barrier_semaphore()
+    pl.semaphore_signal(barrier, inc=1, device_id={"seq": partner}, device_id_type=mesh_type)
+
+    @pl.when(has_up)
+    def greet_above():
+        pl.semaphore_signal(barrier, inc=1, device_id={"seq": above}, device_id_type=mesh_type)
+
+    @pl.when(has_down)
+    def greet_below():
+        pl.semaphore_signal(barrier, inc=1, device_id={"seq": below}, device_id_type=mesh_type)
+
+    decay = gain_t_ref[SPAN - 1 : SPAN, :]
+    for b in range(1, blocks):
+        decay = decay * gain_t_ref[(b + 1) * SPAN - 1 : (b + 1) * SPAN, :]
+    own_decay[...] = jnp.broadcast_to(decay, own_decay.shape)
+
+    @pl.when(jnp.logical_not(has_down))
+    def clear_near():
+        near[...] = jnp.zeros_like(near)
+        near_decay[...] = jnp.zeros_like(near_decay)
+
+    @pl.when(jnp.logical_not(has_far))
+    def clear_far():
+        far[...] = jnp.zeros_like(far)
+
+    @pl.when(has_up & has_down)
+    def meet_three():
+        pl.semaphore_wait(barrier, 3)
+
+    @pl.when(jnp.logical_not(has_up & has_down))
+    def meet_two():
+        pl.semaphore_wait(barrier, 2)
+
+    def lanes_of(which, k):
+        return pl.ds(pl.multiple_of((which * pieces + k) * size, size), size)
+
+    def remote(source, landing, send_sem, recv_sem, device):
+        return pltpu.make_async_remote_copy(
+            src_ref=source, dst_ref=landing, send_sem=send_sem, recv_sem=recv_sem,
+            device_id={"seq": device}, device_id_type=mesh_type,
+        )
+
+    def decay_copy():
+        return remote(own_decay, got_decay, decay_sems.at[0], decay_sems.at[1], partner)
+
+    def pair_decay_copy():
+        return remote(pair_decay, near_decay, decay_sems.at[2], decay_sems.at[3], above)
+
+    def state_copy(k):
+        return remote(
+            state_ref.at[:, lanes_of(1 - parity, k)], got.at[k], got_sems.at[0, k],
+            got_sems.at[1, k], partner,
+        )
+
+    def whole_copy(k):
+        return remote(whole.at[k], near.at[k], whole_sems.at[0, k], whole_sems.at[1, k], above)
+
+    def far_copy(k):
+        return remote(near.at[k], far.at[k], far_sems.at[0, k], far_sems.at[1, k], above)
+
+    def land_copy(k):
+        return remote(sent.at[k], landed.at[k], land_sems.at[0, k], land_sems.at[1, k], partner)
+
+    decay_copy().start()
+    for k in range(pieces):
+        state_copy(k).start()
+
+    row_id = lax.broadcasted_iota(jnp.int32, (SPAN, SPAN), 0)
+    col_id = lax.broadcasted_iota(jnp.int32, (SPAN, SPAN), 1)
+    for b in range(blocks):
+        span = slice(b * SPAN, (b + 1) * SPAN)
+        raw = lax.dot_general(
+            bc_ref[span, state_size:], bc_ref[span, :state_size], (((1,), (1,)), ((), ())),
+            preferred_element_type=f32,
+        )
+        same = (ids_col_ref[span, :] == ids_row_ref[:, span]) & (col_id <= row_id)
+        scores[b] = jnp.where(same, raw, 0.0)
+
+    def mix(c, b):
+        lanes = pl.ds(pl.multiple_of(c * size, size), size)
+        span = pl.ds(b * SPAN, SPAN)
+        turn = lax.rem(HEADS_PAD - c * per_group, HEADS_PAD)
+        cum_t = pltpu.roll(cum_t_ref[span, :], turn, 1)
+        steps = spread_heads(pltpu.roll(step_t_ref[span, :], turn, 1), head_size, size)
+        x = mixed_ref[span, lanes].astype(f32)
+        stepped = (x * steps).astype(bf16)
+        tops, bottoms = [], []
+        for k in range(per_group):
+            own = slice(k * head_size, (k + 1) * head_size)
+            column = cum_t[:, k : k + 1]
+            row = cum_ref[pl.ds(c * per_group + k, 1), span]
+            top = scores[b, :half, :half] * jnp.exp(
+                jnp.minimum(column[:half] - row[:, :half], 0.0)
+            )
+            bottom = scores[b, half:, :] * jnp.exp(jnp.minimum(column[half:] - row, 0.0))
+            tops.append(
+                jnp.dot(top.astype(bf16), stepped[:half, own], preferred_element_type=f32)
+            )
+            bottoms.append(
+                jnp.dot(bottom.astype(bf16), stepped[:, own], preferred_element_type=f32)
+            )
+        both = jnp.concatenate(
+            [jnp.concatenate(tops, axis=1), jnp.concatenate(bottoms, axis=1)], axis=0
+        )
+        part_ref[span, lanes] = both + skip_ref[:, lanes] * x
+
+    def decay_row(ref, k):
+        turn = lax.rem(HEADS_PAD - (parity * pieces + k) * per_group, HEADS_PAD)
+        turn = lax.rem(turn + HEADS_PAD, HEADS_PAD)
+        return spread_heads(pltpu.roll(ref[...], turn, 1), head_size, size)[0:1]
+
+    def first_state(k):
+        mine = state_ref[:, lanes_of(parity, k)].astype(f32)
+        theirs = got[k].astype(f32)
+        return jnp.where(odd, theirs, mine), jnp.where(odd, mine, theirs)
+
+    def step(j, unused):
+        @pl.when(j == 0)
+        def take_decay():
+            decay_copy().wait_recv()
+            pair_decay[...] = own_decay[...] * got_decay[...]
+
+            @pl.when(has_up)
+            def pass_decay():
+                pair_decay_copy().start()
+
+        @pl.when(j < pieces)
+        def join():
+            state_copy(j).wait_recv()
+
+            @pl.when(has_up)
+            def send_whole():
+                first, second = first_state(j)
+                odd_decay = jnp.where(odd, decay_row(own_decay, j), decay_row(got_decay, j))
+                whole[j] = (second + odd_decay * first).astype(bf16)
+                whole_copy(j).start()
+
+        @pl.when((j >= 2) & (j < pieces + 2))
+        def forward():
+            @pl.when(has_down)
+            def take_near():
+                whole_copy(j - 2).wait_recv()
+
+                @pl.when(has_up)
+                def pass_near():
+                    far_copy(j - 2).start()
+
+        @pl.when(j >= pieces)
+        def close():
+            k = j - pieces
+
+            @pl.when((k == 0) & has_down)
+            def take_near_decay():
+                pair_decay_copy().wait_recv()
+
+            @pl.when(has_far)
+            def take_far():
+                far_copy(k).wait_recv()
+
+            entering = near[k].astype(f32) + decay_row(near_decay, k) * far[k].astype(f32)
+            first, _ = first_state(k)
+            even_decay = jnp.where(odd, decay_row(got_decay, k), decay_row(own_decay, k))
+            later = first + even_decay * entering
+            enter_ref[:, lanes_of(parity, k)] = jnp.where(odd, later, entering).astype(bf16)
+            sent[k] = jnp.where(odd, entering, later).astype(bf16)
+            land_copy(k).start()
+
+        for b in range(blocks):
+            mix(j, b)
+        return unused
+
+    lax.fori_loop(0, groups, step, 0)
+
+    decay_copy().wait_send()
+    for k in range(pieces):
+        land_copy(k).wait_recv()
+        enter_ref[:, lanes_of(1 - parity, k)] = landed[k]
+    for k in range(pieces):
+        state_copy(k).wait_send()
+        land_copy(k).wait_send()
+
+    @pl.when(has_up)
+    def finish():
+        pair_decay_copy().wait_send()
+        for k in range(pieces):
+            whole_copy(k).wait_send()
+
+    @pl.when(has_up & has_down)
+    def finish_far():
+        for k in range(pieces):
+            far_copy(k).wait_send()
+
+
 def gate_kernel(
     head_size,
     state_ref, bc_ref, gain_t_ref, part_ref, z_ref, norm_ref,
@@ -211,14 +433,14 @@
     )
 
 
-def tail_kernel(head_size, chunk, blocks, *refs):
+def tail_kernel(head_size, chunk, parts, *refs):
     state_ref, fresh_ref, decay_ref, bc_ref, gain_t_ref, z_ref, norm_ref, w_ref = refs[:8]
-    part_refs = refs[8 : 8 + blocks]
-    out_ref = refs[8 + blocks]
+    part_refs = refs[8 : 8 + parts]
+    out_ref = refs[8 + parts]
     (
         w_far, w_near, scaled, state, sums, sends, gots, row_sends, row_gots,
         w_sems, send_sems, got_sems, row_send_sems, row_got_sems,
-    ) = refs[9 + blocks :]
+    ) = refs[9 + parts :]
     rows, width = z_ref.shape
     out_width = out_ref.shape[1]
     count = rows // chunk
@@ -278,7 +500,8 @@
             reached = jnp.dot(
                 bc_ref[here, state_size:], state[:, lanes], preferred_element_type=jnp.float32
             )
-            y = part_refs[b][inner, lanes] + gain * reached
+            part = part_refs[0][here, lanes] if parts == 1 else part_refs[b][inner, lanes]
+            y = part + gain * reached
             y = y.astype(jnp.bfloat16).astype(jnp.float32)
             gated = y * silu(z_ref[here, lanes].astype(jnp.float32))
             scaled[here, lanes] = (gated * norm_ref[:, lanes]).astype(jnp.bfloat16)
@@ -466,21 +689,48 @@
         flags, conv_x.astype(f32), conv_bc.astype(f32),
     )
     skip_row = jnp.repeat(d_skip, head_size)[None, :]
-    parts = []
-    for b in range(blocks):
-        span = slice(b * SPAN, (b + 1) * SPAN)
-        parts.append(
-            call(
-                functools.partial(mix_kernel, head_size),
-                shape((SPAN, width), f32),
-                [pltpu.VMEM((SPAN, SPAN), f32)],
-                2 * SPAN * SPAN * width * 16,
-                8 * SPAN * width,
-                mixed[span], mixed_bc[span], cum[:, span], cum_t[span], step_t[span],
-                own_ids[span][:, None], own_ids[span][None, :], skip_row,
-            )
+    vmem = pl.BlockSpec(memory_space=pltpu.VMEM)
+    pieces = width // 512
+    if lax.axis_size("seq") == 8 and width % 512 == 0 and pieces >= 3:
+        piece = (pieces, state_size, 256)
+        part, state = pl.pallas_call(
+            functools.partial(chain_kernel, head_size),
+            out_shape=(shape((rows, width), f32), shape((state_size, width), bf16)),
+            in_specs=[vmem] * 10,
+            out_specs=(vmem, vmem),
+            scratch_shapes=[pltpu.VMEM((blocks, SPAN, SPAN), f32)]
+            + [pltpu.VMEM(piece, bf16)] * 6
+            + [pltpu.VMEM((8, HEADS_PAD), f32)] * 4
+            + [pltpu.SemaphoreType.DMA((4,))]
+            + [pltpu.SemaphoreType.DMA((2, pieces))] * 4,
+            compiler_params=pltpu.CompilerParams(
+                collective_id=1, has_side_effects=True, vmem_limit_bytes=VMEM_BYTES
+            ),
+            cost_estimate=pl.CostEstimate(
+                flops=2 * rows * SPAN * width * 16, bytes_accessed=8 * rows * width,
+                transcendentals=0,
+            ),
+        )(
+            message[:state_size], mixed, mixed_bc, cum, cum_t, step_t, gain_t,
+            own_ids[:, None], own_ids[None, :], skip_row,
         )
-    state = pass_state(message)
+        parts = [part]
+    else:
+        parts = []
+        for b in range(blocks):
+            span = slice(b * SPAN, (b + 1) * SPAN)
+            parts.append(
+                call(
+                    functools.partial(mix_kernel, head_size),
+                    shape((SPAN, width), f32),
+                    [pltpu.VMEM((SPAN, SPAN), f32)],
+                    2 * SPAN * SPAN * width * 16,
+                    8 * SPAN * width,
+                    mixed[span], mixed_bc[span], cum[:, span], cum_t[span], step_t[span],
+                    own_ids[span][:, None], own_ids[span][None, :], skip_row,
+                )
+            )
+        state = pass_state(message)
 
     members = lax.axis_size("tensor")
     member = lax.axis_index("tensor")
@@ -488,11 +738,10 @@
     if members == 2 and out_width % 128 == 0:
         chunk = 128
         count = rows // chunk
-        vmem = pl.BlockSpec(memory_space=pltpu.VMEM)
         return pl.pallas_call(
-            functools.partial(tail_kernel, head_size, chunk, blocks),
+            functools.partial(tail_kernel, head_size, chunk, len(parts)),
             out_shape=shape((rows, out_width), bf16),
-            in_specs=[vmem] * 7 + [pl.BlockSpec(memory_space=pl.ANY)] + [vmem] * blocks,
+            in_specs=[vmem] * 7 + [pl.BlockSpec(memory_space=pl.ANY)] + [vmem] * len(parts),
             out_specs=vmem,
             scratch_shapes=[
                 pltpu.VMEM((width, out_width), bf16),
@@ -519,6 +768,8 @@
                 transcendentals=0,
             ),
         )(state, fresh, decay, mixed_bc, gain_t, z_gate, norm_gain[None, :], w_out, *parts)
+    if len(parts) != blocks:
+        parts = [parts[0][b * SPAN : (b + 1) * SPAN] for b in range(blocks)]
     pieces = []
     for b in range(blocks):
         span = slice(b * SPAN, (b + 1) * SPAN)

time: 134 us -> 93.3 us (0.70)
  waiting for transfers between devices: 26.9 us -> 0.01 us
  local copies, waits for them, and re-layouts: 18.8 us -> 6.59 us
  Pallas kernels: 64.5 us -> 75.5 us
  starting transfers between devices: 14.3 us -> 4.84 us
  other arithmetic: 8.34 us -> 5.44 us
    pallas_call x1 -> x2, Pallas kernels: 36.5 us -> 62.9 us  [the longest x1 36.3 us: local(): pl.pallas_call(functools.partial(tail_kernel, head_size, chunk, len(parts...]
    pallas_call x3 -> x1, Pallas kernels: 28 us -> 12.5 us  [call(): pl.pallas_call(kernel, out_shape=out_shape, in_specs=[pl.BlockSpec(memory...]
    ppermute x3 -> x1, waiting for transfers between devices: 14.3 us -> 0.01 us  [shifted(): lax.ppermute(block, axis, [(i, i + distance) for i in range(count - dista...]
    ppermute x1 -> x0, waiting for transfers between devices: 12.6 us -> none  [pass_state(): other = lax.ppermute(message, 'seq', [(i, i ^ 1) for i in range(count)])]
    unnamed x41 -> x9, local copies, waits for them, and re-layouts: 11.1 us -> 2.16 us
    ppermute x3 -> x1, starting transfers between devices: 12.8 us -> 4.84 us  [shifted(): lax.ppermute(block, axis, [(i, i + distance) for i in range(count - dista...]
    convert_element_type x4 -> x0, other arithmetic: 2.47 us -> none  [the longest x2 2.25 us: split_message(): wide = message.astype(jnp.float32)]
    ppermute x1 -> x0, starting transfers between devices: 1.55 us -> none  [pass_state(): other = lax.ppermute(message, 'seq', [(i, i ^ 1) for i in range(count)])]
  transfers between devices with their start and end apart: 4 -> 1, of which waited for: 2 -> 0; matrix products, arithmetic and copies ran while one was open for 6% -> 5% of each run, Pallas kernels for 11% -> 0%
where the time goes in v4:
time: 93.3 us; the launch traced here: 92.5 us
  Pallas kernels  75.5 us (81%)
  local copies, waits for them, and re-layouts  6.59 us (7%)
  other arithmetic  5.44 us (6%)
  starting transfers between devices  4.84 us (5%)
    pallas_call x1, Pallas kernels, local(): pl.pallas_call(functools.partial(tail_kernel, head_size, chunk, len(parts...  36.3 us
    pallas_call x1, Pallas kernels, local(): pl.pallas_call(functools.partial(chain_kernel, head_size), out_shape=(sha...  26.6 us
    pallas_call x1, Pallas kernels, call(): pl.pallas_call(kernel, out_shape=out_shape, in_specs=[pl.BlockSpec(memory...  12.5 us
    ppermute x1, starting transfers between devices, shifted(): lax.ppermute(block, axis, [(i, i + distance) for i in range(count - dista...  4.84 us
    unnamed x9, local copies, waits for them, and re-layouts  2.16 us
  transfers between devices with their start and end apart: 1, of which 0 were waited for; matrix products, arithmetic and copies ran while one was open for 5% of the time, Pallas kernels for 0%

profile of v4, /device:TPU:0, one launch (start us, length us, event | category | flops | bytes accessed | tf_op | source)
XLA Modules:
  0.0 92.5 jit_solution(3497082696381205790)
XLA Ops:
  0.0 0.7 fusion.1
  0.7 0.1 slice.48
  0.8 0.8 slice.46
  1.6 0.7 slice.47
  2.3 0.1 broadcast_in_dim.25
  2.3 4.8 %collective-permute-start = (bf16[3,2944]{1,0:T(4,128)(2,1)S(1)}, bf16[3,2944]{1,0:T(4,128)(2,1)S(1)}, u32[]{:S(2)}, u32[]{:S(2)}) collective-permute-start(bf16[3,2944]{1,0:T(4,128)(2,1)S(1)} %pad_maximum_fusion), channel_id=1, source_target_pairs={{0,4},{4,8},{8,12},{12,16},{16,20},{20,24},{24,28},{1,5},{5,9},{9,... | collective-permute-start | bytes 53000 | tf_op jit(solution)/shard_map/ppermute | solution.py:18
  7.2 0.2 slice_reduce_fusion
  7.4 0.7 exponential_negate_fusion
  8.1 0.9 broadcast_multiply_fusion
  9.0 0.1 broadcast_bitcast_fusion
  9.1 0.1 slice.57
  9.2 0.7 convert_element_type.31.conv_x_ref
  9.9 0.7 convert_element_type.32.conv_bc_ref
  10.6 0.1 copy.28.ids_col_ref
  10.8 0.7 broadcast_in_dim.29
  11.5 0.1 broadcast_in_dim_reshape.3.skip_ref
  11.6 0.7 broadcast_in_dim.30.refs_6_
  12.3 0.0 collective-permute-done
  12.3 0.1 convert_select_fusion
  12.4 0.5 slice.55
  12.9 0.8 pad_maximum_fusion.2
  13.7 0.1 broadcast_bitcast_fusion.1
  13.8 0.1 pad_maximum_fusion.1
  13.9 0.8 slice_compare_fusion
  14.7 0.1 copy.27.flags_ref
  14.9 0.0 copy-start.1
  14.9 0.9 %copy-done.1 = bf16[512,256]{1,0:T(8,128)(2,1)S(1)} copy-done((bf16[512,256]{1,0:T(8,128)(2,1)S(1)}, bf16[512,256]{1,0:T(8,128)(2,1)}, u32[]{:S(2)}) %copy-start.1) | copy-done | bytes 262168
  15.9 12.5 %shard_map.118 = (bf16[512,2560]{1,0:T(8,128)(2,1)S(1)}, bf16[512,256]{1,0:T(8,128)(2,1)S(1)}, f32[128,512]{1,0:T(8,128)S(1)}, f32[512,128]{1,0:T(8,128)S(1)}, f...) custom-call(bf16[512,2560]{1,0:T(8,128)(2,1)} %x_ref.1, ...), custom_call_target="tpu_custom_call" | custom-call | flops 335544320 | bytes 10485760 | tf_op jit(solution)/shard_map/pallas_call | solution.py:566
  28.5 0.0 copy-start
  28.5 26.6 %shard_map.119 = (f32[512,2560]{1,0:T(8,128)}, bf16[128,2560]{1,0:T(8,128)(2,1)S(1)}) custom-call(bf16[128,2560]{1,0:T(8,128)(2,1)S(1)} %slice.60.state_ref, bf16[512,2560]{1,0:T(8,128)(2,1)S(1)} %get-tuple-element.17.mixed_ref, bf16[512,256]{1,0:T(8,128)(2,1)S(1)} %get-tuple-element.18.bc_ref.refs_3_, f32[128,512]{1,0:T(8,128)S(1)} %get-tuple-element.19.cum_ref, ...), custom_call_target="tpu_custom_call" | custom-call | flops 10737418240 | bytes 10485760 | tf_op jit(solution)/shard_map/pallas_call | solution.py:696
  55.1 0.0 copy-done
  55.1 36.3 %shard_map.120 = bf16[512,1280]{1,0:T(8,128)(2,1)S(1)} custom-call(bf16[128,2560]{1,0:T(8,128)(2,1)S(1)} %get-tuple-element.23.refs_0_, f32[2,128,2560]{2,1,0:T(8,128)S(1)} %copy-done, f32[2,8,2560]{2,1,0:T(8,128)S(1)} %get-tuple-element.25.refs_2_, bf16[512,256]{1,0:T(8,128)(2,1)S(1)} %get-tuple-element.18.bc_ref.refs_3_, ...), custom_call_target="tpu_custom_call" | custom-call | flops 6710886400 | bytes 13107200 | tf_op jit(solution)/shard_map/pallas_call | solution.py:741
  91.5 1.1 %copy.32 = bf16[512,1280]{1,0:T(8,128)(2,1)} copy(bf16[512,1280]{1,0:T(8,128)(2,1)S(1)} %shard_map.120) | data formatting | bytes 2621440
  (17 shorter events, 0.2 us)
Async XLA Ops:
  2.3 10.0 %collective-permute-start = (bf16[3,2944]{1,0:T(4,128)(2,1)S(1)}, bf16[3,2944]{1,0:T(4,128)(2,1)S(1)}, u32[]{:S(2)}, u32[]{:S(2)}) collective-permute-start(bf16[3,2944]{1,0:T(4,128)(2,1)S(1)} %pad_maximum_fusion), channel_id=1, source_target_pairs={{0,4},{4,8},{8,12},{12,16},{16,20},{20,24},{24,28},{1,5},{5,9},{9,... | collective-permute-start | bytes 53000 | tf_op jit(solution)/shard_map/ppermute | solution.py:18
  14.9 1.0 %copy-start.1 = (bf16[512,256]{1,0:T(8,128)(2,1)S(1)}, bf16[512,256]{1,0:T(8,128)(2,1)}, u32[]{:S(2)}) copy-start(bf16[512,256]{1,0:T(8,128)(2,1)} %bc_ref.1) | copy-start | bytes 786436
  28.5 26.7 %copy-start = (f32[2,128,2560]{2,1,0:T(8,128)S(1)}, f32[2,128,2560]{2,1,0:T(8,128)}, u32[]{:S(2)}) copy-start(f32[2,128,2560]{2,1,0:T(8,128)} %get-tuple-element.24.refs_1_) | copy-start | bytes 7864324

commit v5 on v3

--- a/solution.py
+++ b/solution.py
@@ -211,37 +211,344 @@
     )
 
 
-def tail_kernel(head_size, chunk, blocks, *refs):
-    state_ref, fresh_ref, decay_ref, bc_ref, gain_t_ref, z_ref, norm_ref, w_ref = refs[:8]
-    part_refs = refs[8 : 8 + blocks]
-    out_ref = refs[8 + blocks]
-    (
-        w_far, w_near, scaled, state, sums, sends, gots, row_sends, row_gots,
-        w_sems, send_sems, got_sems, row_send_sems, row_got_sems,
-    ) = refs[9 + blocks :]
-    rows, width = z_ref.shape
+def fused_kernel(
+    head_size, chunk,
+    x_ref, bc_in_ref, z_hbm, dt_ref, ids_row_ref, conv_x_ref, conv_bc_ref, a_log_ref, bias_ref,
+    skip_heads_ref, norm_ref, w_ref,
+    out_ref,
+    ext, ids_ext, rim_x, rim_bc, rim_ids, ids_sent, mixed_ref, bc_ref, cum_ref, cum_t_ref,
+    step_t_ref, gain_t_ref, tail_t, b_t, fresh_ref, decay_ref, state_ref, part_ref, enter_ref,
+    scores, got, whole, near, far, sent, landed, own_decay, got_decay, pair_decay, near_decay,
+    z_ref, w_far, w_near, scaled, state, sums, sends, gots, row_sends, row_gots,
+    halo_sems, load_sems, decay_sems, got_sems, whole_sems, far_sems, land_sems,
+    send_sems, got_out_sems, row_send_sems, row_got_sems,
+):
+    rows, width = x_ref.shape
+    size = group_lanes(width)
+    per_group = size // head_size
+    groups = width // size
+    pieces = groups // 2
+    blocks = rows // SPAN
+    state_size = bc_in_ref.shape[1] // 2
+    half = SPAN // 2
     out_width = out_ref.shape[1]
+    heads = dt_ref.shape[0]
+    f32, bf16 = jnp.float32, jnp.bfloat16
+    seq_count = lax.axis_size("seq")
+    me = lax.axis_index("seq")
+    parity = lax.rem(me, 2)
+    odd = parity == 1
+    partner = me + 1 - 2 * parity
+    beyond = lax.rem(me + seq_count - 1 + 2 * parity, seq_count)
+    has_up = me < seq_count - 2
+    has_down = me >= 2
+    has_far = me >= 4
+    has_next = me < seq_count - 1
+    has_prev = me >= 1
+    inside = has_next & has_prev
+    above = lax.rem(me + 2, seq_count)
+    below = lax.rem(me + seq_count - 2, seq_count)
+    following = lax.rem(me + 1, seq_count)
+    member = lax.axis_index("tensor")
+    peer = 1 - member
+    mesh_type = pl.DeviceIdType.MESH
+
+    barrier = pltpu.get_barrier_semaphore()
+    pl.semaphore_signal(barrier, inc=1, device_id={"seq": partner}, device_id_type=mesh_type)
+    pl.semaphore_signal(barrier, inc=1, device_id={"tensor": peer}, device_id_type=mesh_type)
+
+    @pl.when(has_up)
+    def greet_above():
+        pl.semaphore_signal(barrier, inc=1, device_id={"seq": above}, device_id_type=mesh_type)
+
+    @pl.when(has_down)
+    def greet_below():
+        pl.semaphore_signal(barrier, inc=1, device_id={"seq": below}, device_id_type=mesh_type)
+
+    @pl.when(inside)
+    def greet_beyond():
+        pl.semaphore_signal(barrier, inc=1, device_id={"seq": beyond}, device_id_type=mesh_type)
+
+    loads = [pltpu.make_async_copy(z_hbm, z_ref, load_sems.at[0])]
+    for k, (who, place) in enumerate(((peer, w_far), (member, w_near))):
+        loads.append(
+            pltpu.make_async_copy(
+                w_ref.at[:, pl.ds(pl.multiple_of(who * out_width, 128), out_width)],
+                place,
+                load_sems.at[k + 1],
+            )
+        )
+    for load in loads:
+        load.start()
+    ids_row = ids_row_ref[...].astype(f32)
+    ids_sent[...] = jnp.broadcast_to(ids_row[:, rows - 128 :], ids_sent.shape)
+
+    @pl.when(jnp.logical_not(has_down))
+    def clear_near():
+        near[...] = jnp.zeros_like(near)
+        near_decay[...] = jnp.zeros_like(near_decay)
+
+    @pl.when(jnp.logical_not(has_far))
+    def clear_far():
+        far[...] = jnp.zeros_like(far)
+
+    @pl.when(jnp.logical_not(has_prev))
+    def clear_rim():
+        rim_x[...] = jnp.zeros_like(rim_x)
+        rim_bc[...] = jnp.zeros_like(rim_bc)
+        rim_ids[...] = jnp.full(rim_ids.shape, -1.0, f32)
+
+    @pl.when(has_up & has_down)
+    def meet_five():
+        pl.semaphore_wait(barrier, 5)
+
+    @pl.when(inside & jnp.logical_not(has_up & has_down))
+    def meet_four():
+        pl.semaphore_wait(barrier, 4)
+
+    @pl.when(jnp.logical_not(inside))
+    def meet_three():
+        pl.semaphore_wait(barrier, 3)
+
+    def lanes_of(which, k):
+        return pl.ds(pl.multiple_of((which * pieces + k) * size, size), size)
+
+    def remote(source, landing, send_sem, recv_sem, device):
+        return pltpu.make_async_remote_copy(
+            src_ref=source, dst_ref=landing, send_sem=send_sem, recv_sem=recv_sem,
+            device_id={"seq": device}, device_id_type=mesh_type,
+        )
+
+    def decay_copy():
+        return remote(own_decay, got_decay, decay_sems.at[0], decay_sems.at[1], partner)
+
+    def pair_decay_copy():
+        return remote(pair_decay, near_decay, decay_sems.at[2], decay_sems.at[3], above)
+
+    def state_copy(k):
+        return remote(
+            state_ref.at[:, lanes_of(1 - parity, k)], got.at[k], got_sems.at[0, k],
+            got_sems.at[1, k], partner,
+        )
+
+    def whole_copy(k):
+        return remote(whole.at[k], near.at[k], whole_sems.at[0, k], whole_sems.at[1, k], above)
+
+    def far_copy(k):
+        return remote(near.at[k], far.at[k], far_sems.at[0, k], far_sems.at[1, k], above)
+
+    def land_copy(k):
+        return remote(sent.at[k], landed.at[k], land_sems.at[0, k], land_sems.at[1, k], partner)
+
+    def halo_copies():
+        last = pl.ds(rows - 16, 16)
+        return [
+            remote(x_ref.at[last, :], rim_x, halo_sems.at[0, 0], halo_sems.at[1, 0], following),
+            remote(bc_in_ref.at[last, :], rim_bc, halo_sems.at[0, 1], halo_sems.at[1, 1], following),
+            remote(ids_sent, rim_ids, halo_sems.at[0, 2], halo_sems.at[1, 2], following),
+        ]
+
+    @pl.when(has_next)
+    def send_halo():
+        for copy in halo_copies():
+            copy.start()
+
+    def column(row):
+        return jnp.broadcast_to(row, (128, row.shape[1])).T
+
+    logits = dt_ref[...].astype(f32) + column(bias_ref[...])[:heads, 0:1]
+    step_size = jnp.maximum(logits, 0.0) + jnp.log1p(jnp.exp(-jnp.abs(logits)))
+    rates = -jnp.exp(column(a_log_ref[...])[:heads, 0:1]) * step_size
+    spare = jnp.zeros((HEADS_PAD - heads, rows), f32)
+    step_size = jnp.concatenate([step_size, spare])
+    rates = jnp.concatenate([rates, spare])
+    ids_ext[8 : 8 + rows, :] = column(ids_row)
+    ids = ids_ext[8 : 8 + rows, :]
+
+    @pl.when(has_prev)
+    def take_halo():
+        for copy in halo_copies():
+            copy.wait_recv()
+
+    ids_ext[0:8, :] = column(rim_ids[0:1, :])[120:128, :]
+    taps = conv_x_ref.shape[0]
+    keeps = []
+    for k in range(1, taps):
+        same = ids_ext[8 - k : 8 - k + rows, :] == ids
+        keeps.append(jnp.concatenate([same.astype(f32)] * (size // 128), axis=1) > 0.5)
+    ext[0:8, :] = rim_bc[...].astype(f32)[8:16]
+    ext[8 : 8 + rows, :] = bc_in_ref[...].astype(f32)
+    mixed_bc = conv_taps(ext, conv_bc_ref[...].astype(f32), keeps, rows)
+    bc_ref[...] = mixed_bc.astype(bf16)
+    row_id = lax.broadcasted_iota(jnp.int32, (SPAN, SPAN), 0)
+    col_id = lax.broadcasted_iota(jnp.int32, (SPAN, SPAN), 1)
+    upper = (row_id <= col_id).astype(f32)
+    for b in range(blocks):
+        span = slice(b * SPAN, (b + 1) * SPAN)
+        b_t[:, span] = mixed_bc[span, :state_size].T.astype(bf16)
+        cum = jnp.dot(
+            rates[:, span], upper,
+            precision=lax.Precision.HIGHEST, preferred_element_type=f32,
+        )
+        cum_ref[:, span] = cum
+        cum_t = cum.T
+        step_t = step_size[:, span].T
+        cum_t_ref[span, :] = cum_t
+        step_t_ref[span, :] = step_t
+        prior = ids_ext[8 + b * SPAN - 1 : 8 + b * SPAN, :]
+        final = ids_ext[8 + (b + 1) * SPAN - 1 : 8 + (b + 1) * SPAN, :]
+        gain_t_ref[span, :] = jnp.where(ids[span] == prior, jnp.exp(cum_t), 0.0)
+        tail_t[span, :] = jnp.where(
+            ids[span] == final, jnp.exp(cum_t[SPAN - 1 : SPAN] - cum_t), 0.0
+        ) * step_t
+    decay = gain_t_ref[SPAN - 1 : SPAN, :]
+    for b in range(1, blocks):
+        decay = decay * gain_t_ref[(b + 1) * SPAN - 1 : (b + 1) * SPAN, :]
+    own_decay[...] = jnp.broadcast_to(decay, own_decay.shape)
+    decay_copy().start()
+
+    def decay_row(ref, k):
+        turn = lax.rem(HEADS_PAD - (parity * pieces + k) * per_group, HEADS_PAD)
+        turn = lax.rem(turn + HEADS_PAD, HEADS_PAD)
+        return spread_heads(pltpu.roll(ref[...], turn, 1), head_size, size)[0:1]
+
+    def first_state(k):
+        mine = state_ref[:, lanes_of(parity, k)].astype(f32)
+        theirs = got[k].astype(f32)
+        return jnp.where(odd, theirs, mine), jnp.where(odd, mine, theirs)
+
+    def states(j, unused):
+        c = lax.rem(j + (1 - parity) * pieces, groups)
+        lanes = pl.ds(pl.multiple_of(c * size, size), size)
+        turn = lax.rem(HEADS_PAD - c * per_group, HEADS_PAD)
+        ext[0:8, :] = rim_x[:, lanes].astype(f32)[8:16]
+        ext[8 : 8 + rows, :] = x_ref[:, lanes].astype(f32)
+        mixed = conv_taps(ext, conv_x_ref[:, lanes].astype(f32), keeps, rows).astype(bf16)
+        mixed_ref[:, lanes] = mixed
+        weight = spread_heads(pltpu.roll(tail_t[...], turn, 1), head_size, size)
+        weighted = (mixed.astype(f32) * weight).astype(bf16)
+        running = None
+        for b in range(blocks):
+            span = slice(b * SPAN, (b + 1) * SPAN)
+            fresh = jnp.dot(b_t[:, span], weighted[span], preferred_element_type=f32)
+            ends = gain_t_ref[(b + 1) * SPAN - 8 : (b + 1) * SPAN, :]
+            block_decay = spread_heads(pltpu.roll(ends, turn, 1), head_size, size)[7:8]
+            if b + 1 < blocks:
+                fresh_ref[b, :, lanes] = fresh
+                decay_ref[b, :, lanes] = jnp.broadcast_to(block_decay, (8, size))
+            running = fresh if b == 0 else block_decay * running + fresh
+        state_ref[:, lanes] = running.astype(bf16)
+
+        @pl.when(j < pieces)
+        def send_state():
+            state_copy(j).start()
+
+        @pl.when(j == pieces)
+        def take_decay():
+            decay_copy().wait_recv()
+            pair_decay[...] = own_decay[...] * got_decay[...]
+
+            @pl.when(has_up)
+            def pass_decay():
+                pair_decay_copy().start()
+
+        @pl.when(j >= pieces)
+        def join():
+            k = j - pieces
+            state_copy(k).wait_recv()
+
+            @pl.when(has_up)
+            def send_whole():
+                first, second = first_state(k)
+                odd_decay = jnp.where(odd, decay_row(own_decay, k), decay_row(got_decay, k))
+                whole[k] = (second + odd_decay * first).astype(bf16)
+                whole_copy(k).start()
+
+        return unused
+
+    lax.fori_loop(0, groups, states, 0)
+    ids_wide = jnp.concatenate([ids] * (SPAN // 128), axis=1)
+    skip_tile = jnp.broadcast_to(skip_heads_ref[...], (8, HEADS_PAD))
+    for b in range(blocks):
+        span = slice(b * SPAN, (b + 1) * SPAN)
+        raw = lax.dot_general(
+            bc_ref[span, state_size:], bc_ref[span, :state_size], (((1,), (1,)), ((), ())),
+            preferred_element_type=f32,
+        )
+        same = (ids_wide[span] == ids_row[:, span]) & (col_id <= row_id)
+        scores[b] = jnp.where(same, raw, 0.0)
+
+    def mix(c, b):
+        lanes = pl.ds(pl.multiple_of(c * size, size), size)
+        span = pl.ds(b * SPAN, SPAN)
+        turn = lax.rem(HEADS_PAD - c * per_group, HEADS_PAD)
+        cum_t = pltpu.roll(cum_t_ref[span, :], turn, 1)
+        steps = spread_heads(pltpu.roll(step_t_ref[span, :], turn, 1), head_size, size)
+        x = mixed_ref[span, lanes].astype(f32)
+        stepped = (x * steps).astype(bf16)
+        skip = spread_heads(pltpu.roll(skip_tile, turn, 1), head_size, size)[0:1]
+        tops, bottoms = [], []
+        for k in range(per_group):
+            own = slice(k * head_size, (k + 1) * head_size)
+            column = cum_t[:, k : k + 1]
+            row = cum_ref[pl.ds(c * per_group + k, 1), span]
+            top = scores[b, :half, :half] * jnp.exp(
+                jnp.minimum(column[:half] - row[:, :half], 0.0)
+            )
+            bottom = scores[b, half:, :] * jnp.exp(jnp.minimum(column[half:] - row, 0.0))
+            tops.append(
+                jnp.dot(top.astype(bf16), stepped[:half, own], preferred_element_type=f32)
+            )
+            bottoms.append(
+                jnp.dot(bottom.astype(bf16), stepped[:, own], preferred_element_type=f32)
+            )
+        both = jnp.concatenate(
+            [jnp.concatenate(tops, axis=1), jnp.concatenate(bottoms, axis=1)], axis=0
+        )
+        part_ref[span, lanes] = both + skip * x
+
+    def step(j, unused):
+        @pl.when(j < pieces)
+        def forward():
+            @pl.when(has_down)
+            def take_near():
+                whole_copy(j).wait_recv()
+
+                @pl.when(has_up)
+                def pass_near():
+                    far_copy(j).start()
+
+        @pl.when(j >= pieces)
+        def close():
+            k = j - pieces
+
+            @pl.when((k == 0) & has_down)
+            def take_near_decay():
+                pair_decay_copy().wait_recv()
+
+            @pl.when(has_far)
+            def take_far():
+                far_copy(k).wait_recv()
+
+            entering = near[k].astype(f32) + decay_row(near_decay, k) * far[k].astype(f32)
+            first, _ = first_state(k)
+            even_decay = jnp.where(odd, decay_row(got_decay, k), decay_row(own_decay, k))
+            later = first + even_decay * entering
+            enter_ref[:, lanes_of(parity, k)] = jnp.where(odd, later, entering).astype(bf16)
+            sent[k] = jnp.where(odd, entering, later).astype(bf16)
+            land_copy(k).start()
+
+        for b in range(blocks):
+            mix(j, b)
+        return unused
+
+    lax.fori_loop(0, groups, step, 0)
+    for k in range(pieces):
+        land_copy(k).wait_recv()
+        enter_ref[:, lanes_of(1 - parity, k)] = landed[k]
+    loads[0].wait()
     count = rows // chunk
     per_block = SPAN // chunk
-    size = group_lanes(width)
-    per_group = size // head_size
-    state_size = bc_ref.shape[1] // 2
-    me = lax.axis_index("tensor")
-    peer = 1 - me
-    barrier = pltpu.get_barrier_semaphore()
-    pl.semaphore_signal(
-        barrier, inc=1, device_id={"tensor": peer}, device_id_type=pl.DeviceIdType.MESH
-    )
-    loads = [
-        pltpu.make_async_copy(
-            w_ref.at[:, pl.ds(pl.multiple_of(who * out_width, 128), out_width)],
-            place,
-            w_sems.at[k],
-        )
-        for k, (who, place) in enumerate(((peer, w_far), (me, w_near)))
-    ]
-    for load in loads:
-        load.start()
     tile = 256 if out_width % 256 == 0 else 128
 
     def product(q, weights, store):
@@ -262,13 +569,12 @@
     for q in range(count):
         b, within = q // per_block, q % per_block
         here = slice(q * chunk, (q + 1) * chunk)
-        inner = slice(within * chunk, (within + 1) * chunk)
 
         def group(c, squares):
             lanes = pl.ds(pl.multiple_of(c * size, size), size)
             turn = lax.rem(HEADS_PAD - c * per_group, HEADS_PAD)
             if q == 0:
-                state[:, lanes] = state_ref[:, lanes].astype(jnp.bfloat16)
+                state[:, lanes] = enter_ref[:, lanes]
             elif within == 0:
                 state[:, lanes] = (
                     decay_ref[b - 1, 0:1, lanes] * state[:, lanes].astype(jnp.float32)
@@ -278,7 +584,7 @@
             reached = jnp.dot(
                 bc_ref[here, state_size:], state[:, lanes], preferred_element_type=jnp.float32
             )
-            y = part_refs[b][inner, lanes] + gain * reached
+            y = part_ref[here, lanes] + gain * reached
             y = y.astype(jnp.bfloat16).astype(jnp.float32)
             gated = y * silu(z_ref[here, lanes].astype(jnp.float32))
             scaled[here, lanes] = (gated * norm_ref[:, lanes]).astype(jnp.bfloat16)
@@ -291,14 +597,12 @@
         row = jnp.sum(squares.T, axis=0, keepdims=True)
         row_sends[q] = jnp.broadcast_to(row, (8, chunk))
         if q == 0:
-            loads[0].wait()
+            loads[1].wait()
 
         def put(lanes, value):
             sends[q, :, lanes] = value
 
         product(q, w_far, put)
-        if q == 0:
-            pl.semaphore_wait(barrier, 1)
         pair = [
             pltpu.make_async_remote_copy(
                 src_ref=source.at[q],
@@ -310,14 +614,14 @@
             )
             for source, landing, out_sems, in_sems in (
                 (row_sends, row_gots, row_send_sems, row_got_sems),
-                (sends, gots, send_sems, got_sems),
+                (sends, gots, send_sems, got_out_sems),
             )
         ]
         for copy in pair:
             copy.start()
         copies.append(pair)
 
-    loads[1].wait()
+    loads[2].wait()
     for q in range(count):
         here = slice(q * chunk, (q + 1) * chunk)
 
@@ -337,6 +641,27 @@
     for pair in copies:
         for copy in pair:
             copy.wait_send()
+
+    @pl.when(has_next)
+    def finish_halo():
+        for copy in halo_copies():
+            copy.wait_send()
+
+    decay_copy().wait_send()
+    for k in range(pieces):
+        state_copy(k).wait_send()
+        land_copy(k).wait_send()
+
+    @pl.when(has_up)
+    def finish():
+        pair_decay_copy().wait_send()
+        for k in range(pieces):
+            whole_copy(k).wait_send()
+
+    @pl.when(has_up & has_down)
+    def finish_far():
+        for k in range(pieces):
+            far_copy(k).wait_send()
 
 
 def call(kernel, out_shape, scratch, flops, moved, *operands):
@@ -422,6 +747,86 @@
     blocks = rows // SPAN
     edge = rows - taps + 1
     f32, bf16 = jnp.float32, jnp.bfloat16
+    shape = jax.ShapeDtypeStruct
+    out_width = w_out.shape[1] // lax.axis_size("tensor")
+    if (
+        lax.axis_size("seq") == 8
+        and lax.axis_size("tensor") == 2
+        and width % 512 == 0
+        and width >= 1536
+        and out_width % 128 == 0
+        and bc_width == group_lanes(width)
+        and heads <= HEADS_PAD
+        and heads % 8 == 0
+    ):
+        vmem = pl.BlockSpec(memory_space=pltpu.VMEM)
+        hbm = pl.BlockSpec(memory_space=pl.ANY)
+        pieces = width // 512
+        chunk = 128
+        count = rows // chunk
+        piece = (pieces, state_size, 256)
+
+        def head_row(values):
+            return jnp.pad(values, (0, HEADS_PAD - heads))[None, :]
+
+        return pl.pallas_call(
+            functools.partial(fused_kernel, head_size, chunk),
+            out_shape=shape((rows, out_width), bf16),
+            in_specs=[vmem, vmem, hbm] + [vmem] * 8 + [hbm],
+            out_specs=vmem,
+            scratch_shapes=[
+                pltpu.VMEM((rows + 8, 256), f32),
+                pltpu.VMEM((rows + 8, 128), f32),
+                pltpu.VMEM((16, width), bf16),
+                pltpu.VMEM((16, bc_width), bf16),
+                pltpu.VMEM((8, 128), f32),
+                pltpu.VMEM((8, 128), f32),
+                pltpu.VMEM((rows, width), bf16),
+                pltpu.VMEM((rows, bc_width), bf16),
+                pltpu.VMEM((HEADS_PAD, rows), f32),
+                pltpu.VMEM((rows, HEADS_PAD), f32),
+                pltpu.VMEM((rows, HEADS_PAD), f32),
+                pltpu.VMEM((rows, HEADS_PAD), f32),
+                pltpu.VMEM((rows, HEADS_PAD), f32),
+                pltpu.VMEM((state_size, rows), bf16),
+                pltpu.VMEM((blocks, state_size, width), f32),
+                pltpu.VMEM((blocks, 8, width), f32),
+                pltpu.VMEM((state_size, width), bf16),
+                pltpu.VMEM((rows, width), f32),
+                pltpu.VMEM((state_size, width), bf16),
+                pltpu.VMEM((blocks, SPAN, SPAN), f32),
+            ]
+            + [pltpu.VMEM(piece, bf16)] * 6
+            + [pltpu.VMEM((8, HEADS_PAD), f32)] * 4
+            + [
+                pltpu.VMEM((rows, width), bf16),
+                pltpu.VMEM((width, out_width), bf16),
+                pltpu.VMEM((width, out_width), bf16),
+                pltpu.VMEM((rows, width), bf16),
+                pltpu.VMEM((state_size, width), bf16),
+                pltpu.VMEM((chunk, out_width), bf16),
+                pltpu.VMEM((count, chunk, out_width), bf16),
+                pltpu.VMEM((count, chunk, out_width), bf16),
+                pltpu.VMEM((count, 8, chunk), f32),
+                pltpu.VMEM((count, 8, chunk), f32),
+                pltpu.SemaphoreType.DMA((2, 3)),
+                pltpu.SemaphoreType.DMA((3,)),
+                pltpu.SemaphoreType.DMA((4,)),
+            ]
+            + [pltpu.SemaphoreType.DMA((2, pieces))] * 4
+            + [pltpu.SemaphoreType.DMA((count,))] * 4,
+            compiler_params=pltpu.CompilerParams(
+                collective_id=0, has_side_effects=True, vmem_limit_bytes=VMEM_BYTES
+            ),
+            cost_estimate=pl.CostEstimate(
+                flops=2 * rows * width * w_out.shape[1],
+                bytes_accessed=2 * width * w_out.shape[1],
+                transcendentals=0,
+            ),
+        )(
+            x_stream, bc_stream, z_gate, dt_stream, doc_ids[None, :], conv_x, conv_bc,
+            head_row(a_log), head_row(dt_bias), head_row(d_skip), norm_gain[None, :], w_out,
+        )
     own_ids = doc_ids.astype(f32)
     tail_ids = jnp.broadcast_to(own_ids[edge:].astype(bf16)[:, None], (taps - 1, 128))
     rim = shifted(
@@ -441,7 +846,6 @@
     columns.append((block_ids == block_ids[:, -1:]).reshape(rows))
     flags = jnp.stack([c.astype(f32) for c in columns], axis=1)
 
-    shape = jax.ShapeDtypeStruct
     mixed, mixed_bc, cum, cum_t, step_t, gain_t, fresh, decay, message = call(
         functools.partial(states_kernel, head_size),
         (
@@ -484,41 +888,6 @@
 
     members = lax.axis_size("tensor")
     member = lax.axis_index("tensor")
-    out_width = w_out.shape[1] // members
-    if members == 2 and out_width % 128 == 0:
-        chunk = 128
-        count = rows // chunk
-        vmem = pl.BlockSpec(memory_space=pltpu.VMEM)
-        return pl.pallas_call(
-            functools.partial(tail_kernel, head_size, chunk, blocks),
-            out_shape=shape((rows, out_width), bf16),
-            in_specs=[vmem] * 7 + [pl.BlockSpec(memory_space=pl.ANY)] + [vmem] * blocks,
-            out_specs=vmem,
-            scratch_shapes=[
-                pltpu.VMEM((width, out_width), bf16),
-                pltpu.VMEM((width, out_width), bf16),
-                pltpu.VMEM((rows, width), bf16),
-                pltpu.VMEM((state_size, width), bf16),
-                pltpu.VMEM((chunk, out_width), bf16),
-                pltpu.VMEM((count, chunk, out_width), bf16),
-                pltpu.VMEM((count, chunk, out_width), bf16),
-                pltpu.VMEM((count, 8, chunk), f32),
-                pltpu.VMEM((count, 8, chunk), f32),
-                pltpu.SemaphoreType.DMA((2,)),
-                pltpu.SemaphoreType.DMA((count,)),
-                pltpu.SemaphoreType.DMA((count,)),
-                pltpu.SemaphoreType.DMA((count,)),
-                pltpu.SemaphoreType.DMA((count,)),
-            ],
-            compiler_params=pltpu.CompilerParams(
-                collective_id=0, has_side_effects=True, vmem_limit_bytes=VMEM_BYTES
-            ),
-            cost_estimate=pl.CostEstimate(
-                flops=2 * rows * width * w_out.shape[1],
-                bytes_accessed=2 * width * w_out.shape[1],
-                transcendentals=0,
-            ),
-        )(state, fresh, decay, mixed_bc, gain_t, z_gate, norm_gain[None, :], w_out, *parts)
     pieces = []
     for b in range(blocks):
         span = slice(b * SPAN, (b + 1) * SPAN)

time: 134 us -> 76.8 us (0.57)
  waiting for transfers between devices: 26.9 us -> 0 us
  starting transfers between devices: 14.3 us -> 0 us
  local copies, waits for them, and re-layouts: 18.8 us -> 8.66 us
  other arithmetic: 8.34 us -> 0 us
  Pallas kernels: 64.5 us -> 67.7 us
    ppermute x4 -> x0, waiting for transfers between devices: 26.9 us -> none  [the longest x3 14.3 us: shifted(): lax.ppermute(block, axis, [(i, i + distance) for i in range(count - dista...]
    ppermute x4 -> x0, starting transfers between devices: 14.3 us -> none  [the longest x3 12.8 us: shifted(): lax.ppermute(block, axis, [(i, i + distance) for i in range(count - dista...]
    convert_element_type x7 -> x0, other arithmetic: 4.58 us -> none  [the longest x2 2.25 us: split_message(): wide = message.astype(jnp.float32)]
    unnamed x41 -> x13, local copies, waits for them, and re-layouts: 11.1 us -> 6.61 us
    slice x12 -> x0, local copies, waits for them, and re-layouts: 3.58 us -> none  [the longest x1 0.99 us: local(): cum[:, span]]
    pallas_call x4 -> x1, Pallas kernels: 64.5 us -> 67.7 us  [local(): pl.pallas_call(functools.partial(fused_kernel, head_size, chunk), out_sha...]
    another operation x8 -> x0, local copies, waits for them, and re-layouts: 1.62 us -> none  [the longest x7 0.94 us: local(): flags = jnp.stack([c.astype(f32) for c in columns], axis=1)]
  transfers between devices with their start and end apart: 4 -> 0, of which waited for: 2 -> 0; matrix products, arithmetic and copies ran while one was open for 6% -> 0% of each run, Pallas kernels for 11% -> 0%
where the time goes in v5:
time: 76.8 us; the launch traced here: 76.4 us
  Pallas kernels  67.7 us (88%)
  local copies, waits for them, and re-layouts  8.66 us (11%)
    pallas_call x1, Pallas kernels, local(): pl.pallas_call(functools.partial(fused_kernel, head_size, chunk), out_sha...  67.7 us
    unnamed x13, local copies, waits for them, and re-layouts  6.61 us

profile of v5, /device:TPU:0, one launch (start us, length us, event | category | flops | bytes accessed | tf_op | source)
XLA Modules:
  0.0 76.4 jit_solution(4272630888569410347)
XLA Ops:
  0.0 0.7 pad_bitcast_fusion.2.a_log_ref
  0.7 0.7 pad_bitcast_fusion
  1.3 0.7 broadcast_in_dim.19.norm_ref
  2.0 0.0 copy-start
  2.1 1.7 %copy-done = bf16[512,2560]{1,0:T(8,128)(2,1)S(1)} copy-done((bf16[512,2560]{1,0:T(8,128)(2,1)S(1)}, bf16[512,2560]{1,0:T(8,128)(2,1)}, u32[]{:S(2)}) %copy-start) | copy-done | bytes 2621464
  3.8 0.0 copy-start.1
  3.8 0.9 %copy-done.1 = bf16[512,256]{1,0:T(8,128)(2,1)S(1)} copy-done((bf16[512,256]{1,0:T(8,128)(2,1)S(1)}, bf16[512,256]{1,0:T(8,128)(2,1)}, u32[]{:S(2)}) %copy-start.1) | copy-done | bytes 262168
  4.7 0.0 copy-start.2
  4.7 0.8 %copy-done.2 = bf16[40,512]{1,0:T(8,128)(2,1)S(1)} copy-done((bf16[40,512]{1,0:T(8,128)(2,1)S(1)}, bf16[40,512]{1,0:T(8,128)(2,1)}, u32[]{:S(2)}) %copy-start.2) | copy-done | bytes 40984
  5.5 0.0 copy-start.3
  5.5 0.7 copy-done.3
  6.2 0.0 copy-start.4
  6.2 0.7 copy-done.4
  6.9 0.0 copy-start.5
  6.9 0.7 copy-done.5
  7.6 67.7 %shard_map.118 = bf16[512,1280]{1,0:T(8,128)(2,1)S(1)} custom-call(bf16[512,2560]{1,0:T(8,128)(2,1)S(1)} %copy-done, bf16[512,256]{1,0:T(8,128)(2,1)S(1)} %copy-done.1, bf16[512,2560]{1,0:T(8,128)(2,1)} %z_hbm.1, bf16[40,512]{1,0:T(8,128)(2,1)S(1)} %copy-done.2, s32[1,512]{1,0:T(1,128)S(1)} %bitcast.7, bf16[4,2560]{1,0:T(4,128)(2,1)S(1)} %copy-done.3, ...), custom_call_target="tpu_custom_call" | custom-call | flops 6710886400 | bytes 13107200 | tf_op jit(solution)/shard_map/pallas_call | solution.py:772
  75.3 1.1 %copy.14 = bf16[512,1280]{1,0:T(8,128)(2,1)} copy(bf16[512,1280]{1,0:T(8,128)(2,1)S(1)} %shard_map.118) | data formatting | bytes 2621440
Async XLA Ops:
  2.0 1.7 %copy-start = (bf16[512,2560]{1,0:T(8,128)(2,1)S(1)}, bf16[512,2560]{1,0:T(8,128)(2,1)}, u32[]{:S(2)}) copy-start(bf16[512,2560]{1,0:T(8,128)(2,1)} %x_ref.1) | copy-start | bytes 7864324
  3.8 0.9 %copy-start.1 = (bf16[512,256]{1,0:T(8,128)(2,1)S(1)}, bf16[512,256]{1,0:T(8,128)(2,1)}, u32[]{:S(2)}) copy-start(bf16[512,256]{1,0:T(8,128)(2,1)} %bc_in_ref.1) | copy-start | bytes 786436
  4.7 0.8 %copy-start.2 = (bf16[40,512]{1,0:T(8,128)(2,1)S(1)}, bf16[40,512]{1,0:T(8,128)(2,1)}, u32[]{:S(2)}) copy-start(bf16[40,512]{1,0:T(8,128)(2,1)} %dt_ref.1) | copy-start | bytes 122884
  5.5 0.7 copy-start.3
  6.2 0.7 copy-start.4
  6.9 0.7 copy-start.5

commit v6 on v5

--- a/solution.py
+++ b/solution.py
@@ -11,6 +11,7 @@
 HEADS_PAD = 128
 EXTRA = 16
 VMEM_BYTES = 48 * 1024 * 1024
+FUSED_VMEM_BYTES = 61 * 1024 * 1024
 
 
 def shifted(block, axis, distance):
@@ -213,9 +214,9 @@
 
 def fused_kernel(
     head_size, chunk,
-    x_ref, bc_in_ref, z_hbm, dt_ref, ids_row_ref, conv_x_ref, conv_bc_ref, a_log_ref, bias_ref,
-    skip_heads_ref, norm_ref, w_ref,
+    x_hbm, bc_hbm, z_hbm, w_ref, dt_ref, ids_row_ref, conv_x_ref, conv_bc_ref, rows_ref,
     out_ref,
+    x_ref, bc_in_ref,
     ext, ids_ext, rim_x, rim_bc, rim_ids, ids_sent, mixed_ref, bc_ref, cum_ref, cum_t_ref,
     step_t_ref, gain_t_ref, tail_t, b_t, fresh_ref, decay_ref, state_ref, part_ref, enter_ref,
     scores, got, whole, near, far, sent, landed, own_decay, got_decay, pair_decay, near_decay,
@@ -269,6 +270,14 @@
     def greet_beyond():
         pl.semaphore_signal(barrier, inc=1, device_id={"seq": beyond}, device_id_type=mesh_type)
 
+    first_loads = [
+        pltpu.make_async_copy(source, place, load_sems.at[3 + k])
+        for k, (source, place) in enumerate(
+            ((bc_hbm, bc_in_ref), (x_hbm, x_ref))
+        )
+    ]
+    for load in first_loads:
+        load.start()
     loads = [pltpu.make_async_copy(z_hbm, z_ref, load_sems.at[0])]
     for k, (who, place) in enumerate(((peer, w_far), (member, w_near))):
         loads.append(
@@ -343,8 +352,8 @@
     def halo_copies():
         last = pl.ds(rows - 16, 16)
         return [
-            remote(x_ref.at[last, :], rim_x, halo_sems.at[0, 0], halo_sems.at[1, 0], following),
-            remote(bc_in_ref.at[last, :], rim_bc, halo_sems.at[0, 1], halo_sems.at[1, 1], following),
+            remote(x_hbm.at[last, :], rim_x, halo_sems.at[0, 0], halo_sems.at[1, 0], following),
+            remote(bc_hbm.at[last, :], rim_bc, halo_sems.at[0, 1], halo_sems.at[1, 1], following),
             remote(ids_sent, rim_ids, halo_sems.at[0, 2], halo_sems.at[1, 2], following),
         ]
 
@@ -356,14 +365,17 @@
     def column(row):
         return jnp.broadcast_to(row, (128, row.shape[1])).T
 
-    logits = dt_ref[...].astype(f32) + column(bias_ref[...])[:heads, 0:1]
+    logits = dt_ref[...].astype(f32) + column(rows_ref[:, HEADS_PAD : 2 * HEADS_PAD])[:heads, 0:1]
     step_size = jnp.maximum(logits, 0.0) + jnp.log1p(jnp.exp(-jnp.abs(logits)))
-    rates = -jnp.exp(column(a_log_ref[...])[:heads, 0:1]) * step_size
+    rates = -jnp.exp(column(rows_ref[:, :HEADS_PAD])[:heads, 0:1]) * step_size
     spare = jnp.zeros((HEADS_PAD - heads, rows), f32)
     step_size = jnp.concatenate([step_size, spare])
     rates = jnp.concatenate([rates, spare])
     ids_ext[8 : 8 + rows, :] = column(ids_row)
     ids = ids_ext[8 : 8 + rows, :]
+
+    for load in first_loads:
+        load.wait()
 
     @pl.when(has_prev)
     def take_halo():
@@ -468,7 +480,7 @@
 
     lax.fori_loop(0, groups, states, 0)
     ids_wide = jnp.concatenate([ids] * (SPAN // 128), axis=1)
-    skip_tile = jnp.broadcast_to(skip_heads_ref[...], (8, HEADS_PAD))
+    skip_tile = jnp.broadcast_to(rows_ref[:, 2 * HEADS_PAD : 3 * HEADS_PAD], (8, HEADS_PAD))
     for b in range(blocks):
         span = slice(b * SPAN, (b + 1) * SPAN)
         raw = lax.dot_general(
@@ -549,15 +561,17 @@
     loads[0].wait()
     count = rows // chunk
     per_block = SPAN // chunk
+    gate_size = 512
+    gate_heads = gate_size // head_size
     tile = 256 if out_width % 256 == 0 else 128
 
-    def product(q, weights, store):
+    def product(here, weights, store):
         def columns(j, unused):
             lanes = pl.ds(pl.multiple_of(j * tile, tile), tile)
             store(
                 lanes,
                 jnp.dot(
-                    scaled[q * chunk : (q + 1) * chunk, :], weights[:, lanes],
+                    scaled[here, :], weights[:, lanes],
                     preferred_element_type=jnp.float32,
                 ).astype(jnp.bfloat16),
             )
@@ -571,8 +585,8 @@
         here = slice(q * chunk, (q + 1) * chunk)
 
         def group(c, squares):
-            lanes = pl.ds(pl.multiple_of(c * size, size), size)
-            turn = lax.rem(HEADS_PAD - c * per_group, HEADS_PAD)
+            lanes = pl.ds(pl.multiple_of(c * gate_size, gate_size), gate_size)
+            turn = lax.rem(HEADS_PAD - c * gate_heads, HEADS_PAD)
             if q == 0:
                 state[:, lanes] = enter_ref[:, lanes]
             elif within == 0:
@@ -580,20 +594,21 @@
                     decay_ref[b - 1, 0:1, lanes] * state[:, lanes].astype(jnp.float32)
                     + fresh_ref[b - 1, :, lanes]
                 ).astype(jnp.bfloat16)
-            gain = spread_heads(pltpu.roll(gain_t_ref[here, :], turn, 1), head_size, size)
+            gains = rows_ref[:, pl.ds(pl.multiple_of(3 * HEADS_PAD + c * gate_size, 128), gate_size)]
+            gain = spread_heads(pltpu.roll(gain_t_ref[here, :], turn, 1), head_size, gate_size)
             reached = jnp.dot(
                 bc_ref[here, state_size:], state[:, lanes], preferred_element_type=jnp.float32
             )
             y = part_ref[here, lanes] + gain * reached
             y = y.astype(jnp.bfloat16).astype(jnp.float32)
             gated = y * silu(z_ref[here, lanes].astype(jnp.float32))
-            scaled[here, lanes] = (gated * norm_ref[:, lanes]).astype(jnp.bfloat16)
+            scaled[here, lanes] = (gated * gains).astype(jnp.bfloat16)
             square = gated * gated
-            for k in range(size // 128):
+            for k in range(gate_size // 128):
                 squares = squares + square[:, k * 128 : (k + 1) * 128]
             return squares
 
-        squares = lax.fori_loop(0, width // size, group, jnp.zeros((chunk, 128), jnp.float32))
+        squares = lax.fori_loop(0, width // gate_size, group, jnp.zeros((chunk, 128), jnp.float32))
         row = jnp.sum(squares.T, axis=0, keepdims=True)
         row_sends[q] = jnp.broadcast_to(row, (8, chunk))
         if q == 0:
@@ -602,7 +617,7 @@
         def put(lanes, value):
             sends[q, :, lanes] = value
 
-        product(q, w_far, put)
+        product(here, w_far, put)
         pair = [
             pltpu.make_async_remote_copy(
                 src_ref=source.at[q],
@@ -622,13 +637,13 @@
         copies.append(pair)
 
     loads[2].wait()
+
+    def keep(lanes, value):
+        sums[:, lanes] = value
+
+    product(slice(0, rows), w_near, keep)
     for q in range(count):
         here = slice(q * chunk, (q + 1) * chunk)
-
-        def keep(lanes, value):
-            sums[:, lanes] = value
-
-        product(q, w_near, keep)
         for copy in copies[q]:
             copy.wait_recv()
         row = row_sends[q, 0:1, :] + row_gots[q, 0:1, :]
@@ -636,7 +651,7 @@
         inv = jnp.broadcast_to(inv_row, (128, chunk)).T
         for j in range(out_width // 128):
             lanes = slice(j * 128, (j + 1) * 128)
-            total = sums[:, lanes].astype(jnp.float32) + gots[q, :, lanes].astype(jnp.float32)
+            total = sums[here, lanes].astype(jnp.float32) + gots[q, :, lanes].astype(jnp.float32)
             out_ref[here, lanes] = (total * inv).astype(jnp.bfloat16)
     for pair in copies:
         for copy in pair:
@@ -766,15 +781,17 @@
         count = rows // chunk
         piece = (pieces, state_size, 256)
 
-        def head_row(values):
-            return jnp.pad(values, (0, HEADS_PAD - heads))[None, :]
+        def padded(values):
+            return jnp.pad(values, (0, HEADS_PAD - heads))
 
         return pl.pallas_call(
             functools.partial(fused_kernel, head_size, chunk),
             out_shape=shape((rows, out_width), bf16),
-            in_specs=[vmem, vmem, hbm] + [vmem] * 8 + [hbm],
+            in_specs=[hbm] * 4 + [vmem] * 5,
             out_specs=vmem,
             scratch_shapes=[
+                pltpu.VMEM((rows, width), bf16),
+                pltpu.VMEM((rows, bc_width), bf16),
                 pltpu.VMEM((rows + 8, 256), f32),
                 pltpu.VMEM((rows + 8, 128), f32),
                 pltpu.VMEM((16, width), bf16),
@@ -804,19 +821,19 @@
                 pltpu.VMEM((width, out_width), bf16),
                 pltpu.VMEM((rows, width), bf16),
                 pltpu.VMEM((state_size, width), bf16),
-                pltpu.VMEM((chunk, out_width), bf16),
+                pltpu.VMEM((rows, out_width), bf16),
                 pltpu.VMEM((count, chunk, out_width), bf16),
                 pltpu.VMEM((count, chunk, out_width), bf16),
                 pltpu.VMEM((count, 8, chunk), f32),
                 pltpu.VMEM((count, 8, chunk), f32),
                 pltpu.SemaphoreType.DMA((2, 3)),
-                pltpu.SemaphoreType.DMA((3,)),
+                pltpu.SemaphoreType.DMA((5,)),
                 pltpu.SemaphoreType.DMA((4,)),
             ]
             + [pltpu.SemaphoreType.DMA((2, pieces))] * 4
             + [pltpu.SemaphoreType.DMA((count,))] * 4,
             compiler_params=pltpu.CompilerParams(
-                collective_id=0, has_side_effects=True, vmem_limit_bytes=VMEM_BYTES
+                collective_id=0, has_side_effects=True, vmem_limit_bytes=FUSED_VMEM_BYTES
             ),
             cost_estimate=pl.CostEstimate(
                 flops=2 * rows * width * w_out.shape[1],
@@ -824,8 +841,10 @@
                 transcendentals=0,
             ),
         )(
-            x_stream, bc_stream, z_gate, dt_stream, doc_ids[None, :], conv_x, conv_bc,
-            head_row(a_log), head_row(dt_bias), head_row(d_skip), norm_gain[None, :], w_out,
+            x_stream, bc_stream, z_gate, w_out, dt_stream, doc_ids[None, :], conv_x, conv_bc,
+            jnp.concatenate(
+                [padded(a_log), padded(dt_bias), padded(d_skip), norm_gain]
+            )[None, :],
         )
     own_ids = doc_ids.astype(f32)
     tail_ids = jnp.broadcast_to(own_ids[edge:].astype(bf16)[:, None], (taps - 1, 128))

time: 76.8 us -> 73.3 us (0.954)
  local copies, waits for them, and re-layouts: 8.66 us -> 3.07 us
  Pallas kernels: 67.7 us -> 69.2 us
  other arithmetic: 0 us -> 0.77 us
    unnamed x13 -> x1, local copies, waits for them, and re-layouts: 6.61 us -> 2.46 us
    pallas_call x1, Pallas kernels: 67.7 us -> 69.2 us  [local(): pl.pallas_call(functools.partial(fused_kernel, head_size, chunk), out_sha...]
    broadcast_in_dim x3 -> x1, local copies, waits for them, and re-layouts: 2.05 us -> 0.61 us  [local(): jnp.concatenate([padded(a_log), padded(dt_bias), padded(d_skip), norm_gain])]
where the time goes in v6:
time: 73.3 us; the launch traced here: 73 us
  Pallas kernels  69.2 us (94%)
  local copies, waits for them, and re-layouts  3.07 us (4%)
  other arithmetic  0.77 us (1%)
    pallas_call x1, Pallas kernels, local(): pl.pallas_call(functools.partial(fused_kernel, head_size, chunk), out_sha...  69.2 us
    unnamed x1, local copies, waits for them, and re-layouts  2.46 us

profile of v6, /device:TPU:0, one launch (start us, length us, event | category | flops | bytes accessed | tf_op | source)
XLA Modules:
  0.0 73.0 jit_solution(8593183310589808019)
XLA Ops:
  0.0 0.8 %fusion = f32[2944]{0:T(1024)S(1)} fusion(f32[40]{0:T(128)} %param.21, f32[40]{0:T(128)} %param.20, f32[40]{0:T(128)} %param.19, f32[2560]{0:T(1024)} %param.22), kind=kLoop, calls=%fused_computation.5 | loop fusion | flops 38272 | bytes 22496 | tf_op jit(solution)/shard_map/concatenate | solution.py:845
  0.8 0.6 broadcast_in_dim.7.rows_ref
  1.4 69.2 %shard_map.118 = bf16[512,1280]{1,0:T(8,128)(2,1)} custom-call(bf16[512,2560]{1,0:T(8,128)(2,1)} %x_hbm.1, bf16[512,256]{1,0:T(8,128)(2,1)} %bc_hbm.1, bf16[512,2560]{1,0:T(8,128)(2,1)} %z_hbm.1, bf16[2560,2560]{1,0:T(8,128)(2,1)} %w_ref.1, bf16[40,512]{1,0:T(8,128)(2,1)} %dt_ref.1, s32[1,512]{1,0:T(1,128)} %bitcast.1, bf16[4,2560]{1,0:T(4,128)(2,1)} %conv_x_ref.1, ...), custom_call_target="tpu_custom_call" | custom-call | flops 6710886400 | bytes 13107200 | tf_op jit(solution)/shard_map/pallas_call | solution.py:787
  70.6 2.5 %copy.14 = bf16[512,1280]{1,0:T(8,128)(2,1)} copy(bf16[512,1280]{1,0:T(8,128)(2,1)} %shard_map.118) | data formatting | bytes 2621440

commit v7 on v6

--- a/solution.py
+++ b/solution.py
@@ -24,7 +24,8 @@
 
 
 def silu(v):
-    return v / (1.0 + jnp.exp(-v))
+    scaled = 0.5 * v
+    return scaled + scaled * jnp.tanh(scaled)
 
 
 def spread_heads(columns, width, lanes):
@@ -550,8 +551,7 @@
             sent[k] = jnp.where(odd, entering, later).astype(bf16)
             land_copy(k).start()
 
-        for b in range(blocks):
-            mix(j, b)
+        mix(j, 0)
         return unused
 
     lax.fori_loop(0, groups, step, 0)
@@ -607,6 +607,14 @@
             for k in range(gate_size // 128):
                 squares = squares + square[:, k * 128 : (k + 1) * 128]
             return squares
+
+        if b > 0 and within == 0:
+
+            def mix_later(c, unused, b=b):
+                mix(c, b)
+                return unused
+
+            lax.fori_loop(0, groups, mix_later, 0)
 
         squares = lax.fori_loop(0, width // gate_size, group, jnp.zeros((chunk, 128), jnp.float32))
         row = jnp.sum(squares.T, axis=0, keepdims=True)

time: 73.3 us -> 68.3 us (0.932)
  Pallas kernels: 69.2 us -> 63.7 us
    pallas_call x1, Pallas kernels: 69.2 us -> 63.7 us  [local(): pl.pallas_call(functools.partial(fused_kernel, head_size, chunk), out_sha...]
where the time goes in v7:
time: 68.3 us; the launch traced here: 67.5 us
  Pallas kernels  63.7 us (93%)
  local copies, waits for them, and re-layouts  3.07 us (4%)
  other arithmetic  0.77 us (1%)
    pallas_call x1, Pallas kernels, local(): pl.pallas_call(functools.partial(fused_kernel, head_size, chunk), out_sha...  63.7 us
    unnamed x1, local copies, waits for them, and re-layouts  2.46 us

profile of v7, /device:TPU:0, one launch (start us, length us, event | category | flops | bytes accessed | tf_op | source)
XLA Modules:
  0.0 67.5 jit_solution(1930848268473165709)
XLA Ops:
  0.0 0.8 %fusion = f32[2944]{0:T(1024)S(1)} fusion(f32[40]{0:T(128)} %param.21, f32[40]{0:T(128)} %param.20, f32[40]{0:T(128)} %param.19, f32[2560]{0:T(1024)} %param.22), kind=kLoop, calls=%fused_computation.5 | loop fusion | flops 38272 | bytes 22496 | tf_op jit(solution)/shard_map/concatenate | solution.py:853
  0.8 0.6 broadcast_in_dim.7.rows_ref
  1.4 63.7 %shard_map.118 = bf16[512,1280]{1,0:T(8,128)(2,1)} custom-call(bf16[512,2560]{1,0:T(8,128)(2,1)} %x_hbm.1, bf16[512,256]{1,0:T(8,128)(2,1)} %bc_hbm.1, bf16[512,2560]{1,0:T(8,128)(2,1)} %z_hbm.1, bf16[2560,2560]{1,0:T(8,128)(2,1)} %w_ref.1, bf16[40,512]{1,0:T(8,128)(2,1)} %dt_ref.1, s32[1,512]{1,0:T(1,128)} %bitcast.1, bf16[4,2560]{1,0:T(4,128)(2,1)} %conv_x_ref.1, ...), custom_call_target="tpu_custom_call" | custom-call | flops 6710886400 | bytes 13107200 | tf_op jit(solution)/shard_map/pallas_call | solution.py:795
  65.1 2.5 %copy.14 = bf16[512,1280]{1,0:T(8,128)(2,1)} copy(bf16[512,1280]{1,0:T(8,128)(2,1)} %shard_map.118) | data formatting | bytes 2621440

commit v8 on v7

--- a/solution.py
+++ b/solution.py
@@ -11,7 +11,7 @@
 HEADS_PAD = 128
 EXTRA = 16
 VMEM_BYTES = 48 * 1024 * 1024
-FUSED_VMEM_BYTES = 61 * 1024 * 1024
+FUSED_VMEM_BYTES = 58 * 1024 * 1024
 
 
 def shifted(block, axis, distance):

time: 68.3 us -> 68.3 us (level)
  no operation moved by 1% of the time
where the time goes in v8:
time: 68.3 us; the launch traced here: 67.5 us
  Pallas kernels  63.7 us (93%)
  local copies, waits for them, and re-layouts  3.07 us (4%)
  other arithmetic  0.77 us (1%)
    pallas_call x1, Pallas kernels, local(): pl.pallas_call(functools.partial(fused_kernel, head_size, chunk), out_sha...  63.7 us
    unnamed x1, local copies, waits for them, and re-layouts  2.46 us

profile of v8, /device:TPU:0, one launch (start us, length us, event | category | flops | bytes accessed | tf_op | source)
XLA Modules:
  0.0 67.5 jit_solution(1930848268473165709)
XLA Ops:
  0.0 0.8 %fusion = f32[2944]{0:T(1024)S(1)} fusion(f32[40]{0:T(128)} %param.21, f32[40]{0:T(128)} %param.20, f32[40]{0:T(128)} %param.19, f32[2560]{0:T(1024)} %param.22), kind=kLoop, calls=%fused_computation.5 | loop fusion | flops 38272 | bytes 22496 | tf_op jit(solution)/shard_map/concatenate | solution.py:853
  0.8 0.6 broadcast_in_dim.7.rows_ref
  1.4 63.7 %shard_map.118 = bf16[512,1280]{1,0:T(8,128)(2,1)} custom-call(bf16[512,2560]{1,0:T(8,128)(2,1)} %x_hbm.1, bf16[512,256]{1,0:T(8,128)(2,1)} %bc_hbm.1, bf16[512,2560]{1,0:T(8,128)(2,1)} %z_hbm.1, bf16[2560,2560]{1,0:T(8,128)(2,1)} %w_ref.1, bf16[40,512]{1,0:T(8,128)(2,1)} %dt_ref.1, s32[1,512]{1,0:T(1,128)} %bitcast.1, bf16[4,2560]{1,0:T(4,128)(2,1)} %conv_x_ref.1, ...), custom_call_target="tpu_custom_call" | custom-call | flops 6710886400 | bytes 13107200 | tf_op jit(solution)/shard_map/pallas_call | solution.py:795
  65.1 2.5 %copy.14 = bf16[512,1280]{1,0:T(8,128)(2,1)} copy(bf16[512,1280]{1,0:T(8,128)(2,1)} %shard_map.118) | data formatting | bytes 2621440
